TPU v7x, 32 devices: a whole 2x2x4 slice. The times are simulated.
32 devices in a mesh: node: 8 (over y, x, core), local: 4 (over z).
Axes of the slice: x: 2, y: 2, z: 4, core: 2. Of those that a mesh axis runs over, the one named last changes fastest.
Arguments:
- tokens: bfloat16 [256, 7168], P(('node', 'local')), may hold values from -6 to 6
- grad_out: bfloat16 [256, 7168], P(('node', 'local')), may hold values from -6 to 6
- expert_ids: int32 [256, 4], P(('node', 'local')), may hold values from 0 to 7, all different within a row; in each aligned block of 8 rows (0 to 7, 8 to 15, ...) at most 8 rows name the same one
- gate_weights: bfloat16 [256, 4], P(('node', 'local')), may hold values from 0.049804688 to 1
- w_gate: bfloat16 [8, 7168, 1024], P('node', None, 'local'), may hold values from -0.0625 to 0.0625
- w_up: bfloat16 [8, 7168, 1024], P('node', None, 'local'), may hold values from -0.0625 to 0.0625
- w_down: bfloat16 [8, 1024, 7168], P('node', 'local'), may hold values from -0.1875 to 0.1875
Outputs:
- grad_in: bfloat16 [256, 7168], P(('node', 'local'))
- grad_gate: bfloat16 [256, 4], P(('node', 'local'))
- grad_w_gate: bfloat16 [8, 7168, 1024], P('node', None, 'local')
- grad_w_up: bfloat16 [8, 7168, 1024], P('node', None, 'local')
- grad_w_down: bfloat16 [8, 1024, 7168], P('node', 'local')
Inputs may be any that keep to these rules, and one draw needn't show every extreme that they name: `expert_ids`: the 4 experts of a token differ. Among one device's 8 tokens no expert is named more than 8 times, and in every draw some expert is named exactly 8 times by some device.
All inputs are finite; a program needn't handle non-finite values.
Results may differ from a plain program's by a relative error of at most 0.024.
Values may be sent and summed in bfloat16 or wider, within the bound.
No kernel may reach another device: no remote copies, remote signals or barrier semaphores. Data moves between devices by JAX's collectives and lax.ppermute only.
A program may use at most 128 MiB of HBM per device.

v0:
```python
import jax
import jax.numpy as jnp
from jax import lax
from jax.sharding import PartitionSpec as P


def per_device(tokens, grad_out, expert_ids, gate_weights, w_gate, w_up, w_down):
    tok_count = tokens.shape[0]
    width = tokens.shape[1]
    top_count = expert_ids.shape[1]
    node_count = lax.axis_size("node")
    local_count = lax.axis_size("local")
    capacity = max(2, 2 * tok_count * top_count // node_count)
    onehot = (
        expert_ids[:, :, None] == jnp.arange(node_count, dtype=jnp.int32)[None, None, :]
    ).astype(jnp.int32)
    per_token = jnp.sum(onehot, axis=1)
    earlier = jnp.cumsum(per_token, axis=0) - per_token
    slot_index = jnp.sum(earlier[:, None, :] * onehot, axis=2)
    flat_slot = expert_ids * capacity + slot_index
    placing = (
        flat_slot[:, :, None] == jnp.arange(node_count * capacity, dtype=jnp.int32)[None, None, :]
    ).astype(jnp.float32)
    placing_tok = jnp.sum(placing, axis=1).astype(jnp.bfloat16)
    send_in = (
        jnp.dot(placing_tok.T, tokens, preferred_element_type=jnp.float32)
        .astype(jnp.bfloat16)
        .reshape(node_count, capacity, width)
    )
    send_grad = (
        jnp.dot(placing_tok.T, grad_out, preferred_element_type=jnp.float32)
        .astype(jnp.bfloat16)
        .reshape(node_count, capacity, width)
    )
    send_gate = (
        jnp.einsum(
            "tks,tk->s", placing, gate_weights.astype(jnp.float32), precision=lax.Precision.HIGHEST
        )
        .astype(jnp.bfloat16)
        .reshape(node_count, capacity)
    )
    recv_in, recv_grad, recv_gate = (
        lax.all_to_all(send_in, "node", split_axis=0, concat_axis=0, tiled=True),
        lax.all_to_all(send_grad, "node", split_axis=0, concat_axis=0, tiled=True),
        lax.all_to_all(send_gate, "node", split_axis=0, concat_axis=0, tiled=True),
    )
    rows_in, rows_grad, rows_gate = (
        lax.all_gather(recv_in[None], "local", axis=0, tiled=True),
        lax.all_gather(recv_grad[None], "local", axis=0, tiled=True),
        lax.all_gather(recv_gate[None], "local", axis=0, tiled=True),
    )
    rows_total = local_count * node_count * capacity
    flat_in = rows_in.reshape(rows_total, width)
    flat_grad = rows_grad.reshape(rows_total, width)
    flat_gate = rows_gate.reshape(rows_total).astype(jnp.float32)
    gate_proj = w_gate[0]
    up_proj = w_up[0]
    down_proj = w_down[0]
    contract_rows = (((0,), (0,)), ((), ()))
    contract_cols = (((1,), (1,)), ((), ()))
    gate_pre = jnp.dot(flat_in, gate_proj, preferred_element_type=jnp.float32)
    up_pre = jnp.dot(flat_in, up_proj, preferred_element_type=jnp.float32)
    sigmoid_val = jax.nn.sigmoid(gate_pre)
    activated = gate_pre * sigmoid_val
    slope = sigmoid_val * (1.0 + gate_pre * (1.0 - sigmoid_val))
    hidden = (activated * up_pre).astype(jnp.bfloat16)
    grad_hidden = lax.dot_general(
        flat_grad, down_proj, contract_cols, preferred_element_type=jnp.float32
    )
    gate_partial = jnp.sum(hidden.astype(jnp.float32) * grad_hidden, axis=1)
    scaled = flat_gate[:, None] * grad_hidden
    grad_gate_pre = (scaled * up_pre * slope).astype(jnp.bfloat16)
    grad_up_pre = (scaled * activated).astype(jnp.bfloat16)
    weighted = (flat_gate[:, None] * hidden.astype(jnp.float32)).astype(jnp.bfloat16)
    grad_down = lax.dot_general(
        weighted, flat_grad, contract_rows, preferred_element_type=jnp.float32
    ).astype(jnp.bfloat16)
    grad_gate_w = lax.dot_general(
        flat_in, grad_gate_pre, contract_rows, preferred_element_type=jnp.float32
    ).astype(jnp.bfloat16)
    grad_up_w = lax.dot_general(
        flat_in, grad_up_pre, contract_rows, preferred_element_type=jnp.float32
    ).astype(jnp.bfloat16)
    input_partial = lax.dot_general(
        grad_gate_pre, gate_proj, contract_cols, preferred_element_type=jnp.float32
    )
    input_partial = input_partial + lax.dot_general(
        grad_up_pre, up_proj, contract_cols, preferred_element_type=jnp.float32
    )
    input_blocks = input_partial.reshape(local_count, node_count, capacity, width)
    gate_blocks = gate_partial.reshape(local_count, node_count, capacity)
    summed_in, summed_gate = (
        lax.psum_scatter(
            input_blocks.astype(jnp.bfloat16), "local", scatter_dimension=0, tiled=True
        ).astype(jnp.float32),
        lax.psum_scatter(
            gate_blocks.astype(jnp.bfloat16), "local", scatter_dimension=0, tiled=True
        ).astype(jnp.float32),
    )
    back_in, back_gate = (
        lax.all_to_all(
            summed_in[0].astype(jnp.bfloat16), "node", split_axis=0, concat_axis=0, tiled=True
        ),
        lax.all_to_all(
            summed_gate[0].astype(jnp.bfloat16), "node", split_axis=0, concat_axis=0, tiled=True
        ),
    )
    grad_in = jnp.dot(
        placing_tok,
        back_in.reshape(node_count * capacity, width),
        preferred_element_type=jnp.float32,
    ).astype(jnp.bfloat16)
    grad_gate = jnp.einsum(
        "tks,s->tk",
        placing,
        back_gate.reshape(node_count * capacity).astype(jnp.float32),
        precision=lax.Precision.HIGHEST,
    ).astype(jnp.bfloat16)
    return (grad_in, grad_gate, grad_gate_w[None], grad_up_w[None], grad_down[None])


def solution(mesh):
    placed = (
        P(("node", "local"), None),
        P(("node", "local"), None),
        P(("node", "local"), None),
        P(("node", "local"), None),
        P("node", None, "local"),
        P("node", None, "local"),
        P("node", "local", None),
    )
    return jax.shard_map(
        per_device,
        mesh=mesh,
        in_specs=placed,
        out_specs=(
            P(("node", "local"), None),
            P(("node", "local"), None),
            P("node", None, "local"),
            P("node", None, "local"),
            P("node", "local", None),
        ),
        check_vma=False,
    )
```

profile of v0, /device:TPU:0, one launch (start us, length us, event | category | flops | bytes accessed | tf_op | source)
XLA Modules:
  0.0 275.4 jit_solution(15693449912067309396)
XLA Ops:
  7.2 0.0 copy-start
  7.2 0.0 copy-start.6
  7.2 0.0 all-gather.8.cloned.1.call-start
  7.2 0.8 convert_reduce_fusion.1
  8.1 0.9 select_reduce_fusion
  9.0 0.7 multiply_add_fusion
  9.7 0.1 convert_reduce_fusion
  9.7 0.0 copy-done
  9.7 0.0 copy-start.7
  9.7 0.4 fusion.5
  10.2 19.0 %all_to_all.31 = bf16[8,8,7168]{2,1,0:T(8,128)(2,1)} all-to-all(bf16[8,8,7168]{2,1,0:T(8,128)(2,1)S(1)} %fusion.5), channel_id=1, replica_groups=mesh['node'=8,'local'=4] {'node'}, dimensions={0} | all-to-all | bytes 1835008 | tf_op jit(solution)/shard_map/all_to_all | solution.py:43
  29.2 0.0 all-gather.8.cloned.1.call-update
  29.2 0.0 all-gather.6.cloned.1.call-start
  29.3 0.0 copy-done.6
  29.3 0.4 fusion.4
  29.7 17.1 %all_to_all.32 = bf16[8,8,7168]{2,1,0:T(8,128)(2,1)} all-to-all(bf16[8,8,7168]{2,1,0:T(8,128)(2,1)S(1)} %fusion.4), channel_id=1, replica_groups=mesh['node'=8,'local'=4] {'node'}, dimensions={0} | all-to-all | bytes 1835008 | tf_op jit(solution)/shard_map/all_to_all | solution.py:44
  46.8 0.0 all-gather.6.cloned.1.call-update
  46.9 0.0 reduce-scatter.2.cloned.1.call-start
  46.9 0.0 copy-done.7
  46.9 0.2 fusion.21
  47.1 0.1 all_to_all.25
  47.2 7.0 %all_to_all.33 = bf16[8,1,8]{2,1,0:T(2,128)(2,1)S(1)} all-to-all(bf16[8,1,8]{2,1,0:T(2,128)(2,1)S(1)} %all_to_all.25), channel_id=1, replica_groups=mesh['node'=8,'local'=4] {'node'}, dimensions={0} | all-to-all | bytes 256 | tf_op jit(solution)/shard_map/all_to_all | solution.py:45
  54.2 13.9 %all-gather = bf16[32,1,8]{2,0,1:T(8,128)(2,1)S(1)} all-gather(bf16[8,1,8]{2,0,1:T(8,128)(2,1)S(1)} %copy.30), channel_id=2, replica_groups=mesh['node'=8,'local'=4] {'local'}, dimensions={0}, use_global_device_ids=true | all-gather | bytes 640 | tf_op jit(solution)/shard_map/all_gather | solution.py:50
  68.1 0.1 reshape.77
  68.2 32.8 %all-gather.8.cloned.1.call-done = bf16[32,8,7168]{2,1,0:T(8,128)(2,1)} async-done(((bf16[8,8,7168]{2,1,0:T(8,128)(2,1)}), bf16[32,8,7168]{2,1,0:T(8,128)(2,1)}) %all-gather.8.cloned.1.call-update) | async-done | bytes 3670032 | tf_op jit(solution)/shard_map/all_gather | solution.py:48
  101.0 0.0 copy-start.1
  101.0 0.0 copy-start.4
  101.0 4.8 %fusion.11 = f32[256,256]{0,1:T(8,128)S(1)} fusion(bf16[1,7168,256]{2,1,0:T(8,128)(2,1)} %param.12, bf16[32,8,7168]{2,1,0:T(8,128)(2,1)} %all-gather.8.cloned.1.call-done), kind=kOutput, calls=%fused_computation.18 | convolution fusion | flops 939524096 | bytes 7602176 | tf_op jit(solution)/shard_map/dot_general | solution.py:62
  105.9 0.0 copy-done.1
  105.9 0.5 copy-done.4
  106.3 1.6 fusion.8
  107.9 65.4 %all-gather.6.cloned.1.call-done = bf16[32,8,7168]{2,1,0:T(8,128)(2,1)} async-done(((bf16[8,8,7168]{2,1,0:T(8,128)(2,1)}), bf16[32,8,7168]{2,1,0:T(8,128)(2,1)}) %all-gather.6.cloned.1.call-update) | async-done | bytes 3670032 | tf_op jit(solution)/shard_map/all_gather | solution.py:49
  173.3 0.0 copy-start.5
  173.3 4.5 %fusion.23 = (bf16[256]{0:T(256)(128)(2,1)S(1)}, bf16[256,256]{0,1:T(8,128)(2,1)S(1)}, bf16[256,256]{0,1:T(8,128)(2,1)S(1)}, bf16[256,256]{0,1:T(8,128)(2,1)S(1)}) fusion(f32[256,256]{0,1:T(8,128)S(1)} %fusion.11, f32[256,256]{0,1:T(8,128)S(1)} %fusion.8, f32[256]{0:T(256)S(1)} %reshape.77, bf16[1,256,7168]{2,1,0:T(8,128)(2,1)} %param.13, ...), kind=kOutput, calls=%fused_computation.33 | convolution fusion | flops 940769024 | bytes 8259072 | tf_op jit(solution)/shard_map/dot_general | solution.py:67
  177.8 0.0 copy-done.5
  177.8 0.0 copy-start.3
  177.8 1.2 fusion.6
  179.0 0.8 copy-done.3
  179.8 3.0 %fusion = bf16[256,7168]{1,0:T(8,128)(2,1)} fusion(f32[256,7168]{1,0:T(8,128)S(1)} %fusion.6, bf16[256,256]{0,1:T(8,128)(2,1)S(1)} %get-tuple-element.8, bf16[1,7168,256]{2,1,0:T(8,128)(2,1)S(1)} %copy-done.3), kind=kOutput, calls=%fused_computation.1 | convolution fusion | flops 943194112 | bytes 14811136 | tf_op jit(solution)/shard_map/dot_general | solution.py:87
  182.9 0.0 copy-start.8
  182.9 0.0 reduce-scatter.2.cloned.1.call-update
  182.9 0.6 copy-done.8
  183.5 0.6 dynamic-slice
  184.1 0.1 convert_element_type.107
  184.2 9.4 %all-reduce = bf16[4,8,8]{2,1,0:T(8,128)(2,1)S(1)} all-reduce(bf16[4,8,8]{2,1,0:T(8,128)(2,1)S(1)} %convert_element_type.107), channel_id=6, replica_groups=mesh['node'=8,'local'=4] {'local'}, use_global_device_ids=true, to_apply=%region_6.7.clone | all-reduce | flops 256 | bytes 1024
  193.6 0.7 dynamic-slice_bitcast_fusion
  194.2 0.6 copy.31
  194.8 4.0 %all-to-all-start.4 = ((bf16[8,1,8]{2,1,0:T(2,128)(2,1)}), bf16[8,1,8]{2,1,0:T(2,128)(2,1)S(1)}, u32[]{:S(2)}, u32[]{:S(2)}) async-start(bf16[8,1,8]{2,1,0:T(2,128)(2,1)} %copy.31), calls=%async_computation.5 | async-start | bytes 8192 | tf_op jit(solution)/shard_map/all_to_all | solution.py:104
  198.8 5.1 %fusion.1 = bf16[1,7168,256]{2,1,0:T(8,128)(2,1)} fusion(bf16[256,256]{0,1:T(8,128)(2,1)S(1)} %get-tuple-element.7, bf16[32,8,7168]{2,1,0:T(8,128)(2,1)} %all-gather.8.cloned.1.call-done), kind=kOutput, calls=%fused_computation.5 | convolution fusion | flops 941359104 | bytes 7471104 | tf_op jit(solution)/shard_map/dot_general | solution.py:78
  203.9 0.0 all-to-all-done.4
  203.9 46.4 %reduce-scatter.2.cloned.1.call-done = bf16[1,8,8,7168]{3,2,1,0:T(8,128)(2,1)} async-done(((bf16[4,8,8,7168]{3,2,1,0:T(8,128)(2,1)}), bf16[1,8,8,7168]{3,2,1,0:T(8,128)(2,1)}) %reduce-scatter.2.cloned.1.call-update) | async-done | bytes 917520 | tf_op jit(solution)/shard_map/reduce_scatter | solution.py:93
  250.3 3.7 %all-to-all-start.3 = ((bf16[8,8,7168]{2,1,0:T(8,128)(2,1)}), bf16[8,8,7168]{2,1,0:T(8,128)(2,1)S(1)}, u32[]{:S(2)}, u32[]{:S(2)}) async-start(bf16[8,8,7168]{2,1,0:T(8,128)(2,1)} %bitcast.70), calls=%async_computation.4 | async-start | bytes 1835008 | tf_op jit(solution)/shard_map/all_to_all | solution.py:101
  254.0 0.0 copy-start.2
  254.0 5.2 %fusion.3 = bf16[1,256,7168]{2,1,0:T(8,128)(2,1)} fusion(bf16[32,8,7168]{2,1,0:T(8,128)(2,1)} %all-gather.6.cloned.1.call-done, bf16[256,256]{0,1:T(8,128)(2,1)S(1)} %get-tuple-element.6, f32[256]{0:T(256)S(1)} %reshape.77), kind=kOutput, calls=%fused_computation.7 | convolution fusion | flops 941555712 | bytes 7472128 | tf_op jit(solution)/shard_map/dot_general | solution.py:75
  259.2 0.0 copy-done.2
  259.2 3.0 %fusion.2 = bf16[1,7168,256]{2,1,0:T(8,128)(2,1)} fusion(bf16[256,256]{0,1:T(8,128)(2,1)S(1)} %get-tuple-element.8, bf16[32,8,7168]{2,1,0:T(8,128)(2,1)S(1)} %copy-done.2), kind=kOutput, calls=%fused_computation.6 | convolution fusion | flops 941359104 | bytes 7471104 | tf_op jit(solution)/shard_map/dot_general | solution.py:81
  262.2 0.1 reshape.87
  262.3 0.2 fusion.28
  262.5 0.6 convert_element_type.109
  263.1 4.8 %all-to-all-done.3 = bf16[8,8,7168]{2,1,0:T(8,128)(2,1)S(1)} async-done(((bf16[8,8,7168]{2,1,0:T(8,128)(2,1)}), bf16[8,8,7168]{2,1,0:T(8,128)(2,1)S(1)}, u32[]{:S(2)}, u32[]{:S(2)}) %all-to-all-start.3) | async-done | bytes 917536 | tf_op jit(solution)/shard_map/all_to_all | solution.py:101
  268.0 0.9 convolution_convert_fusion.5
  (4 shorter events, 0.1 us)
Async XLA Ops:
  7.2 2.6 copy-start
  7.2 22.1 %copy-start.6 = (bf16[8,7168]{1,0:T(8,128)(2,1)S(1)}, bf16[8,7168]{1,0:T(8,128)(2,1)}, u32[]{:S(2)}) copy-start(bf16[8,7168]{1,0:T(8,128)(2,1)} %param.8) | copy-start | bytes 344068
  7.2 93.8 %all-gather.8.cloned.1.call-start = ((), (), s32[]{:S(2)}) async-start(), calls=%async_computation.8 | async-start | bytes 4587520 | tf_op jit(solution)/shard_map/all_gather | solution.py:48
  9.7 37.2 %copy-start.7 = (bf16[8,4]{0,1:T(4,128)(2,1)S(1)}, bf16[8,4]{0,1:T(4,128)(2,1)}, u32[]{:S(2)}) copy-start(bf16[8,4]{0,1:T(4,128)(2,1)} %param.10) | copy-start | bytes 196
  29.2 144.1 %all-gather.6.cloned.1.call-start = ((), (), s32[]{:S(2)}) async-start(), calls=%async_computation.7 | async-start | bytes 4587520 | tf_op jit(solution)/shard_map/all_gather | solution.py:49
  46.9 203.4 %reduce-scatter.2.cloned.1.call-start = ((), (), s32[]{:S(2)}) async-start(), calls=%async_computation.6 | async-start | bytes 4587520 | tf_op jit(solution)/shard_map/reduce_scatter | solution.py:93
  101.0 4.8 %copy-start.1 = (bf16[32,8,7168]{2,1,0:T(8,128)(2,1)S(1)}, bf16[32,8,7168]{2,1,0:T(8,128)(2,1)}, u32[]{:S(2)}) copy-start(bf16[32,8,7168]{2,1,0:T(8,128)(2,1)} %all-gather.8.cloned.1.call-done) | copy-start | bytes 11010052
  101.0 5.3 %copy-start.4 = (bf16[1,7168,256]{2,1,0:T(8,128)(2,1)S(1)}, bf16[1,7168,256]{2,1,0:T(8,128)(2,1)}, u32[]{:S(2)}) copy-start(bf16[1,7168,256]{2,1,0:T(8,128)(2,1)} %param.11) | copy-start | bytes 11010052
  173.3 4.5 %copy-start.5 = (bf16[1,7168,256]{2,1,0:T(8,128)(2,1)S(1)}, bf16[1,7168,256]{2,1,0:T(8,128)(2,1)}, u32[]{:S(2)}) copy-start(bf16[1,7168,256]{2,1,0:T(8,128)(2,1)} %param.11) | copy-start | bytes 11010052
  177.8 2.0 copy-start.3
  182.9 0.7 copy-start.8
  194.8 9.0 %all-to-all-start.4 = ((bf16[8,1,8]{2,1,0:T(2,128)(2,1)}), bf16[8,1,8]{2,1,0:T(2,128)(2,1)S(1)}, u32[]{:S(2)}, u32[]{:S(2)}) async-start(bf16[8,1,8]{2,1,0:T(2,128)(2,1)} %copy.31), calls=%async_computation.5 | async-start | bytes 8192 | tf_op jit(solution)/shard_map/all_to_all | solution.py:104
  250.3 17.7 %all-to-all-start.3 = ((bf16[8,8,7168]{2,1,0:T(8,128)(2,1)}), bf16[8,8,7168]{2,1,0:T(8,128)(2,1)S(1)}, u32[]{:S(2)}, u32[]{:S(2)}) async-start(bf16[8,8,7168]{2,1,0:T(8,128)(2,1)} %bitcast.70), calls=%async_computation.4 | async-start | bytes 1835008 | tf_op jit(solution)/shard_map/all_to_all | solution.py:101
  254.0 5.2 %copy-start.2 = (bf16[32,8,7168]{2,1,0:T(8,128)(2,1)S(1)}, bf16[32,8,7168]{2,1,0:T(8,128)(2,1)}, u32[]{:S(2)}) copy-start(bf16[32,8,7168]{2,1,0:T(8,128)(2,1)} %all-gather.8.cloned.1.call-done) | copy-start | bytes 11010052
Sparse Core Ops, SparseCore 0:
  29.4 71.6 all-gather.7
  102.6 70.6 all-gather.5
  183.0 67.2 reduce-scatter.1
where the time goes:
time: 276 us; the launch traced here: 275 us
  waiting for transfers between devices  150 us (54%)
  blocking collectives  66.4 us (24%)
  matrix products  30.5 us (11%)
  between operations  13.9 us (5%)
  starting transfers between devices  7.82 us (3%)
  local copies, waits for them, and re-layouts  4.16 us (2%)
  other arithmetic  3.1 us (1%)
    all_gather x1, waiting for transfers between devices, per_device(): lax.all_gather(recv_grad[None], 'local', axis=0, tiled=True)  65.4 us
    reduce_scatter x1, waiting for transfers between devices, per_device(): lax.psum_scatter(input_blocks.astype(jnp.bfloat16), 'local', scatter_dime...  46.4 us
    all_gather x1, waiting for transfers between devices, per_device(): lax.all_gather(recv_in[None], 'local', axis=0, tiled=True)  32.8 us
    all_to_all x1, blocking collectives, per_device(): lax.all_to_all(send_in, 'node', split_axis=0, concat_axis=0, tiled=True)  19 us
    all_to_all x1, blocking collectives, per_device(): lax.all_to_all(send_grad, 'node', split_axis=0, concat_axis=0, tiled=True)  17.1 us
    all_gather x1, blocking collectives, per_device(): lax.all_gather(recv_gate[None], 'local', axis=0, tiled=True)  13.9 us
    unnamed x1, blocking collectives  9.39 us
    all_to_all x1, blocking collectives, per_device(): lax.all_to_all(send_gate, 'node', split_axis=0, concat_axis=0, tiled=True)  7.02 us
  transfers between devices with their start and end apart: 5, of which 4 were waited for; matrix products, arithmetic and copies ran while one was open for 8% of the time, Pallas kernels for 0%

commit v1 on v0

--- a/solution.py
+++ b/solution.py
@@ -3,8 +3,132 @@
 from jax import lax
 from jax.sharding import PartitionSpec as P
 
-
-def per_device(tokens, grad_out, expert_ids, gate_weights, w_gate, w_up, w_down):
+AXES = ("node", "local")
+LANES = 128
+CONTRACT_ROWS = (((0,), (0,)), ((), ()))
+CONTRACT_COLS = (((1,), (1,)), ((), ()))
+CHUNKS = 2
+
+
+def permute(value, node_count, local_count, target):
+    pairs = []
+    for node in range(node_count):
+        for place in range(local_count):
+            to_node, to_place = target(node, place)
+            pairs.append((node * local_count + place, to_node * local_count + to_place))
+    return lax.ppermute(value, AXES, pairs)
+
+
+def dense(tokens, grad_out, expert_ids, gate_weights, w_gate, w_up, w_down):
+    tok_count, width = tokens.shape
+    node_count = lax.axis_size("node")
+    local_count = lax.axis_size("local")
+    bits = [1 << i for i in range(1, node_count.bit_length() - 1)]
+    steps = len(bits)
+
+    def exchange(value, step):
+        def target(node, place):
+            bit = bits[step] if node % 2 == 0 else bits[steps - 1 - step]
+            return node ^ bit, place
+
+        return permute(value, node_count, local_count, target)
+
+    def sibling(value):
+        return permute(value, node_count, local_count, lambda n, p: (n ^ 1, p))
+
+    def rotate(value, k):
+        return permute(value, node_count, local_count, lambda n, p: (n, (p + k) % local_count))
+
+    onehot = expert_ids[:, :, None] == jnp.arange(LANES, dtype=jnp.int32)[None, None, :]
+    gates = jnp.sum(
+        jnp.where(onehot, gate_weights.astype(jnp.float32)[:, :, None], 0.0), axis=1
+    ).astype(jnp.bfloat16)
+    own = jnp.concatenate([tokens, grad_out, gates], axis=1)
+
+    arrived = [own] + [rotate(own, -k) for k in range(1, local_count)]
+    order = [[0], [1, local_count - 1], list(range(2, local_count - 1))] if local_count > 2 else [[k] for k in range(local_count)]
+    order = [g for g in order if g]
+    mine, theirs = [], []
+    for group in order:
+        held = jnp.concatenate([arrived[k][None, None] for k in group], axis=0)
+        for step in range(steps):
+            held = jnp.concatenate([held, exchange(held, step)], axis=1)
+        mine.append(held)
+        theirs.append(sibling(held))
+    spots = 1 << steps
+    half = local_count * spots * tok_count
+    rows = jnp.concatenate(
+        [v.reshape(-1, v.shape[-1]) for v in mine] + [v.reshape(-1, v.shape[-1]) for v in theirs],
+        axis=0,
+    )
+    flat_in = rows[:, :width]
+    flat_grad = rows[:, width : 2 * width]
+    me = lax.axis_index("node")
+    lane = lax.broadcasted_iota(jnp.int32, (1, LANES), 1) == me
+    flat_gate = jnp.sum(
+        jnp.where(lane, rows[:, 2 * width :].astype(jnp.float32), 0.0), axis=1, keepdims=True
+    )
+
+    gate_proj, up_proj, down_proj = w_gate[0], w_up[0], w_down[0]
+    gate_pre = jnp.dot(flat_in, gate_proj, preferred_element_type=jnp.float32)
+    up_pre = jnp.dot(flat_in, up_proj, preferred_element_type=jnp.float32)
+    sigmoid_val = jax.nn.sigmoid(gate_pre)
+    activated = gate_pre * sigmoid_val
+    slope = sigmoid_val * (1.0 + gate_pre * (1.0 - sigmoid_val))
+    hidden = (activated * up_pre).astype(jnp.bfloat16)
+    grad_hidden = lax.dot_general(
+        flat_grad, down_proj, CONTRACT_COLS, preferred_element_type=jnp.float32
+    )
+    gate_partial = jnp.sum(hidden.astype(jnp.float32) * grad_hidden, axis=1, keepdims=True)
+    scaled = flat_gate * grad_hidden
+    grad_gate_pre = (scaled * up_pre * slope).astype(jnp.bfloat16)
+    grad_up_pre = (scaled * activated).astype(jnp.bfloat16)
+    weighted = (flat_gate * hidden.astype(jnp.float32)).astype(jnp.bfloat16)
+
+    def returned(value):
+        value = value.astype(jnp.bfloat16)
+        total = value[:half].astype(jnp.float32) + sibling(value[half:]).astype(jnp.float32)
+        total = total.reshape(local_count, spots, tok_count, -1)
+        for step in reversed(range(steps)):
+            keep = 1 << step
+            sent = total[:, keep:].astype(jnp.bfloat16)
+            total = total[:, :keep] + exchange(sent, step).astype(jnp.float32)
+        total = total[:, 0].astype(jnp.bfloat16)
+        places = [k for g in order for k in g]
+        answer = total[0].astype(jnp.float32)
+        for i in range(1, local_count):
+            answer = answer + rotate(total[i], places[i]).astype(jnp.float32)
+        return answer
+
+    answers = []
+    for chunk in range(CHUNKS):
+        cols = slice(chunk * width // CHUNKS, (chunk + 1) * width // CHUNKS)
+        part = lax.dot_general(
+            grad_gate_pre, gate_proj[cols], CONTRACT_COLS, preferred_element_type=jnp.float32
+        ) + lax.dot_general(
+            grad_up_pre, up_proj[cols], CONTRACT_COLS, preferred_element_type=jnp.float32
+        )
+        if chunk == 0:
+            part = jnp.concatenate([part, jnp.where(lane, gate_partial, 0.0)], axis=1)
+        answers.append(returned(part))
+    first = width // CHUNKS
+    grad_in = jnp.concatenate([answers[0][:, :first]] + answers[1:], axis=1).astype(jnp.bfloat16)
+    sums = answers[0][:, first:].astype(jnp.bfloat16).astype(jnp.float32)
+    grad_gate = jnp.sum(jnp.where(onehot, sums[:, None, :], 0.0), axis=2).astype(jnp.bfloat16)
+
+    grad_down = lax.dot_general(
+        weighted, flat_grad, CONTRACT_ROWS, preferred_element_type=jnp.float32
+    ).astype(jnp.bfloat16)
+    grad_gate_w = lax.dot_general(
+        flat_in, grad_gate_pre, CONTRACT_ROWS, preferred_element_type=jnp.float32
+    ).astype(jnp.bfloat16)
+    grad_up_w = lax.dot_general(
+        flat_in, grad_up_pre, CONTRACT_ROWS, preferred_element_type=jnp.float32
+    ).astype(jnp.bfloat16)
+    return (grad_in, grad_gate, grad_gate_w[None], grad_up_w[None], grad_down[None])
+
+
+def slotted(tokens, grad_out, expert_ids, gate_weights, w_gate, w_up, w_down):
     tok_count = tokens.shape[0]
     width = tokens.shape[1]
     top_count = expert_ids.shape[1]
@@ -119,6 +243,15 @@
     return (grad_in, grad_gate, grad_gate_w[None], grad_up_w[None], grad_down[None])
 
 
+def per_device(tokens, grad_out, expert_ids, gate_weights, w_gate, w_up, w_down):
+    tok_count, top_count = expert_ids.shape
+    node_count = lax.axis_size("node")
+    capacity = max(2, 2 * tok_count * top_count // node_count)
+    paired = node_count & (node_count - 1) == 0 and 1 < node_count <= LANES
+    plan = dense if capacity >= tok_count and paired else slotted
+    return plan(tokens, grad_out, expert_ids, gate_weights, w_gate, w_up, w_down)
+
+
 def solution(mesh):
     placed = (
         P(("node", "local"), None),

time: 276 us -> 113 us (0.41)
  waiting for transfers between devices: 150 us -> 63.5 us
  blocking collectives: 66.4 us -> 0 us
  starting transfers between devices: 7.82 us -> 24.6 us
  matrix products: 30.5 us -> 16.5 us
  between operations: 13.9 us -> 0.98 us
  other arithmetic: 3.1 us -> 5.91 us
    all_gather x2 -> x0, waiting for transfers between devices: 98.2 us -> none  [the longest x1 65.4 us: per_device(): lax.all_gather(recv_grad[None], 'local', axis=0, tiled=True)]
    ppermute x0 -> x24, waiting for transfers between devices: none -> 63.5 us  [permute(): return lax.ppermute(value, AXES, pairs)]
    reduce_scatter x1 -> x0, waiting for transfers between devices: 46.4 us -> none  [per_device(): lax.psum_scatter(input_blocks.astype(jnp.bfloat16), 'local', scatter_dime...]
    all_to_all x3 -> x0, blocking collectives: 43.1 us -> none  [the longest x1 19 us: per_device(): lax.all_to_all(send_in, 'node', split_axis=0, concat_axis=0, tiled=True)]
    ppermute x0 -> x24, starting transfers between devices: none -> 24.6 us  [permute(): return lax.ppermute(value, AXES, pairs)]
    dot_general x13 -> x10, matrix products: 30.5 us -> 16.5 us  [the longest x1 3.22 us: dense(): lax.dot_general(flat_in, grad_up_pre, CONTRACT_ROWS, preferred_element_ty...]
    all_gather x1 -> x0, blocking collectives: 13.9 us -> none  [per_device(): lax.all_gather(recv_gate[None], 'local', axis=0, tiled=True)]
    unnamed x1 -> x0, blocking collectives: 9.39 us -> none
  transfers between devices with their start and end apart: 5 -> 24, of which waited for: 4 -> 11; matrix products, arithmetic and copies ran while one was open for 8% -> 11% of each run, Pallas kernels for 0% -> 0%
where the time goes in v1:
time: 113 us
  waiting for transfers between devices  63.5 us (56%)
  starting transfers between devices  24.6 us (22%)
  matrix products  16.5 us (15%)
  other arithmetic  5.91 us (5%)
  local copies, waits for them, and re-layouts  1.7 us (2%)
    ppermute x24, waiting for transfers between devices, permute(): return lax.ppermute(value, AXES, pairs)  63.5 us
    ppermute x24, starting transfers between devices, permute(): return lax.ppermute(value, AXES, pairs)  24.6 us
    dot_general x1, matrix products, dense(): lax.dot_general(flat_in, grad_up_pre, CONTRACT_ROWS, preferred_element_ty...  3.22 us
    dot_general x1, matrix products, dense(): lax.dot_general(flat_in, grad_gate_pre, CONTRACT_ROWS, preferred_element_...  3.02 us
    dot_general x1, matrix products, dense(): lax.dot_general(weighted, flat_grad, CONTRACT_ROWS, preferred_element_typ...  2.96 us
  transfers between devices with their start and end apart: 24, of which 11 were waited for; matrix products, arithmetic and copies ran while one was open for 11% of the time, Pallas kernels for 0%

profile of v1, /device:TPU:0, one launch (start us, length us, event | category | flops | bytes accessed | tf_op | source)
XLA Modules:
  0.0 113.2 jit_solution(1622433317989733368)
XLA Ops:
  0.6 0.7 convert_element_type.114
  1.3 0.8 select_reduce_fusion.2
  2.1 1.0 pad_maximum_fusion.8
  3.1 3.0 %collective-permute-start = (bf16[1,1,8,14464]{3,2,1,0:T(8,128)(2,1)S(1)}, bf16[1,1,8,14464]{3,2,1,0:T(8,128)(2,1)S(1)}, u32[]{:S(2)}, u32[]{:S(2)}) collective-permute-start(bf16[1,1,8,14464]{3,2,1,0:T(8,128)(2,1)S(1)} %get-tuple-element.13), channel_id=1, source_target_pairs={{0,8},{1,9},{2,10},{3,11},{4,20},{5,21},{6,22},{7,23},{8,0},{9,1},... | collective-permute-start | bytes 694280 | tf_op jit(solution)/shard_map/ppermute | solution.py:19
  6.1 1.6 %collective-permute-start.3 = (bf16[8,14464]{1,0:T(8,128)(2,1)S(1)}, bf16[8,14464]{1,0:T(8,128)(2,1)S(1)}, u32[]{:S(2)}, u32[]{:S(2)}) collective-permute-start(bf16[8,14464]{1,0:T(8,128)(2,1)S(1)} %get-tuple-element.12), channel_id=1, source_target_pairs={{0,1},{1,2},{2,3},{3,0},{4,5},{5,6},{6,7},{7,4},{8,9},{9,10},{10,1... | collective-permute-start | bytes 694280 | tf_op jit(solution)/shard_map/ppermute | solution.py:19
  7.6 2.2 %collective-permute-start.2 = (bf16[8,14464]{1,0:T(8,128)(2,1)S(1)}, bf16[8,14464]{1,0:T(8,128)(2,1)S(1)}, u32[]{:S(2)}, u32[]{:S(2)}) collective-permute-start(bf16[8,14464]{1,0:T(8,128)(2,1)S(1)} %get-tuple-element.12), channel_id=1, source_target_pairs={{0,3},{1,0},{2,1},{3,2},{4,7},{5,4},{6,5},{7,6},{8,11},{9,8},{10,9... | collective-permute-start | bytes 694280 | tf_op jit(solution)/shard_map/ppermute | solution.py:19
  9.9 0.8 collective-permute-start.6
  10.7 1.6 %collective-permute-start.1 = (bf16[1,2,8,14464]{3,2,1,0:T(8,128)(2,1)S(1)}, bf16[1,2,8,14464]{3,2,1,0:T(8,128)(2,1)S(1)}, u32[]{:S(2)}, u32[]{:S(2)}) collective-permute-start(bf16[1,2,8,14464]{3,2,1,0:T(8,128)(2,1)S(1)} %pad_maximum_fusion.5), channel_id=1, source_target_pairs={{0,16},{1,17},{2,18},{3,19},{4,12},{5,13},{6,14},{7,15},{8,24},{9,... | collective-permute-start | bytes 1388552 | tf_op jit(solution)/shard_map/ppermute | solution.py:19
  12.3 17.6 %collective-permute-done.6 = bf16[8,14464]{1,0:T(8,128)(2,1)S(1)} collective-permute-done((bf16[8,14464]{1,0:T(8,128)(2,1)S(1)}, bf16[8,14464]{1,0:T(8,128)(2,1)S(1)}, u32[]{:S(2)}, u32[]{:S(2)}) %collective-permute-start.6) | collective-permute-done | bytes 231456 | tf_op jit(solution)/shard_map/ppermute | solution.py:19
  29.9 1.5 %collective-permute-start.7 = (bf16[1,1,8,14464]{3,2,1,0:T(8,128)(2,1)S(1)}, bf16[1,1,8,14464]{3,2,1,0:T(8,128)(2,1)S(1)}, u32[]{:S(2)}, u32[]{:S(2)}) collective-permute-start(bf16[1,1,8,14464]{3,2,1,0:T(8,128)(2,1)S(1)} %bitcast.85), channel_id=1, source_target_pairs={{0,8},{1,9},{2,10},{3,11},{4,20},{5,21},{6,22},{7,23},{8,0},{9,1},... | collective-permute-start | bytes 694280 | tf_op jit(solution)/shard_map/ppermute | solution.py:19
  31.5 0.6 collective-permute-start.4
  32.1 3.9 %collective-permute-done.7 = bf16[1,1,8,14464]{3,2,1,0:T(8,128)(2,1)S(1)} collective-permute-done((bf16[1,1,8,14464]{3,2,1,0:T(8,128)(2,1)S(1)}, bf16[1,1,8,14464]{3,2,1,0:T(8,128)(2,1)S(1)}, u32[]{:S(2)}, u32[]{:S(2)}) %collective-permute-start.7) | collective-permute-done | bytes 231456 | tf_op jit(solution)/shard_map/ppermute | solution.py:19
  36.0 0.6 collective-permute-start.8
  36.6 7.3 %collective-permute-done.4 = bf16[2,1,8,14464]{3,2,1,0:T(8,128)(2,1)S(1)} collective-permute-done((bf16[2,1,8,14464]{3,2,1,0:T(8,128)(2,1)S(1)}, bf16[2,1,8,14464]{3,2,1,0:T(8,128)(2,1)S(1)}, u32[]{:S(2)}, u32[]{:S(2)}) %collective-permute-start.4) | collective-permute-done | bytes 462880 | tf_op jit(solution)/shard_map/ppermute | solution.py:19
  44.0 0.1 pad_maximum_fusion.3
  44.1 0.8 collective-permute-start.5
  44.8 0.1 pad_maximum_fusion.2
  45.1 0.1 pad_maximum_fusion.4
  45.2 0.7 collective-permute-start.11
  45.9 11.7 %collective-permute-done.5 = bf16[2,2,8,14464]{3,2,1,0:T(8,128)(2,1)S(1)} collective-permute-done((bf16[2,2,8,14464]{3,2,1,0:T(8,128)(2,1)S(1)}, bf16[2,2,8,14464]{3,2,1,0:T(8,128)(2,1)S(1)}, u32[]{:S(2)}, u32[]{:S(2)}) %collective-permute-start.5) | collective-permute-done | bytes 925728 | tf_op jit(solution)/shard_map/ppermute | solution.py:19
  57.6 0.2 pad_maximum_fusion
  58.0 0.2 constant_dynamic-update-slice_fusion.1
  58.2 0.1 bitcast_dynamic-update-slice_fusion.2
  58.3 0.1 bitcast_dynamic-update-slice_fusion.1
  58.5 3.3 %collective-permute-done.10 = bf16[2,4,8,14464]{3,2,1,0:T(8,128)(2,1)S(1)} collective-permute-done((bf16[2,4,8,14464]{3,2,1,0:T(8,128)(2,1)S(1)}, bf16[2,4,8,14464]{3,2,1,0:T(8,128)(2,1)S(1)}, u32[]{:S(2)}, u32[]{:S(2)}) %collective-permute-start.10) | collective-permute-done | bytes 1851424 | tf_op jit(solution)/shard_map/ppermute | solution.py:19
  61.7 0.2 constant_dynamic-update-slice_fusion
  62.0 0.1 bitcast_dynamic-update-slice_fusion
  62.1 1.6 %fusion.7 = f32[256,256]{0,1:T(8,128)S(1)} fusion(bf16[1,7168,256]{2,1,0:T(8,128)(2,1)S(1)} %copy-done, bf16[256,14464]{1,0:T(8,128)(2,1)S(1)} %bitcast_dynamic-update-slice_fusion), kind=kOutput, calls=%fused_computation.12 | convolution fusion | flops 939524096 | bytes 7602176 | tf_op jit(solution)/shard_map/dot_general | solution.py:74
  63.7 0.4 copy-done.1
  64.2 1.6 %fusion.5 = f32[256,256]{0,1:T(8,128)S(1)} fusion(bf16[1,7168,256]{2,1,0:T(8,128)(2,1)S(1)} %copy-done.1, bf16[256,14464]{1,0:T(8,128)(2,1)S(1)} %bitcast_dynamic-update-slice_fusion), kind=kOutput, calls=%fused_computation.10 | convolution fusion | flops 939524096 | bytes 7602176 | tf_op jit(solution)/shard_map/dot_general | solution.py:73
  65.8 0.1 select_reduce_fusion
  65.9 0.3 copy-done.3
  66.2 1.2 %fusion.30 = (bf16[256]{0:T(256)(128)(2,1)S(1)}, bf16[256,256]{0,1:T(8,128)(2,1)S(1)}, bf16[256,256]{0,1:T(8,128)(2,1)S(1)}, bf16[256,256]{0,1:T(8,128)(2,1)S(1)}) fusion(f32[256,256]{0,1:T(8,128)S(1)} %fusion.7, f32[256,256]{0,1:T(8,128)S(1)} %fusion.5, f32[256]{0:T(256)S(1)} %select_reduce_fusion, bf16[1,256,7168]{2,1,0:T(8,128)(2,1)S(1)} %copy-done.3, ...), kind=kOutput, calls=%fused_computation.61 | convolution fusion | flops 940769024 | bytes 8259072 | tf_op jit(solution)/shard_map/dot_general | solution.py:79
  67.4 0.7 fusion.18
  68.1 0.7 fusion.21
  68.8 0.8 fusion.4
  69.7 0.2 collective-permute-start.18
  69.9 0.1 select_convert_fusion
  70.0 0.7 fusion.3
  70.8 0.4 collective-permute-start.12
  71.2 3.0 %fusion.2 = bf16[1,256,7168]{2,1,0:T(8,128)(2,1)} fusion(bf16[256,14464]{1,0:T(8,128)(2,1)S(1)} %bitcast_dynamic-update-slice_fusion, bf16[256,256]{0,1:T(8,128)(2,1)S(1)} %get-tuple-element.6, f32[256]{0:T(256)S(1)} %select_reduce_fusion), kind=kOutput, calls=%fused_computation.5 | convolution fusion | flops 941555712 | bytes 7472128 | tf_op jit(solution)/shard_map/dot_general | solution.py:119
  74.2 3.0 %fusion = bf16[1,7168,256]{2,1,0:T(8,128)(2,1)} fusion(bf16[256,256]{0,1:T(8,128)(2,1)S(1)} %get-tuple-element.7, bf16[256,14464]{1,0:T(8,128)(2,1)S(1)} %bitcast_dynamic-update-slice_fusion), kind=kOutput, calls=%fused_computation.3 | convolution fusion | flops 941359104 | bytes 7471104 | tf_op jit(solution)/shard_map/dot_general | solution.py:122
  77.2 3.2 %fusion.1 = bf16[1,7168,256]{2,1,0:T(8,128)(2,1)} fusion(bf16[256,256]{0,1:T(8,128)(2,1)S(1)} %get-tuple-element.8, bf16[256,14464]{1,0:T(8,128)(2,1)S(1)} %bitcast_dynamic-update-slice_fusion), kind=kOutput, calls=%fused_computation.4 | convolution fusion | flops 941359104 | bytes 7471104 | tf_op jit(solution)/shard_map/dot_general | solution.py:125
  80.5 0.3 convert_add_fusion.1
  80.8 0.8 collective-permute-start.19
  81.6 0.2 convert_add_fusion
  81.9 1.4 %collective-permute-start.13 = (bf16[4,2,8,3712]{3,2,1,0:T(8,128)(2,1)S(1)}, bf16[4,2,8,3712]{3,2,1,0:T(8,128)(2,1)S(1)}, u32[]{:S(2)}, u32[]{:S(2)}) collective-permute-start(bf16[4,2,8,3712]{3,2,1,0:T(8,128)(2,1)S(1)} %slice.234), channel_id=1, source_target_pairs={{0,16},{1,17},{2,18},{3,19},{4,12},{5,13},{6,14},{7,15},{8,24},{9,... | collective-permute-start | bytes 1425416 | tf_op jit(solution)/shard_map/ppermute | solution.py:19
  83.3 6.1 %collective-permute-done.19 = bf16[4,2,8,3584]{3,2,1,0:T(8,128)(2,1)S(1)} collective-permute-done((bf16[4,2,8,3584]{3,2,1,0:T(8,128)(2,1)S(1)}, bf16[4,2,8,3584]{3,2,1,0:T(8,128)(2,1)S(1)}, u32[]{:S(2)}, u32[]{:S(2)}) %collective-permute-start.19) | collective-permute-done | bytes 458784 | tf_op jit(solution)/shard_map/ppermute | solution.py:19
  89.3 0.1 slice_add_fusion.1
  89.5 1.5 %collective-permute-start.20 = (bf16[4,1,8,3584]{3,2,1,0:T(8,128)(2,1)S(1)}, bf16[4,1,8,3584]{3,2,1,0:T(8,128)(2,1)S(1)}, u32[]{:S(2)}, u32[]{:S(2)}) collective-permute-start(bf16[4,1,8,3584]{3,2,1,0:T(8,128)(2,1)S(1)} %slice.237), channel_id=1, source_target_pairs={{0,8},{1,9},{2,10},{3,11},{4,20},{5,21},{6,22},{7,23},{8,0},{9,1},... | collective-permute-start | bytes 688136 | tf_op jit(solution)/shard_map/ppermute | solution.py:19
  91.0 5.9 %collective-permute-done.13 = bf16[4,2,8,3712]{3,2,1,0:T(8,128)(2,1)S(1)} collective-permute-done((bf16[4,2,8,3712]{3,2,1,0:T(8,128)(2,1)S(1)}, bf16[4,2,8,3712]{3,2,1,0:T(8,128)(2,1)S(1)}, u32[]{:S(2)}, u32[]{:S(2)}) %collective-permute-start.13) | collective-permute-done | bytes 475168 | tf_op jit(solution)/shard_map/ppermute | solution.py:19
  96.9 0.1 slice_add_fusion
  97.0 1.5 %collective-permute-start.14 = (bf16[4,1,8,3712]{3,2,1,0:T(8,128)(2,1)S(1)}, bf16[4,1,8,3712]{3,2,1,0:T(8,128)(2,1)S(1)}, u32[]{:S(2)}, u32[]{:S(2)}) collective-permute-start(bf16[4,1,8,3712]{3,2,1,0:T(8,128)(2,1)S(1)} %slice.236), channel_id=1, source_target_pairs={{0,8},{1,9},{2,10},{3,11},{4,20},{5,21},{6,22},{7,23},{8,0},{9,1},... | collective-permute-start | bytes 712712 | tf_op jit(solution)/shard_map/ppermute | solution.py:19
  98.7 2.0 %collective-permute-start.22 = (bf16[8,3584]{1,0:T(8,128)(2,1)S(1)}, bf16[8,3584]{1,0:T(8,128)(2,1)S(1)}, u32[]{:S(2)}, u32[]{:S(2)}) collective-permute-start(bf16[8,3584]{1,0:T(8,128)(2,1)S(1)} %get-tuple-element.16), channel_id=1, source_target_pairs={{0,3},{1,0},{2,1},{3,2},{4,7},{5,4},{6,5},{7,6},{8,11},{9,8},{10,9... | collective-permute-start | bytes 172040 | tf_op jit(solution)/shard_map/ppermute | solution.py:19
  100.7 0.5 collective-permute-start.21
  101.2 2.0 %collective-permute-done.14 = bf16[4,1,8,3712]{3,2,1,0:T(8,128)(2,1)S(1)} collective-permute-done((bf16[4,1,8,3712]{3,2,1,0:T(8,128)(2,1)S(1)}, bf16[4,1,8,3712]{3,2,1,0:T(8,128)(2,1)S(1)}, u32[]{:S(2)}, u32[]{:S(2)}) %collective-permute-start.14) | collective-permute-done | bytes 237600 | tf_op jit(solution)/shard_map/ppermute | solution.py:19
  103.3 0.5 collective-permute-start.17
  103.8 1.9 %collective-permute-start.16 = (bf16[8,3712]{1,0:T(8,128)(2,1)S(1)}, bf16[8,3712]{1,0:T(8,128)(2,1)S(1)}, u32[]{:S(2)}, u32[]{:S(2)}) collective-permute-start(bf16[8,3712]{1,0:T(8,128)(2,1)S(1)} %get-tuple-element.11), channel_id=1, source_target_pairs={{0,3},{1,0},{2,1},{3,2},{4,7},{5,4},{6,5},{7,6},{8,11},{9,8},{10,9... | collective-permute-start | bytes 178184 | tf_op jit(solution)/shard_map/ppermute | solution.py:19
  105.7 0.3 collective-permute-start.15
  106.1 0.7 collective-permute-done.21
  106.8 2.5 %collective-permute-done.17 = bf16[8,3712]{1,0:T(8,128)(2,1)S(1)} collective-permute-done((bf16[8,3712]{1,0:T(8,128)(2,1)S(1)}, bf16[8,3712]{1,0:T(8,128)(2,1)S(1)}, u32[]{:S(2)}, u32[]{:S(2)}) %collective-permute-start.17) | collective-permute-done | bytes 59424 | tf_op jit(solution)/shard_map/ppermute | solution.py:19
  109.3 2.5 %collective-permute-done.15 = bf16[8,3712]{1,0:T(8,128)(2,1)S(1)} collective-permute-done((bf16[8,3712]{1,0:T(8,128)(2,1)S(1)}, bf16[8,3712]{1,0:T(8,128)(2,1)S(1)}, u32[]{:S(2)}, u32[]{:S(2)}) %collective-permute-start.15) | collective-permute-done | bytes 59424 | tf_op jit(solution)/shard_map/ppermute | solution.py:19
  111.8 0.7 select_reduce_fusion.1
  112.5 0.7 pad_maximum_fusion.9
  (41 shorter events, 1.0 us)
Async XLA Ops:
  3.1 7.6 %collective-permute-start = (bf16[1,1,8,14464]{3,2,1,0:T(8,128)(2,1)S(1)}, bf16[1,1,8,14464]{3,2,1,0:T(8,128)(2,1)S(1)}, u32[]{:S(2)}, u32[]{:S(2)}) collective-permute-start(bf16[1,1,8,14464]{3,2,1,0:T(8,128)(2,1)S(1)} %get-tuple-element.13), channel_id=1, source_target_pairs={{0,8},{1,9},{2,10},{3,11},{4,20},{5,21},{6,22},{7,23},{8,0},{9,1},... | collective-permute-start | bytes 694280 | tf_op jit(solution)/shard_map/ppermute | solution.py:19
  6.1 25.4 %collective-permute-start.3 = (bf16[8,14464]{1,0:T(8,128)(2,1)S(1)}, bf16[8,14464]{1,0:T(8,128)(2,1)S(1)}, u32[]{:S(2)}, u32[]{:S(2)}) collective-permute-start(bf16[8,14464]{1,0:T(8,128)(2,1)S(1)} %get-tuple-element.12), channel_id=1, source_target_pairs={{0,1},{1,2},{2,3},{3,0},{4,5},{5,6},{6,7},{7,4},{8,9},{9,10},{10,1... | collective-permute-start | bytes 694280 | tf_op jit(solution)/shard_map/ppermute | solution.py:19
  7.6 23.8 %collective-permute-start.2 = (bf16[8,14464]{1,0:T(8,128)(2,1)S(1)}, bf16[8,14464]{1,0:T(8,128)(2,1)S(1)}, u32[]{:S(2)}, u32[]{:S(2)}) collective-permute-start(bf16[8,14464]{1,0:T(8,128)(2,1)S(1)} %get-tuple-element.12), channel_id=1, source_target_pairs={{0,3},{1,0},{2,1},{3,2},{4,7},{5,4},{6,5},{7,6},{8,11},{9,8},{10,9... | collective-permute-start | bytes 694280 | tf_op jit(solution)/shard_map/ppermute | solution.py:19
  9.9 20.0 %collective-permute-start.6 = (bf16[8,14464]{1,0:T(8,128)(2,1)S(1)}, bf16[8,14464]{1,0:T(8,128)(2,1)S(1)}, u32[]{:S(2)}, u32[]{:S(2)}) collective-permute-start(bf16[8,14464]{1,0:T(8,128)(2,1)S(1)} %get-tuple-element.12), channel_id=1, source_target_pairs={{0,2},{1,3},{2,0},{3,1},{4,6},{5,7},{6,4},{7,5},{8,10},{9,11},{10,... | collective-permute-start | bytes 694280 | tf_op jit(solution)/shard_map/ppermute | solution.py:19
  10.7 34.1 %collective-permute-start.1 = (bf16[1,2,8,14464]{3,2,1,0:T(8,128)(2,1)S(1)}, bf16[1,2,8,14464]{3,2,1,0:T(8,128)(2,1)S(1)}, u32[]{:S(2)}, u32[]{:S(2)}) collective-permute-start(bf16[1,2,8,14464]{3,2,1,0:T(8,128)(2,1)S(1)} %pad_maximum_fusion.5), channel_id=1, source_target_pairs={{0,16},{1,17},{2,18},{3,19},{4,12},{5,13},{6,14},{7,15},{8,24},{9,... | collective-permute-start | bytes 1388552 | tf_op jit(solution)/shard_map/ppermute | solution.py:19
  29.9 6.0 %collective-permute-start.7 = (bf16[1,1,8,14464]{3,2,1,0:T(8,128)(2,1)S(1)}, bf16[1,1,8,14464]{3,2,1,0:T(8,128)(2,1)S(1)}, u32[]{:S(2)}, u32[]{:S(2)}) collective-permute-start(bf16[1,1,8,14464]{3,2,1,0:T(8,128)(2,1)S(1)} %bitcast.85), channel_id=1, source_target_pairs={{0,8},{1,9},{2,10},{3,11},{4,20},{5,21},{6,22},{7,23},{8,0},{9,1},... | collective-permute-start | bytes 694280 | tf_op jit(solution)/shard_map/ppermute | solution.py:19
  31.5 12.5 %collective-permute-start.4 = (bf16[2,1,8,14464]{3,2,1,0:T(8,128)(2,1)S(1)}, bf16[2,1,8,14464]{3,2,1,0:T(8,128)(2,1)S(1)}, u32[]{:S(2)}, u32[]{:S(2)}) collective-permute-start(bf16[2,1,8,14464]{3,2,1,0:T(8,128)(2,1)S(1)} %pad_maximum_fusion.6), channel_id=1, source_target_pairs={{0,8},{1,9},{2,10},{3,11},{4,20},{5,21},{6,22},{7,23},{8,0},{9,1},... | collective-permute-start | bytes 1388552 | tf_op jit(solution)/shard_map/ppermute | solution.py:19
  36.0 9.1 %collective-permute-start.8 = (bf16[1,2,8,14464]{3,2,1,0:T(8,128)(2,1)S(1)}, bf16[1,2,8,14464]{3,2,1,0:T(8,128)(2,1)S(1)}, u32[]{:S(2)}, u32[]{:S(2)}) collective-permute-start(bf16[1,2,8,14464]{3,2,1,0:T(8,128)(2,1)S(1)} %pad_maximum_fusion.7), channel_id=1, source_target_pairs={{0,16},{1,17},{2,18},{3,19},{4,12},{5,13},{6,14},{7,15},{8,24},{9,... | collective-permute-start | bytes 1388552 | tf_op jit(solution)/shard_map/ppermute | solution.py:19
  44.1 13.5 %collective-permute-start.5 = (bf16[2,2,8,14464]{3,2,1,0:T(8,128)(2,1)S(1)}, bf16[2,2,8,14464]{3,2,1,0:T(8,128)(2,1)S(1)}, u32[]{:S(2)}, u32[]{:S(2)}) collective-permute-start(bf16[2,2,8,14464]{3,2,1,0:T(8,128)(2,1)S(1)} %pad_maximum_fusion.3), channel_id=1, source_target_pairs={{0,16},{1,17},{2,18},{3,19},{4,12},{5,13},{6,14},{7,15},{8,24},{9,... | collective-permute-start | bytes 2777096 | tf_op jit(solution)/shard_map/ppermute | solution.py:19
  45.0 13.4 %collective-permute-start.9 = (bf16[1,4,8,14464]{3,2,1,0:T(8,128)(2,1)S(1)}, bf16[1,4,8,14464]{3,2,1,0:T(8,128)(2,1)S(1)}, u32[]{:S(2)}, u32[]{:S(2)}) collective-permute-start(bf16[1,4,8,14464]{3,2,1,0:T(8,128)(2,1)S(1)} %pad_maximum_fusion.2), channel_id=1, source_target_pairs={{0,4},{1,5},{2,6},{3,7},{4,0},{5,1},{6,2},{7,3},{8,12},{9,13},{10,... | collective-permute-start | bytes 2777096 | tf_op jit(solution)/shard_map/ppermute | solution.py:19
  45.2 16.7 %collective-permute-start.11 = (bf16[1,4,8,14464]{3,2,1,0:T(8,128)(2,1)S(1)}, bf16[1,4,8,14464]{3,2,1,0:T(8,128)(2,1)S(1)}, u32[]{:S(2)}, u32[]{:S(2)}) collective-permute-start(bf16[1,4,8,14464]{3,2,1,0:T(8,128)(2,1)S(1)} %pad_maximum_fusion.4), channel_id=1, source_target_pairs={{0,4},{1,5},{2,6},{3,7},{4,0},{5,1},{6,2},{7,3},{8,12},{9,13},{10,... | collective-permute-start | bytes 2777096 | tf_op jit(solution)/shard_map/ppermute | solution.py:19
  57.9 3.9 %collective-permute-start.10 = (bf16[2,4,8,14464]{3,2,1,0:T(8,128)(2,1)S(1)}, bf16[2,4,8,14464]{3,2,1,0:T(8,128)(2,1)S(1)}, u32[]{:S(2)}, u32[]{:S(2)}) collective-permute-start(bf16[2,4,8,14464]{3,2,1,0:T(8,128)(2,1)S(1)} %pad_maximum_fusion), channel_id=1, source_target_pairs={{0,4},{1,5},{2,6},{3,7},{4,0},{5,1},{6,2},{7,3},{8,12},{9,13},{10,... | collective-permute-start | bytes 5554184 | tf_op jit(solution)/shard_map/ppermute | solution.py:19
  58.3 3.8 %copy-start = (bf16[1,7168,256]{2,1,0:T(8,128)(2,1)S(1)}, bf16[1,7168,256]{2,1,0:T(8,128)(2,1)}, u32[]{:S(2)}) copy-start(bf16[1,7168,256]{2,1,0:T(8,128)(2,1)} %param.12) | copy-start | bytes 11010052
  62.1 2.0 %copy-start.1 = (bf16[1,7168,256]{2,1,0:T(8,128)(2,1)S(1)}, bf16[1,7168,256]{2,1,0:T(8,128)(2,1)}, u32[]{:S(2)}) copy-start(bf16[1,7168,256]{2,1,0:T(8,128)(2,1)} %param.11) | copy-start | bytes 11010052
  64.2 2.0 %copy-start.3 = (bf16[1,256,7168]{2,1,0:T(8,128)(2,1)S(1)}, bf16[1,256,7168]{2,1,0:T(8,128)(2,1)}, u32[]{:S(2)}) copy-start(bf16[1,256,7168]{2,1,0:T(8,128)(2,1)} %param.13) | copy-start | bytes 11010052
  69.7 10.8 %collective-permute-start.18 = (bf16[128,3584]{1,0:T(8,128)(2,1)S(1)}, bf16[128,3584]{1,0:T(8,128)(2,1)S(1)}, u32[]{:S(2)}, u32[]{:S(2)}) collective-permute-start(bf16[128,3584]{1,0:T(8,128)(2,1)S(1)} %slice.161), channel_id=1, source_target_pairs={{0,4},{1,5},{2,6},{3,7},{4,0},{5,1},{6,2},{7,3},{8,12},{9,13},{10,... | collective-permute-start | bytes 2752520 | tf_op jit(solution)/shard_map/ppermute | solution.py:19
  70.8 10.8 %collective-permute-start.12 = (bf16[128,3712]{1,0:T(8,128)(2,1)S(1)}, bf16[128,3712]{1,0:T(8,128)(2,1)S(1)}, u32[]{:S(2)}, u32[]{:S(2)}) collective-permute-start(bf16[128,3712]{1,0:T(8,128)(2,1)S(1)} %pad_maximum_fusion.1), channel_id=1, source_target_pairs={{0,4},{1,5},{2,6},{3,7},{4,0},{5,1},{6,2},{7,3},{8,12},{9,13},{10,... | collective-permute-start | bytes 2850824 | tf_op jit(solution)/shard_map/ppermute | solution.py:19
  80.8 8.5 %collective-permute-start.19 = (bf16[4,2,8,3584]{3,2,1,0:T(8,128)(2,1)S(1)}, bf16[4,2,8,3584]{3,2,1,0:T(8,128)(2,1)S(1)}, u32[]{:S(2)}, u32[]{:S(2)}) collective-permute-start(bf16[4,2,8,3584]{3,2,1,0:T(8,128)(2,1)S(1)} %slice.235), channel_id=1, source_target_pairs={{0,16},{1,17},{2,18},{3,19},{4,12},{5,13},{6,14},{7,15},{8,24},{9,... | collective-permute-start | bytes 1376264 | tf_op jit(solution)/shard_map/ppermute | solution.py:19
  81.9 15.0 %collective-permute-start.13 = (bf16[4,2,8,3712]{3,2,1,0:T(8,128)(2,1)S(1)}, bf16[4,2,8,3712]{3,2,1,0:T(8,128)(2,1)S(1)}, u32[]{:S(2)}, u32[]{:S(2)}) collective-permute-start(bf16[4,2,8,3712]{3,2,1,0:T(8,128)(2,1)S(1)} %slice.234), channel_id=1, source_target_pairs={{0,16},{1,17},{2,18},{3,19},{4,12},{5,13},{6,14},{7,15},{8,24},{9,... | collective-permute-start | bytes 1425416 | tf_op jit(solution)/shard_map/ppermute | solution.py:19
  89.5 22.3 %copy-start.2 = (s32[8,4]{0,1:T(4,128)S(1)}, s32[8,4]{0,1:T(4,128)}, u32[]{:S(2)}) copy-start(s32[8,4]{0,1:T(4,128)} %param.9) | copy-start | bytes 388
  89.5 9.1 %collective-permute-start.20 = (bf16[4,1,8,3584]{3,2,1,0:T(8,128)(2,1)S(1)}, bf16[4,1,8,3584]{3,2,1,0:T(8,128)(2,1)S(1)}, u32[]{:S(2)}, u32[]{:S(2)}) collective-permute-start(bf16[4,1,8,3584]{3,2,1,0:T(8,128)(2,1)S(1)} %slice.237), channel_id=1, source_target_pairs={{0,8},{1,9},{2,10},{3,11},{4,20},{5,21},{6,22},{7,23},{8,0},{9,1},... | collective-permute-start | bytes 688136 | tf_op jit(solution)/shard_map/ppermute | solution.py:19
  97.0 6.2 %collective-permute-start.14 = (bf16[4,1,8,3712]{3,2,1,0:T(8,128)(2,1)S(1)}, bf16[4,1,8,3712]{3,2,1,0:T(8,128)(2,1)S(1)}, u32[]{:S(2)}, u32[]{:S(2)}) collective-permute-start(bf16[4,1,8,3712]{3,2,1,0:T(8,128)(2,1)S(1)} %slice.236), channel_id=1, source_target_pairs={{0,8},{1,9},{2,10},{3,11},{4,20},{5,21},{6,22},{7,23},{8,0},{9,1},... | collective-permute-start | bytes 712712 | tf_op jit(solution)/shard_map/ppermute | solution.py:19
  98.6 7.1 %collective-permute-start.23 = (bf16[8,3584]{1,0:T(8,128)(2,1)S(1)}, bf16[8,3584]{1,0:T(8,128)(2,1)S(1)}, u32[]{:S(2)}, u32[]{:S(2)}) collective-permute-start(bf16[8,3584]{1,0:T(8,128)(2,1)S(1)} %get-tuple-element.15), channel_id=1, source_target_pairs={{0,2},{1,3},{2,0},{3,1},{4,6},{5,7},{6,4},{7,5},{8,10},{9,11},{10,... | collective-permute-start | bytes 172040 | tf_op jit(solution)/shard_map/ppermute | solution.py:19
  98.7 7.4 %collective-permute-start.22 = (bf16[8,3584]{1,0:T(8,128)(2,1)S(1)}, bf16[8,3584]{1,0:T(8,128)(2,1)S(1)}, u32[]{:S(2)}, u32[]{:S(2)}) collective-permute-start(bf16[8,3584]{1,0:T(8,128)(2,1)S(1)} %get-tuple-element.16), channel_id=1, source_target_pairs={{0,3},{1,0},{2,1},{3,2},{4,7},{5,4},{6,5},{7,6},{8,11},{9,8},{10,9... | collective-permute-start | bytes 172040 | tf_op jit(solution)/shard_map/ppermute | solution.py:19
  100.7 6.1 %collective-permute-start.21 = (bf16[8,3584]{1,0:T(8,128)(2,1)S(1)}, bf16[8,3584]{1,0:T(8,128)(2,1)S(1)}, u32[]{:S(2)}, u32[]{:S(2)}) collective-permute-start(bf16[8,3584]{1,0:T(8,128)(2,1)S(1)} %get-tuple-element.14), channel_id=1, source_target_pairs={{0,1},{1,2},{2,3},{3,0},{4,5},{5,6},{6,7},{7,4},{8,9},{9,10},{10,1... | collective-permute-start | bytes 172040 | tf_op jit(solution)/shard_map/ppermute | solution.py:19
  103.3 6.0 %collective-permute-start.17 = (bf16[8,3712]{1,0:T(8,128)(2,1)S(1)}, bf16[8,3712]{1,0:T(8,128)(2,1)S(1)}, u32[]{:S(2)}, u32[]{:S(2)}) collective-permute-start(bf16[8,3712]{1,0:T(8,128)(2,1)S(1)} %get-tuple-element.10), channel_id=1, source_target_pairs={{0,2},{1,3},{2,0},{3,1},{4,6},{5,7},{6,4},{7,5},{8,10},{9,11},{10,... | collective-permute-start | bytes 178184 | tf_op jit(solution)/shard_map/ppermute | solution.py:19
  103.8 5.5 %collective-permute-start.16 = (bf16[8,3712]{1,0:T(8,128)(2,1)S(1)}, bf16[8,3712]{1,0:T(8,128)(2,1)S(1)}, u32[]{:S(2)}, u32[]{:S(2)}) collective-permute-start(bf16[8,3712]{1,0:T(8,128)(2,1)S(1)} %get-tuple-element.11), channel_id=1, source_target_pairs={{0,3},{1,0},{2,1},{3,2},{4,7},{5,4},{6,5},{7,6},{8,11},{9,8},{10,9... | collective-permute-start | bytes 178184 | tf_op jit(solution)/shard_map/ppermute | solution.py:19
  105.7 6.0 %collective-permute-start.15 = (bf16[8,3712]{1,0:T(8,128)(2,1)S(1)}, bf16[8,3712]{1,0:T(8,128)(2,1)S(1)}, u32[]{:S(2)}, u32[]{:S(2)}) collective-permute-start(bf16[8,3712]{1,0:T(8,128)(2,1)S(1)} %get-tuple-element.9), channel_id=1, source_target_pairs={{0,1},{1,2},{2,3},{3,0},{4,5},{5,6},{6,7},{7,4},{8,9},{9,10},{10,1... | collective-permute-start | bytes 178184 | tf_op jit(solution)/shard_map/ppermute | solution.py:19

commit v2 on v0

--- a/solution.py
+++ b/solution.py
@@ -1,10 +1,368 @@
+import functools
+
 import jax
 import jax.numpy as jnp
 from jax import lax
+from jax.experimental import pallas as pl
+from jax.experimental.pallas import tpu as pltpu
 from jax.sharding import PartitionSpec as P
 
-
-def per_device(tokens, grad_out, expert_ids, gate_weights, w_gate, w_up, w_down):
+AXES = ("node", "local")
+LANES = 128
+NO_COST = pl.CostEstimate(flops=0, bytes_accessed=0, transcendentals=0)
+CONTRACT_ROWS = (((0,), (0,)), ((), ()))
+CONTRACT_COLS = (((1,), (1,)), ((), ()))
+
+
+def whole(count):
+    return (pl.BlockSpec(memory_space=pltpu.VMEM),) * count
+
+
+def in_hbm(value):
+    return pltpu.with_memory_space_constraint(value, pltpu.HBM)
+
+
+def pack_kernel(
+    tokens_hbm, grad_hbm, ids_hbm, gates_hbm, own_ref, ids_ref, gates_ref, square, sems
+):
+    width = tokens_hbm.shape[1]
+    pairs = (
+        (ids_hbm, ids_ref),
+        (gates_hbm, gates_ref),
+        (tokens_hbm, own_ref.at[:, pl.ds(0, width)]),
+        (grad_hbm, own_ref.at[:, pl.ds(width, width)]),
+    )
+    copies = [pltpu.make_async_copy(*pair, sems.at[i]) for i, pair in enumerate(pairs)]
+    for copy in copies:
+        copy.start()
+    copies[0].wait()
+    copies[1].wait()
+    ids, gates = ids_ref[...], gates_ref[...].astype(jnp.float32)
+    top_count, tok_count = ids.shape
+    experts = lax.broadcasted_iota(jnp.int32, (LANES, tok_count), 0)
+    table = jnp.zeros(experts.shape, jnp.float32)
+    for k in range(top_count):
+        table = table + jnp.where(experts == ids[k : k + 1], gates[k : k + 1], 0.0)
+    square[...] = jnp.zeros(square.shape, jnp.float32)
+    square[:, :tok_count] = table
+    own_ref[:, 2 * width :] = square[...].T[:tok_count].astype(jnp.bfloat16)
+    copies[2].wait()
+    copies[3].wait()
+
+
+def pack(tokens, grad_out, expert_ids, gate_weights):
+    rows, width = tokens.shape
+    hbm = pl.BlockSpec(memory_space=pl.ANY)
+    return pl.pallas_call(
+        pack_kernel,
+        out_shape=jax.ShapeDtypeStruct((rows, 2 * width + LANES), tokens.dtype),
+        in_specs=[hbm] * 4,
+        out_specs=whole(1)[0],
+        scratch_shapes=[
+            pltpu.VMEM(expert_ids.T.shape, expert_ids.dtype),
+            pltpu.VMEM(gate_weights.T.shape, gate_weights.dtype),
+            pltpu.VMEM((LANES, LANES), jnp.float32),
+            pltpu.SemaphoreType.DMA((4,)),
+        ],
+        compiler_params=pltpu.CompilerParams(vmem_limit_bytes=4 << 20),
+        cost_estimate=NO_COST,
+    )(*(in_hbm(v) for v in (tokens, grad_out, expert_ids.T, gate_weights.T)))
+
+
+def finish_kernel(*refs):
+    *terms, ids_ref, rows_ref, gates_ref, square = refs
+    width = rows_ref.shape[1]
+    total = terms[0][...].astype(jnp.float32)
+    for term in terms[1:]:
+        total = total + term[...].astype(jnp.float32)
+    rows_ref[...] = total[:, :width].astype(jnp.bfloat16)
+    ids = ids_ref[...]
+    top_count, tok_count = ids.shape
+    square[...] = jnp.zeros(square.shape, jnp.float32)
+    square[:tok_count] = total[:, width:].astype(jnp.bfloat16).astype(jnp.float32)
+    sums = square[...].T[:, :tok_count]
+    experts = lax.broadcasted_iota(jnp.int32, sums.shape, 0)
+    slots = lax.broadcasted_iota(jnp.int32, ids.shape, 0)
+    picked = jnp.zeros(ids.shape, jnp.float32)
+    for k in range(top_count):
+        value = jnp.sum(jnp.where(experts == ids[k : k + 1], sums, 0.0), axis=0, keepdims=True)
+        picked = picked + jnp.where(slots == k, value, 0.0)
+    gates_ref[...] = picked.astype(jnp.bfloat16)
+
+
+def finish(terms, expert_ids):
+    rows, columns = terms[0].shape
+    ids = expert_ids.T
+    grad_in, grad_gate = pl.pallas_call(
+        finish_kernel,
+        out_shape=(
+            jax.ShapeDtypeStruct((rows, columns - LANES), jnp.bfloat16),
+            jax.ShapeDtypeStruct(ids.shape, jnp.bfloat16),
+        ),
+        in_specs=list(whole(len(terms) + 1)),
+        out_specs=whole(2),
+        scratch_shapes=[pltpu.VMEM((LANES, LANES), jnp.float32)],
+        compiler_params=pltpu.CompilerParams(vmem_limit_bytes=4 << 20),
+        cost_estimate=NO_COST,
+    )(*terms, ids)
+    return grad_in, grad_gate.T
+
+
+def weights_kernel(*refs, blocks, groups, width, chunk):
+    rows, refs = refs[:blocks], refs[blocks:]
+    da, du, hw, refs = refs[:groups], refs[groups : 2 * groups], refs[2 * groups : 3 * groups], refs[3 * groups :]
+    outs, parts, sems = refs[:3], refs[3:6], refs[6]
+
+    def stacked(pieces, span=slice(None)):
+        return jnp.concatenate([p[:, span] for p in pieces], axis=0)
+
+    def outer(left, right):
+        product = lax.dot_general(left, right, CONTRACT_ROWS, preferred_element_type=jnp.float32)
+        return product.astype(jnp.bfloat16)
+
+    gate_side, up_side, down_side = stacked(da), stacked(du), stacked(hw)
+    copies = []
+    for c in range(width // chunk):
+        span = pl.ds(c * chunk, chunk)
+        part_in = stacked(rows, span)
+        parts[0][span, :] = outer(part_in, gate_side)
+        parts[1][span, :] = outer(part_in, up_side)
+        parts[2][:, span] = outer(down_side, stacked(rows, pl.ds(width + c * chunk, chunk)))
+        places = ((span, slice(None)), (span, slice(None)), (slice(None), span))
+        for i, place in enumerate(places):
+            copies.append(pltpu.make_async_copy(parts[i].at[place], outs[i].at[place], sems.at[i, c]))
+            copies[-1].start()
+    for copy in copies:
+        copy.wait()
+
+
+def weight_terms(rows, da, du, hw, width):
+    hid = da[0].shape[1]
+    chunk = next(c for c in (1024, 512, 256, 128) if width % c == 0)
+    shapes = ((width, hid), (width, hid), (hid, width))
+    hbm = pl.BlockSpec(memory_space=pl.ANY)
+    return pl.pallas_call(
+        functools.partial(
+            weights_kernel, blocks=len(rows), groups=len(da), width=width, chunk=chunk
+        ),
+        out_shape=tuple(jax.ShapeDtypeStruct(s, jnp.bfloat16) for s in shapes),
+        in_specs=list(whole(len(rows) + 3 * len(da))),
+        out_specs=(hbm,) * 3,
+        scratch_shapes=[
+            *(pltpu.VMEM(s, jnp.bfloat16) for s in shapes),
+            pltpu.SemaphoreType.DMA((3, width // chunk)),
+        ],
+        compiler_params=pltpu.CompilerParams(vmem_limit_bytes=28 << 20),
+        cost_estimate=NO_COST,
+    )(*rows, *da, *du, *hw)
+
+
+def in_vmem(value):
+    return pltpu.with_memory_space_constraint(value, pltpu.VMEM)
+
+
+def group_kernel(*refs, width, chunk, loads):
+    me_ref, held_ref, other_ref = refs[:3]
+    sources, refs = refs[3:6], refs[6:]
+    mine_ref, send_ref, da_ref, du_ref, hw_ref = refs[:5]
+    spans = [pl.ds(c * chunk, chunk) for c in range(width // chunk)]
+    copies = [[] for _ in spans]
+    gate_w, up_w, down_w = refs[5:8] if loads else sources
+    if loads:
+        sems = refs[8]
+        for c, span in enumerate(spans):
+            places = ((span, slice(None)), (span, slice(None)), (slice(None), span))
+            for i, place in enumerate(places):
+                copies[c].append(
+                    pltpu.make_async_copy(sources[i].at[place], refs[5 + i].at[place], sems.at[i, c])
+                )
+                copies[c][-1].start()
+    half = held_ref.shape[0]
+
+    def rows(start, size):
+        span = pl.ds(start, size)
+        return jnp.concatenate([held_ref[:, span], other_ref[:, span]], axis=0)
+
+    extra = rows(2 * width, LANES).astype(jnp.float32)
+    named = lax.broadcasted_iota(jnp.int32, extra.shape, 1) == me_ref[0]
+    flat_gate = jnp.sum(jnp.where(named, extra, 0.0), axis=1, keepdims=True)
+
+    def plain(a, b):
+        return lax.dot_general(a, b, (((1,), (0,)), ((), ())), preferred_element_type=jnp.float32)
+
+    def turned(a, b):
+        return lax.dot_general(a, b, CONTRACT_COLS, preferred_element_type=jnp.float32)
+
+    gate_pre = up_pre = grad_hidden = 0.0
+    for c, span in enumerate(spans):
+        for copy in copies[c]:
+            copy.wait()
+        part_in = rows(c * chunk, chunk)
+        gate_pre += plain(part_in, gate_w[span, :])
+        up_pre += plain(part_in, up_w[span, :])
+        grad_hidden += turned(rows(width + c * chunk, chunk), down_w[:, span])
+    sigmoid_val = jax.nn.sigmoid(gate_pre)
+    activated = gate_pre * sigmoid_val
+    slope = sigmoid_val * (1.0 + gate_pre * (1.0 - sigmoid_val))
+    hidden = (activated * up_pre).astype(jnp.bfloat16).astype(jnp.float32)
+    gate_partial = jnp.sum(hidden * grad_hidden, axis=1, keepdims=True)
+    scaled = flat_gate * grad_hidden
+    grad_gate_pre = (scaled * up_pre * slope).astype(jnp.bfloat16)
+    grad_up_pre = (scaled * activated).astype(jnp.bfloat16)
+    da_ref[...] = grad_gate_pre
+    du_ref[...] = grad_up_pre
+    hw_ref[...] = (flat_gate * hidden).astype(jnp.bfloat16)
+    for span in spans:
+        part = turned(grad_gate_pre, gate_w[span, :]) + turned(grad_up_pre, up_w[span, :])
+        part = part.astype(jnp.bfloat16)
+        mine_ref[:, span] = part[:half]
+        send_ref[:, span] = part[half:]
+    gate_term = jnp.where(named, gate_partial, 0.0).astype(jnp.bfloat16)
+    last = pl.ds(width, LANES)
+    mine_ref[:, last] = gate_term[:half]
+    send_ref[:, last] = gate_term[half:]
+
+
+def group_terms(held, other, weights, loads):
+    count, columns = held.shape
+    width, hid = weights[0].shape
+    chunk = next(c for c in (1024, 512, 256, 128) if width % c == 0)
+    me = lax.axis_index("node").astype(jnp.int32).reshape(1)
+    back = jax.ShapeDtypeStruct((count, width + LANES), jnp.bfloat16)
+    unit = jax.ShapeDtypeStruct((2 * count, hid), jnp.bfloat16)
+    shapes = (back, back, unit, unit, unit)
+    if loads:
+        shapes += tuple(pltpu.VMEM(w.shape, w.dtype) for w in weights)
+    space = pl.ANY if loads else pltpu.VMEM
+    place = in_hbm if loads else in_vmem
+    *terms, = pl.pallas_call(
+        functools.partial(group_kernel, width=width, chunk=chunk, loads=loads),
+        out_shape=shapes,
+        in_specs=[
+            pl.BlockSpec(memory_space=pltpu.SMEM),
+            *whole(2),
+            *(pl.BlockSpec(memory_space=space),) * 3,
+        ],
+        out_specs=whole(len(shapes)),
+        scratch_shapes=[pltpu.SemaphoreType.DMA((3, width // chunk))] if loads else [],
+        compiler_params=pltpu.CompilerParams(vmem_limit_bytes=16 << 20),
+        cost_estimate=NO_COST,
+    )(me, held, other, *(place(w) for w in weights))
+    return terms[:5], terms[5:]
+
+
+def dense(tokens, grad_out, expert_ids, gate_weights, w_gate, w_up, w_down):
+    tok_count, width = tokens.shape
+    node_count = lax.axis_size("node")
+    local_count = lax.axis_size("local")
+    clock = []
+
+    def tick(*values):
+        held = lax.optimization_barrier((*values, *clock))[: len(values)]
+        return held[0] if len(values) == 1 else held
+
+    def tock(value):
+        clock[:] = [value]
+        return value
+
+    def permute(value, target):
+        pairs = []
+        for node in range(node_count):
+            for place in range(local_count):
+                to_node, to_place = target(node, place)
+                pairs.append((node * local_count + place, to_node * local_count + to_place))
+        return lax.ppermute(value, AXES, pairs)
+
+    def cross(value, step):
+        return permute(value, lambda n, p: (n ^ (2 if (n % 2 == 0) == (step == 0) else 4), p))
+
+    def sibling(value):
+        return permute(value, lambda n, p: (n ^ 1, p))
+
+    def rotate(value, k):
+        return permute(value, lambda n, p: (n, (p + k) % local_count))
+
+    def joined(*values):
+        return jnp.concatenate(values, axis=1)
+
+    own = pack(tokens, grad_out, expert_ids, gate_weights)[None, None]
+
+    weights = (w_gate[0], w_up[0], w_down[0])
+
+    def terms(held, other, weights, loads):
+        flat = [v.reshape(-1, v.shape[-1]) for v in (held, other)]
+        return group_terms(*flat, weights, loads)
+
+    def summed(mine, received):
+        total = mine.astype(jnp.float32) + received.astype(jnp.float32)
+        return total.reshape(-1, 4, tok_count, total.shape[-1]).astype(jnp.bfloat16)
+
+    def folded(total, received):
+        keep = received.shape[1]
+        return (total[:, :keep].astype(jnp.float32) + received.astype(jnp.float32)).astype(jnp.bfloat16)
+
+    def upper(total):
+        return total[:, total.shape[1] // 2 :]
+
+
+    weights = (w_gate[0], w_up[0], w_down[0])
+    near_x = cross(own, 0)
+    up_in = rotate(own, -1)
+    down_in = rotate(own, 1)
+    near = tock(joined(*tick(own, near_x)))
+    near_y = cross(near, 1)
+    up = tock(tick(up_in))
+    up_x = cross(up, 0)
+    far_in = rotate(up, -1)
+    down = tock(tick(down_in))
+    down_x = cross(down, 0)
+    up = tock(joined(*tick(up, up_x)))
+    up_y = cross(up, 1)
+    far = tock(tick(far_in))
+    far_x = cross(far, 0)
+    down = tock(joined(*tick(down, down_x)))
+    down_y = cross(down, 1)
+    up = tock(joined(*tick(up, up_y)))
+    near = tock(joined(*tick(near, near_y)))
+    first = tock(jnp.concatenate(tick(near, up), axis=0))
+    first_other = sibling(first)
+    far = tock(joined(*tick(far, far_x)))
+    far_y = cross(far, 1)
+    down = tock(joined(*tick(down, down_y)))
+    first_terms, weights = terms(*tick(first, first_other), weights, True)
+    tock(first_terms[0])
+    first_back = sibling(first_terms[1])
+    far = tock(joined(*tick(far, far_y)))
+    second = tock(jnp.concatenate(tick(down, far), axis=0))
+    second_other = sibling(second)
+    first_sum = tock(summed(*tick(first_terms[0], first_back)))
+    first_r1 = cross(upper(first_sum), 1)
+    second_terms, _ = terms(*tick(second, second_other), weights, False)
+    tock(second_terms[0])
+    second_back = sibling(second_terms[1])
+    first_sum = tock(folded(*tick(first_sum, first_r1)))
+    first_r2 = cross(upper(first_sum), 0)
+    second_sum = tock(summed(*tick(second_terms[0], second_back)))
+    second_r1 = cross(upper(second_sum), 1)
+    first_sum = tock(folded(*tick(first_sum, first_r2)))
+    from_up = rotate(first_sum[1], 1)
+    second_sum = tock(folded(*tick(second_sum, second_r1)))
+    second_r2 = cross(upper(second_sum), 0)
+    from_up = tock(tick(from_up))
+    second_sum = tock(folded(*tick(second_sum, second_r2)))
+    from_down = rotate(second_sum[0], -1)
+    from_far = rotate(second_sum[1], 2)
+    rows = [v.reshape(-1, v.shape[-1]) for v in (first, first_other, second, second_other)]
+    rows[0] = tick(rows[0])
+    sides = [[t[i] for t in (first_terms, second_terms)] for i in (2, 3, 4)]
+    grad_gate_w, grad_up_w, grad_down = weight_terms(rows, *sides, width)
+    tock(grad_down)
+    ends = tick(first_sum[0], from_up, from_down, from_far)
+    grad_in, grad_gate = finish([e[0] for e in ends], expert_ids)
+    return (grad_in, grad_gate, grad_gate_w[None], grad_up_w[None], grad_down[None])
+
+
+def slotted(tokens, grad_out, expert_ids, gate_weights, w_gate, w_up, w_down):
     tok_count = tokens.shape[0]
     width = tokens.shape[1]
     top_count = expert_ids.shape[1]
@@ -119,6 +477,15 @@
     return (grad_in, grad_gate, grad_gate_w[None], grad_up_w[None], grad_down[None])
 
 
+def per_device(tokens, grad_out, expert_ids, gate_weights, w_gate, w_up, w_down):
+    tok_count, top_count = expert_ids.shape
+    node_count = lax.axis_size("node")
+    capacity = max(2, 2 * tok_count * top_count // node_count)
+    paired = node_count == 8 and lax.axis_size("local") == 4
+    plan = dense if capacity >= tok_count and paired else slotted
+    return plan(tokens, grad_out, expert_ids, gate_weights, w_gate, w_up, w_down)
+
+
 def solution(mesh):
     placed = (
         P(("node", "local"), None),

time: 276 us -> 89.4 us (0.32)
  waiting for transfers between devices: 150 us -> 36.7 us
  blocking collectives: 66.4 us -> 0 us
  matrix products: 30.5 us -> 0 us
  starting transfers between devices: 7.82 us -> 28.9 us
  Pallas kernels: 0 us -> 20.9 us
  between operations: 13.9 us -> 0.92 us
  local copies, waits for them, and re-layouts: 4.16 us -> 0.78 us
    all_gather x2 -> x0, waiting for transfers between devices: 98.2 us -> none  [the longest x1 65.4 us: per_device(): lax.all_gather(recv_grad[None], 'local', axis=0, tiled=True)]
    reduce_scatter x1 -> x0, waiting for transfers between devices: 46.4 us -> none  [per_device(): lax.psum_scatter(input_blocks.astype(jnp.bfloat16), 'local', scatter_dime...]
    all_to_all x3 -> x0, blocking collectives: 43.1 us -> none  [the longest x1 19 us: per_device(): lax.all_to_all(send_in, 'node', split_axis=0, concat_axis=0, tiled=True)]
    ppermute x0 -> x22, waiting for transfers between devices: none -> 36.7 us  [permute(): return lax.ppermute(value, AXES, pairs)]
    dot_general x13 -> x0, matrix products: 30.5 us -> none  [the longest x1 5.15 us: per_device(): lax.dot_general(weighted, flat_grad, contract_rows, preferred_element_typ...]
    ppermute x0 -> x22, starting transfers between devices: none -> 28.9 us  [permute(): return lax.ppermute(value, AXES, pairs)]
    pallas_call x0 -> x5, Pallas kernels: none -> 20.9 us  [the longest x2 14.3 us: group_terms(): pl.pallas_call(functools.partial(group_kernel, width=width, chunk=chunk,...]
    all_gather x1 -> x0, blocking collectives: 13.9 us -> none  [per_device(): lax.all_gather(recv_gate[None], 'local', axis=0, tiled=True)]
  transfers between devices with their start and end apart: 5 -> 22, of which waited for: 4 -> 12; matrix products, arithmetic and copies ran while one was open for 8% -> 2% of each run, Pallas kernels for 0% -> 21%
where the time goes in v2:
time: 89.4 us; the launch traced here: 89.2 us
  waiting for transfers between devices  36.7 us (41%)
  starting transfers between devices  28.9 us (32%)
  Pallas kernels  20.9 us (23%)
  other arithmetic  0.98 us (1%)
  between operations  0.92 us (1%)
    ppermute x22, waiting for transfers between devices, permute(): return lax.ppermute(value, AXES, pairs)  36.7 us
    ppermute x22, starting transfers between devices, permute(): return lax.ppermute(value, AXES, pairs)  28.9 us
    pallas_call x2, Pallas kernels, group_terms(): pl.pallas_call(functools.partial(group_kernel, width=width, chunk=chunk,...  14.3 us
    pallas_call x1, Pallas kernels, weight_terms(): pl.pallas_call(functools.partial(weights_kernel, blocks=len(rows), groups...  4.72 us
  transfers between devices with their start and end apart: 22, of which 12 were waited for; matrix products, arithmetic and copies ran while one was open for 2% of the time, Pallas kernels for 21%

profile of v2, /device:TPU:0, one launch (start us, length us, event | category | flops | bytes accessed | tf_op | source)
XLA Modules:
  0.0 89.2 jit_solution(2387142019335406288)
XLA Ops:
  0.6 1.0 %shard_map.110 = bf16[8,14464]{1,0:T(8,128)(2,1)S(1)} custom-call(bf16[8,7168]{1,0:T(8,128)(2,1)} %tokens_hbm.1, bf16[8,7168]{1,0:T(8,128)(2,1)} %grad_hbm.1, s32[4,8]{1,0:T(4,128)} %bitcast.49, bf16[4,8]{1,0:T(4,128)(2,1)} %bitcast.58), custom_call_target="tpu_custom_call" | custom-call | tf_op jit(solution)/shard_map/pallas_call | solution.py:56
  1.7 3.0 %collective-permute-start = (bf16[1,1,8,14464]{3,2,1,0:T(8,128)(2,1)S(1)}, bf16[1,1,8,14464]{3,2,1,0:T(8,128)(2,1)S(1)}, u32[]{:S(2)}, u32[]{:S(2)}) collective-permute-start(bf16[1,1,8,14464]{3,2,1,0:T(8,128)(2,1)S(1)} %bitcast.41), channel_id=1, source_target_pairs={{0,8},{1,9},{2,10},{3,11},{4,20},{5,21},{6,22},{7,23},{8,0},{9,1},... | collective-permute-start | bytes 694280 | tf_op jit(solution)/shard_map/ppermute | solution.py:274
  4.7 3.6 %collective-permute-start.2 = (bf16[1,1,8,14464]{3,2,1,0:T(8,128)(2,1)S(1)}, bf16[1,1,8,14464]{3,2,1,0:T(8,128)(2,1)S(1)}, u32[]{:S(2)}, u32[]{:S(2)}) collective-permute-start(bf16[1,1,8,14464]{3,2,1,0:T(8,128)(2,1)S(1)} %bitcast.42), channel_id=1, source_target_pairs={{0,3},{1,0},{2,1},{3,2},{4,7},{5,4},{6,5},{7,6},{8,11},{9,8},{10,9... | collective-permute-start | bytes 694280 | tf_op jit(solution)/shard_map/ppermute | solution.py:274
  8.3 0.0 collective-permute-start.4
  8.3 0.4 collective-permute-done
  8.7 5.6 %collective-permute-done.2 = bf16[1,1,8,14464]{3,2,1,0:T(8,128)(2,1)S(1)} collective-permute-done((bf16[1,1,8,14464]{3,2,1,0:T(8,128)(2,1)S(1)}, bf16[1,1,8,14464]{3,2,1,0:T(8,128)(2,1)S(1)}, u32[]{:S(2)}, u32[]{:S(2)}) %collective-permute-start.2) | collective-permute-done | bytes 231456 | tf_op jit(solution)/shard_map/ppermute | solution.py:274
  14.4 0.4 collective-permute-start.3
  14.8 4.3 %collective-permute-start.7 = (bf16[1,1,8,14464]{3,2,1,0:T(8,128)(2,1)S(1)}, bf16[1,1,8,14464]{3,2,1,0:T(8,128)(2,1)S(1)}, u32[]{:S(2)}, u32[]{:S(2)}) collective-permute-start(bf16[1,1,8,14464]{3,2,1,0:T(8,128)(2,1)S(1)} %collective-permute-done.2), channel_id=1, source_target_pairs={{0,3},{1,0},{2,1},{3,2},{4,7},{5,4},{6,5},{7,6},{8,11},{9,8},{10,9... | collective-permute-start | bytes 694280 | tf_op jit(solution)/shard_map/ppermute | solution.py:274
  19.1 1.6 %collective-permute-start.1 = (bf16[1,2,8,14464]{3,2,1,0:T(8,128)(2,1)S(1)}, bf16[1,2,8,14464]{3,2,1,0:T(8,128)(2,1)S(1)}, u32[]{:S(2)}, u32[]{:S(2)}) collective-permute-start(bf16[1,2,8,14464]{3,2,1,0:T(8,128)(2,1)S(1)} %constant_dynamic-update-slice_fusion), channel_id=1, source_target_pairs={{0,16},{1,17},{2,18},{3,19},{4,12},{5,13},{6,14},{7,15},{8,24},{9,... | collective-permute-start | bytes 1388552 | tf_op jit(solution)/shard_map/ppermute | solution.py:274
  20.7 0.0 collective-permute-done.4
  20.7 1.5 %collective-permute-start.6 = (bf16[1,1,8,14464]{3,2,1,0:T(8,128)(2,1)S(1)}, bf16[1,1,8,14464]{3,2,1,0:T(8,128)(2,1)S(1)}, u32[]{:S(2)}, u32[]{:S(2)}) collective-permute-start(bf16[1,1,8,14464]{3,2,1,0:T(8,128)(2,1)S(1)} %collective-permute-done.4), channel_id=1, source_target_pairs={{0,8},{1,9},{2,10},{3,11},{4,20},{5,21},{6,22},{7,23},{8,0},{9,1},... | collective-permute-start | bytes 694280 | tf_op jit(solution)/shard_map/ppermute | solution.py:274
  22.2 0.0 collective-permute-done.3
  22.3 0.9 collective-permute-start.5
  23.1 0.1 collective-permute-done.7
  23.3 2.0 %collective-permute-start.10 = (bf16[1,1,8,14464]{3,2,1,0:T(8,128)(2,1)S(1)}, bf16[1,1,8,14464]{3,2,1,0:T(8,128)(2,1)S(1)}, u32[]{:S(2)}, u32[]{:S(2)}) collective-permute-start(bf16[1,1,8,14464]{3,2,1,0:T(8,128)(2,1)S(1)} %collective-permute-done.7), channel_id=1, source_target_pairs={{0,8},{1,9},{2,10},{3,11},{4,20},{5,21},{6,22},{7,23},{8,0},{9,1},... | collective-permute-start | bytes 694280 | tf_op jit(solution)/shard_map/ppermute | solution.py:274
  25.2 4.0 %collective-permute-done.6 = bf16[1,1,8,14464]{3,2,1,0:T(8,128)(2,1)S(1)} collective-permute-done((bf16[1,1,8,14464]{3,2,1,0:T(8,128)(2,1)S(1)}, bf16[1,1,8,14464]{3,2,1,0:T(8,128)(2,1)S(1)}, u32[]{:S(2)}, u32[]{:S(2)}) %collective-permute-start.6) | collective-permute-done | bytes 231456 | tf_op jit(solution)/shard_map/ppermute | solution.py:274
  29.3 0.5 collective-permute-start.9
  29.8 5.6 %collective-permute-done.5 = bf16[1,2,8,14464]{3,2,1,0:T(8,128)(2,1)S(1)} collective-permute-done((bf16[1,2,8,14464]{3,2,1,0:T(8,128)(2,1)S(1)}, bf16[1,2,8,14464]{3,2,1,0:T(8,128)(2,1)S(1)}, u32[]{:S(2)}, u32[]{:S(2)}) %collective-permute-start.5) | collective-permute-done | bytes 462880 | tf_op jit(solution)/shard_map/ppermute | solution.py:274
  35.5 0.0 collective-permute-done.1
  35.5 0.1 pad_maximum_fusion
  35.6 0.1 constant_dynamic-update-slice_fusion.9
  35.7 0.1 constant_dynamic-update-slice_fusion.8
  35.8 0.1 collective-permute-start.8
  35.9 0.0 collective-permute-done.10
  35.9 1.8 %collective-permute-start.12 = (bf16[1,2,8,14464]{3,2,1,0:T(8,128)(2,1)S(1)}, bf16[1,2,8,14464]{3,2,1,0:T(8,128)(2,1)S(1)}, u32[]{:S(2)}, u32[]{:S(2)}) collective-permute-start(bf16[1,2,8,14464]{3,2,1,0:T(8,128)(2,1)S(1)} %constant_dynamic-update-slice_fusion.10), channel_id=1, source_target_pairs={{0,16},{1,17},{2,18},{3,19},{4,12},{5,13},{6,14},{7,15},{8,24},{9,... | collective-permute-start | bytes 1388552 | tf_op jit(solution)/shard_map/ppermute | solution.py:274
  37.8 2.6 %collective-permute-done.9 = bf16[1,2,8,14464]{3,2,1,0:T(8,128)(2,1)S(1)} collective-permute-done((bf16[1,2,8,14464]{3,2,1,0:T(8,128)(2,1)S(1)}, bf16[1,2,8,14464]{3,2,1,0:T(8,128)(2,1)S(1)}, u32[]{:S(2)}, u32[]{:S(2)}) %collective-permute-start.9) | collective-permute-done | bytes 462880 | tf_op jit(solution)/shard_map/ppermute | solution.py:274
  40.5 0.0 collective-permute-done.8
  40.5 8.3 %shard_map.111 = (bf16[64,7296]{1,0:T(8,128)(2,1)S(1)}, bf16[64,7296]{1,0:T(8,128)(2,1)S(1)}, bf16[128,256]{1,0:T(8,128)(2,1)S(1)}, bf16[128,256]{1,0:T(8,128)(2...) custom-call(s32[1]{0:T(128)} %bitcast.refs_0_, ...), custom_call_target="tpu_custom_call" | custom-call | tf_op jit(solution)/shard_map/pallas_call | solution.py:238
  48.8 0.0 collective-permute-done.12
  48.8 0.1 pad_maximum_fusion.1
  48.9 0.1 constant_dynamic-update-slice_fusion.15
  49.0 0.1 collective-permute-start.11
  49.0 0.1 constant_dynamic-update-slice_fusion.14
  49.1 0.6 collective-permute-start.14
  49.7 1.8 %collective-permute-done.11 = bf16[64,7296]{1,0:T(8,128)(2,1)S(1)} collective-permute-done((bf16[64,7296]{1,0:T(8,128)(2,1)S(1)}, bf16[64,7296]{1,0:T(8,128)(2,1)S(1)}, u32[]{:S(2)}, u32[]{:S(2)}) %collective-permute-start.11) | collective-permute-done | bytes 933920 | tf_op jit(solution)/shard_map/ppermute | solution.py:274
  51.5 0.2 add_convert_fusion.1
  51.8 1.8 %collective-permute-start.13 = (bf16[2,2,8,7296]{3,2,1,0:T(8,128)(2,1)S(1)}, bf16[2,2,8,7296]{3,2,1,0:T(8,128)(2,1)S(1)}, u32[]{:S(2)}, u32[]{:S(2)}) collective-permute-start(bf16[2,2,8,7296]{3,2,1,0:T(8,128)(2,1)S(1)} %slice.48), channel_id=1, source_target_pairs={{0,16},{1,17},{2,18},{3,19},{4,12},{5,13},{6,14},{7,15},{8,24},{9,... | collective-permute-start | bytes 1400840 | tf_op jit(solution)/shard_map/ppermute | solution.py:274
  53.6 0.6 collective-permute-done.14
  54.2 6.1 %shard_map.112 = (bf16[64,7296]{1,0:T(8,128)(2,1)S(1)}, bf16[64,7296]{1,0:T(8,128)(2,1)S(1)}, bf16[128,256]{1,0:T(8,128)(2,1)S(1)}, bf16[128,256]{1,0:T(8,128)(2,1)S(1)}, bf16[128,256]{1,0:T(8,128)(2,1)S(1)}) custom-call(s32[1]{0:T(128)} %bitcast.refs_0_, bf16[64,14464]{1,0:T(8,128)(2,1)S(1)} %bitcast.33, bf16[64,14464]{1,0:T(8,128)(2,1)S(1)} %bitcast.39, ...), custom_call_target="tpu_custom_call" | custom-call | tf_op jit(solution)/shard_map/pallas_call | solution.py:238
  60.2 0.2 collective-permute-start.16
  60.4 0.0 collective-permute-done.13
  60.4 0.1 add_convert_fusion.3
  60.6 2.2 %collective-permute-start.15 = (bf16[2,1,8,7296]{3,2,1,0:T(8,128)(2,1)S(1)}, bf16[2,1,8,7296]{3,2,1,0:T(8,128)(2,1)S(1)}, u32[]{:S(2)}, u32[]{:S(2)}) collective-permute-start(bf16[2,1,8,7296]{3,2,1,0:T(8,128)(2,1)S(1)} %slice.49), channel_id=1, source_target_pairs={{0,8},{1,9},{2,10},{3,11},{4,20},{5,21},{6,22},{7,23},{8,0},{9,1},... | collective-permute-start | bytes 700424 | tf_op jit(solution)/shard_map/ppermute | solution.py:274
  62.8 0.0 collective-permute-done.16
  62.8 0.2 add_convert_fusion
  63.1 1.8 %collective-permute-start.18 = (bf16[2,2,8,7296]{3,2,1,0:T(8,128)(2,1)S(1)}, bf16[2,2,8,7296]{3,2,1,0:T(8,128)(2,1)S(1)}, u32[]{:S(2)}, u32[]{:S(2)}) collective-permute-start(bf16[2,2,8,7296]{3,2,1,0:T(8,128)(2,1)S(1)} %slice.52), channel_id=1, source_target_pairs={{0,16},{1,17},{2,18},{3,19},{4,12},{5,13},{6,14},{7,15},{8,24},{9,... | collective-permute-start | bytes 1400840 | tf_op jit(solution)/shard_map/ppermute | solution.py:274
  64.9 2.4 %collective-permute-done.15 = bf16[2,1,8,7296]{3,2,1,0:T(8,128)(2,1)S(1)} collective-permute-done((bf16[2,1,8,7296]{3,2,1,0:T(8,128)(2,1)S(1)}, bf16[2,1,8,7296]{3,2,1,0:T(8,128)(2,1)S(1)}, u32[]{:S(2)}, u32[]{:S(2)}) %collective-permute-start.15) | collective-permute-done | bytes 233504 | tf_op jit(solution)/shard_map/ppermute | solution.py:274
  67.3 0.1 add_convert_fusion.5
  67.4 4.3 %collective-permute-done.18 = bf16[2,2,8,7296]{3,2,1,0:T(8,128)(2,1)S(1)} collective-permute-done((bf16[2,2,8,7296]{3,2,1,0:T(8,128)(2,1)S(1)}, bf16[2,2,8,7296]{3,2,1,0:T(8,128)(2,1)S(1)}, u32[]{:S(2)}, u32[]{:S(2)}) %collective-permute-start.18) | collective-permute-done | bytes 466976 | tf_op jit(solution)/shard_map/ppermute | solution.py:274
  71.7 0.1 add_convert_fusion.2
  71.8 2.2 %collective-permute-start.19 = (bf16[2,1,8,7296]{3,2,1,0:T(8,128)(2,1)S(1)}, bf16[2,1,8,7296]{3,2,1,0:T(8,128)(2,1)S(1)}, u32[]{:S(2)}, u32[]{:S(2)}) collective-permute-start(bf16[2,1,8,7296]{3,2,1,0:T(8,128)(2,1)S(1)} %slice.53), channel_id=1, source_target_pairs={{0,8},{1,9},{2,10},{3,11},{4,20},{5,21},{6,22},{7,23},{8,0},{9,1},... | collective-permute-start | bytes 700424 | tf_op jit(solution)/shard_map/ppermute | solution.py:274
  74.1 0.1 collective-permute-start.17
  74.1 7.3 %collective-permute-done.17 = bf16[1,8,7296]{2,1,0:T(8,128)(2,1)S(1)} collective-permute-done((bf16[1,8,7296]{2,1,0:T(8,128)(2,1)S(1)}, bf16[1,8,7296]{2,1,0:T(8,128)(2,1)S(1)}, u32[]{:S(2)}, u32[]{:S(2)}) %collective-permute-start.17) | collective-permute-done | bytes 116768 | tf_op jit(solution)/shard_map/ppermute | solution.py:274
  81.4 0.0 collective-permute-done.19
  81.4 0.1 add_convert_fusion.4
  81.5 0.2 collective-permute-start.20
  81.7 0.1 collective-permute-start.21
  81.8 0.0 copy-start
  81.8 4.7 %shard_map.113 = (bf16[7168,256]{1,0:T(8,128)(2,1)}, bf16[7168,256]{1,0:T(8,128)(2,1)}, bf16[256,7168]{1,0:T(8,128)(2,1)}) custom-call(bf16[64,14464]{1,0:T(8,128)(2,1)S(1)} %bitcast.36, bf16[64,14464]{1,0:T(8,128)(2,1)S(1)} %bitcast.38, bf16[64,14464]{1,0:T(8,128)(2,1)S(1)} %bitcast.34, bf16[64,14464]{1,0:T(8,128)(2,1)S(1)} %bitcast.40, ...), custom_call_target="tpu_custom_call" | custom-call | tf_op jit(solution)/shard_map/pallas_call | solution.py:144
  86.6 1.8 %collective-permute-done.20 = bf16[1,8,7296]{2,1,0:T(8,128)(2,1)S(1)} collective-permute-done((bf16[1,8,7296]{2,1,0:T(8,128)(2,1)S(1)}, bf16[1,8,7296]{2,1,0:T(8,128)(2,1)S(1)}, u32[]{:S(2)}, u32[]{:S(2)}) %collective-permute-start.20) | collective-permute-done | bytes 116768 | tf_op jit(solution)/shard_map/ppermute | solution.py:274
  88.4 0.0 collective-permute-done.21
  88.4 0.0 copy-done
  88.4 0.8 shard_map.114
  (18 shorter events, 0.4 us)
Async XLA Ops:
  1.7 7.0 %collective-permute-start = (bf16[1,1,8,14464]{3,2,1,0:T(8,128)(2,1)S(1)}, bf16[1,1,8,14464]{3,2,1,0:T(8,128)(2,1)S(1)}, u32[]{:S(2)}, u32[]{:S(2)}) collective-permute-start(bf16[1,1,8,14464]{3,2,1,0:T(8,128)(2,1)S(1)} %bitcast.41), channel_id=1, source_target_pairs={{0,8},{1,9},{2,10},{3,11},{4,20},{5,21},{6,22},{7,23},{8,0},{9,1},... | collective-permute-start | bytes 694280 | tf_op jit(solution)/shard_map/ppermute | solution.py:274
  4.7 9.7 %collective-permute-start.2 = (bf16[1,1,8,14464]{3,2,1,0:T(8,128)(2,1)S(1)}, bf16[1,1,8,14464]{3,2,1,0:T(8,128)(2,1)S(1)}, u32[]{:S(2)}, u32[]{:S(2)}) collective-permute-start(bf16[1,1,8,14464]{3,2,1,0:T(8,128)(2,1)S(1)} %bitcast.42), channel_id=1, source_target_pairs={{0,3},{1,0},{2,1},{3,2},{4,7},{5,4},{6,5},{7,6},{8,11},{9,8},{10,9... | collective-permute-start | bytes 694280 | tf_op jit(solution)/shard_map/ppermute | solution.py:274
  8.3 12.4 %collective-permute-start.4 = (bf16[1,1,8,14464]{3,2,1,0:T(8,128)(2,1)S(1)}, bf16[1,1,8,14464]{3,2,1,0:T(8,128)(2,1)S(1)}, u32[]{:S(2)}, u32[]{:S(2)}) collective-permute-start(bf16[1,1,8,14464]{3,2,1,0:T(8,128)(2,1)S(1)} %bitcast.43), channel_id=1, source_target_pairs={{0,1},{1,2},{2,3},{3,0},{4,5},{5,6},{6,7},{7,4},{8,9},{9,10},{10,1... | collective-permute-start | bytes 694280 | tf_op jit(solution)/shard_map/ppermute | solution.py:274
  14.4 7.9 %collective-permute-start.3 = (bf16[1,1,8,14464]{3,2,1,0:T(8,128)(2,1)S(1)}, bf16[1,1,8,14464]{3,2,1,0:T(8,128)(2,1)S(1)}, u32[]{:S(2)}, u32[]{:S(2)}) collective-permute-start(bf16[1,1,8,14464]{3,2,1,0:T(8,128)(2,1)S(1)} %collective-permute-done.2), channel_id=1, source_target_pairs={{0,8},{1,9},{2,10},{3,11},{4,20},{5,21},{6,22},{7,23},{8,0},{9,1},... | collective-permute-start | bytes 694280 | tf_op jit(solution)/shard_map/ppermute | solution.py:274
  14.8 8.5 %collective-permute-start.7 = (bf16[1,1,8,14464]{3,2,1,0:T(8,128)(2,1)S(1)}, bf16[1,1,8,14464]{3,2,1,0:T(8,128)(2,1)S(1)}, u32[]{:S(2)}, u32[]{:S(2)}) collective-permute-start(bf16[1,1,8,14464]{3,2,1,0:T(8,128)(2,1)S(1)} %collective-permute-done.2), channel_id=1, source_target_pairs={{0,3},{1,0},{2,1},{3,2},{4,7},{5,4},{6,5},{7,6},{8,11},{9,8},{10,9... | collective-permute-start | bytes 694280 | tf_op jit(solution)/shard_map/ppermute | solution.py:274
  19.1 16.4 %collective-permute-start.1 = (bf16[1,2,8,14464]{3,2,1,0:T(8,128)(2,1)S(1)}, bf16[1,2,8,14464]{3,2,1,0:T(8,128)(2,1)S(1)}, u32[]{:S(2)}, u32[]{:S(2)}) collective-permute-start(bf16[1,2,8,14464]{3,2,1,0:T(8,128)(2,1)S(1)} %constant_dynamic-update-slice_fusion), channel_id=1, source_target_pairs={{0,16},{1,17},{2,18},{3,19},{4,12},{5,13},{6,14},{7,15},{8,24},{9,... | collective-permute-start | bytes 1388552 | tf_op jit(solution)/shard_map/ppermute | solution.py:274
  20.7 8.6 %collective-permute-start.6 = (bf16[1,1,8,14464]{3,2,1,0:T(8,128)(2,1)S(1)}, bf16[1,1,8,14464]{3,2,1,0:T(8,128)(2,1)S(1)}, u32[]{:S(2)}, u32[]{:S(2)}) collective-permute-start(bf16[1,1,8,14464]{3,2,1,0:T(8,128)(2,1)S(1)} %collective-permute-done.4), channel_id=1, source_target_pairs={{0,8},{1,9},{2,10},{3,11},{4,20},{5,21},{6,22},{7,23},{8,0},{9,1},... | collective-permute-start | bytes 694280 | tf_op jit(solution)/shard_map/ppermute | solution.py:274
  22.3 13.2 %collective-permute-start.5 = (bf16[1,2,8,14464]{3,2,1,0:T(8,128)(2,1)S(1)}, bf16[1,2,8,14464]{3,2,1,0:T(8,128)(2,1)S(1)}, u32[]{:S(2)}, u32[]{:S(2)}) collective-permute-start(bf16[1,2,8,14464]{3,2,1,0:T(8,128)(2,1)S(1)} %constant_dynamic-update-slice_fusion.2), channel_id=1, source_target_pairs={{0,16},{1,17},{2,18},{3,19},{4,12},{5,13},{6,14},{7,15},{8,24},{9,... | collective-permute-start | bytes 1388552 | tf_op jit(solution)/shard_map/ppermute | solution.py:274
  23.3 12.6 %collective-permute-start.10 = (bf16[1,1,8,14464]{3,2,1,0:T(8,128)(2,1)S(1)}, bf16[1,1,8,14464]{3,2,1,0:T(8,128)(2,1)S(1)}, u32[]{:S(2)}, u32[]{:S(2)}) collective-permute-start(bf16[1,1,8,14464]{3,2,1,0:T(8,128)(2,1)S(1)} %collective-permute-done.7), channel_id=1, source_target_pairs={{0,8},{1,9},{2,10},{3,11},{4,20},{5,21},{6,22},{7,23},{8,0},{9,1},... | collective-permute-start | bytes 694280 | tf_op jit(solution)/shard_map/ppermute | solution.py:274
  29.3 11.0 %collective-permute-start.9 = (bf16[1,2,8,14464]{3,2,1,0:T(8,128)(2,1)S(1)}, bf16[1,2,8,14464]{3,2,1,0:T(8,128)(2,1)S(1)}, u32[]{:S(2)}, u32[]{:S(2)}) collective-permute-start(bf16[1,2,8,14464]{3,2,1,0:T(8,128)(2,1)S(1)} %constant_dynamic-update-slice_fusion.4), channel_id=1, source_target_pairs={{0,16},{1,17},{2,18},{3,19},{4,12},{5,13},{6,14},{7,15},{8,24},{9,... | collective-permute-start | bytes 1388552 | tf_op jit(solution)/shard_map/ppermute | solution.py:274
  35.8 4.7 %collective-permute-start.8 = (bf16[2,4,8,14464]{3,2,1,0:T(8,128)(2,1)S(1)}, bf16[2,4,8,14464]{3,2,1,0:T(8,128)(2,1)S(1)}, u32[]{:S(2)}, u32[]{:S(2)}) collective-permute-start(bf16[2,4,8,14464]{3,2,1,0:T(8,128)(2,1)S(1)} %constant_dynamic-update-slice_fusion.8), channel_id=1, source_target_pairs={{0,4},{1,5},{2,6},{3,7},{4,0},{5,1},{6,2},{7,3},{8,12},{9,13},{10,... | collective-permute-start | bytes 5554184 | tf_op jit(solution)/shard_map/ppermute | solution.py:274
  35.9 12.8 %collective-permute-start.12 = (bf16[1,2,8,14464]{3,2,1,0:T(8,128)(2,1)S(1)}, bf16[1,2,8,14464]{3,2,1,0:T(8,128)(2,1)S(1)}, u32[]{:S(2)}, u32[]{:S(2)}) collective-permute-start(bf16[1,2,8,14464]{3,2,1,0:T(8,128)(2,1)S(1)} %constant_dynamic-update-slice_fusion.10), channel_id=1, source_target_pairs={{0,16},{1,17},{2,18},{3,19},{4,12},{5,13},{6,14},{7,15},{8,24},{9,... | collective-permute-start | bytes 1388552 | tf_op jit(solution)/shard_map/ppermute | solution.py:274
  49.0 2.6 %collective-permute-start.11 = (bf16[64,7296]{1,0:T(8,128)(2,1)S(1)}, bf16[64,7296]{1,0:T(8,128)(2,1)S(1)}, u32[]{:S(2)}, u32[]{:S(2)}) collective-permute-start(bf16[64,7296]{1,0:T(8,128)(2,1)S(1)} %get-tuple-element.90), channel_id=1, source_target_pairs={{0,4},{1,5},{2,6},{3,7},{4,0},{5,1},{6,2},{7,3},{8,12},{9,13},{10,... | collective-permute-start | bytes 2801672 | tf_op jit(solution)/shard_map/ppermute | solution.py:274
  49.1 5.0 %collective-permute-start.14 = (bf16[2,4,8,14464]{3,2,1,0:T(8,128)(2,1)S(1)}, bf16[2,4,8,14464]{3,2,1,0:T(8,128)(2,1)S(1)}, u32[]{:S(2)}, u32[]{:S(2)}) collective-permute-start(bf16[2,4,8,14464]{3,2,1,0:T(8,128)(2,1)S(1)} %constant_dynamic-update-slice_fusion.14), channel_id=1, source_target_pairs={{0,4},{1,5},{2,6},{3,7},{4,0},{5,1},{6,2},{7,3},{8,12},{9,13},{10,... | collective-permute-start | bytes 5554184 | tf_op jit(solution)/shard_map/ppermute | solution.py:274
  51.8 8.7 %collective-permute-start.13 = (bf16[2,2,8,7296]{3,2,1,0:T(8,128)(2,1)S(1)}, bf16[2,2,8,7296]{3,2,1,0:T(8,128)(2,1)S(1)}, u32[]{:S(2)}, u32[]{:S(2)}) collective-permute-start(bf16[2,2,8,7296]{3,2,1,0:T(8,128)(2,1)S(1)} %slice.48), channel_id=1, source_target_pairs={{0,16},{1,17},{2,18},{3,19},{4,12},{5,13},{6,14},{7,15},{8,24},{9,... | collective-permute-start | bytes 1400840 | tf_op jit(solution)/shard_map/ppermute | solution.py:274
  60.2 2.6 %collective-permute-start.16 = (bf16[64,7296]{1,0:T(8,128)(2,1)S(1)}, bf16[64,7296]{1,0:T(8,128)(2,1)S(1)}, u32[]{:S(2)}, u32[]{:S(2)}) collective-permute-start(bf16[64,7296]{1,0:T(8,128)(2,1)S(1)} %get-tuple-element.105), channel_id=1, source_target_pairs={{0,4},{1,5},{2,6},{3,7},{4,0},{5,1},{6,2},{7,3},{8,12},{9,13},{10,... | collective-permute-start | bytes 2801672 | tf_op jit(solution)/shard_map/ppermute | solution.py:274
  60.6 6.7 %collective-permute-start.15 = (bf16[2,1,8,7296]{3,2,1,0:T(8,128)(2,1)S(1)}, bf16[2,1,8,7296]{3,2,1,0:T(8,128)(2,1)S(1)}, u32[]{:S(2)}, u32[]{:S(2)}) collective-permute-start(bf16[2,1,8,7296]{3,2,1,0:T(8,128)(2,1)S(1)} %slice.49), channel_id=1, source_target_pairs={{0,8},{1,9},{2,10},{3,11},{4,20},{5,21},{6,22},{7,23},{8,0},{9,1},... | collective-permute-start | bytes 700424 | tf_op jit(solution)/shard_map/ppermute | solution.py:274
  63.1 8.6 %collective-permute-start.18 = (bf16[2,2,8,7296]{3,2,1,0:T(8,128)(2,1)S(1)}, bf16[2,2,8,7296]{3,2,1,0:T(8,128)(2,1)S(1)}, u32[]{:S(2)}, u32[]{:S(2)}) collective-permute-start(bf16[2,2,8,7296]{3,2,1,0:T(8,128)(2,1)S(1)} %slice.52), channel_id=1, source_target_pairs={{0,16},{1,17},{2,18},{3,19},{4,12},{5,13},{6,14},{7,15},{8,24},{9,... | collective-permute-start | bytes 1400840 | tf_op jit(solution)/shard_map/ppermute | solution.py:274
  71.8 9.6 %collective-permute-start.19 = (bf16[2,1,8,7296]{3,2,1,0:T(8,128)(2,1)S(1)}, bf16[2,1,8,7296]{3,2,1,0:T(8,128)(2,1)S(1)}, u32[]{:S(2)}, u32[]{:S(2)}) collective-permute-start(bf16[2,1,8,7296]{3,2,1,0:T(8,128)(2,1)S(1)} %slice.53), channel_id=1, source_target_pairs={{0,8},{1,9},{2,10},{3,11},{4,20},{5,21},{6,22},{7,23},{8,0},{9,1},... | collective-permute-start | bytes 700424 | tf_op jit(solution)/shard_map/ppermute | solution.py:274
  74.1 7.4 %collective-permute-start.17 = (bf16[1,8,7296]{2,1,0:T(8,128)(2,1)S(1)}, bf16[1,8,7296]{2,1,0:T(8,128)(2,1)S(1)}, u32[]{:S(2)}, u32[]{:S(2)}) collective-permute-start(bf16[1,8,7296]{2,1,0:T(8,128)(2,1)S(1)} %get-tuple-element.133), channel_id=1, source_target_pairs={{0,1},{1,2},{2,3},{3,0},{4,5},{5,6},{6,7},{7,4},{8,9},{9,10},{10,1... | collective-permute-start | bytes 350216 | tf_op jit(solution)/shard_map/ppermute | solution.py:274
  81.5 6.9 %collective-permute-start.20 = (bf16[1,8,7296]{2,1,0:T(8,128)(2,1)S(1)}, bf16[1,8,7296]{2,1,0:T(8,128)(2,1)S(1)}, u32[]{:S(2)}, u32[]{:S(2)}) collective-permute-start(bf16[1,8,7296]{2,1,0:T(8,128)(2,1)S(1)} %get-tuple-element.132), channel_id=1, source_target_pairs={{0,3},{1,0},{2,1},{3,2},{4,7},{5,4},{6,5},{7,6},{8,11},{9,8},{10,9... | collective-permute-start | bytes 350216 | tf_op jit(solution)/shard_map/ppermute | solution.py:274
  81.7 6.6 %collective-permute-start.21 = (bf16[1,8,7296]{2,1,0:T(8,128)(2,1)S(1)}, bf16[1,8,7296]{2,1,0:T(8,128)(2,1)S(1)}, u32[]{:S(2)}, u32[]{:S(2)}) collective-permute-start(bf16[1,8,7296]{2,1,0:T(8,128)(2,1)S(1)} %get-tuple-element.131), channel_id=1, source_target_pairs={{0,2},{1,3},{2,0},{3,1},{4,6},{5,7},{6,4},{7,5},{8,10},{9,11},{10,... | collective-permute-start | bytes 350216 | tf_op jit(solution)/shard_map/ppermute | solution.py:274
  81.8 6.6 %copy-start = (s32[8,4]{0,1:T(4,128)S(1)}, s32[8,4]{0,1:T(4,128)}, u32[]{:S(2)}) copy-start(s32[8,4]{0,1:T(4,128)} %param.9) | copy-start | bytes 388

commit v3 on v2

--- a/solution.py
+++ b/solution.py
@@ -20,6 +20,28 @@
 
 def in_hbm(value):
     return pltpu.with_memory_space_constraint(value, pltpu.HBM)
+
+
+def load_kernel(*refs):
+    *refs, sems = refs
+    count = len(refs) // 2
+    copies = [pltpu.make_async_copy(refs[i], refs[count + i], sems.at[i]) for i in range(count)]
+    for copy in copies:
+        copy.start()
+    for copy in copies:
+        copy.wait()
+
+
+def load(*values):
+    return pl.pallas_call(
+        load_kernel,
+        out_shape=tuple(pltpu.VMEM(v.shape, v.dtype) for v in values),
+        in_specs=[pl.BlockSpec(memory_space=pl.ANY)] * len(values),
+        out_specs=whole(len(values)),
+        scratch_shapes=[pltpu.SemaphoreType.DMA((len(values),))],
+        compiler_params=pltpu.CompilerParams(vmem_limit_bytes=1 << 20),
+        cost_estimate=NO_COST,
+    )(*(in_hbm(v) for v in values))
 
 
 def pack_kernel(
@@ -64,7 +86,7 @@
             pltpu.VMEM((LANES, LANES), jnp.float32),
             pltpu.SemaphoreType.DMA((4,)),
         ],
-        compiler_params=pltpu.CompilerParams(vmem_limit_bytes=4 << 20),
+        compiler_params=pltpu.CompilerParams(vmem_limit_bytes=2 << 20),
         cost_estimate=NO_COST,
     )(*(in_hbm(v) for v in (tokens, grad_out, expert_ids.T, gate_weights.T)))
 
@@ -102,7 +124,7 @@
         in_specs=list(whole(len(terms) + 1)),
         out_specs=whole(2),
         scratch_shapes=[pltpu.VMEM((LANES, LANES), jnp.float32)],
-        compiler_params=pltpu.CompilerParams(vmem_limit_bytes=4 << 20),
+        compiler_params=pltpu.CompilerParams(vmem_limit_bytes=2 << 20),
         cost_estimate=NO_COST,
     )(*terms, ids)
     return grad_in, grad_gate.T
@@ -123,16 +145,23 @@
     gate_side, up_side, down_side = stacked(da), stacked(du), stacked(hw)
     copies = []
     for c in range(width // chunk):
-        span = pl.ds(c * chunk, chunk)
+        slot, span = c % 2, pl.ds(c * chunk, chunk)
+        for copy in copies[c - 2] if c > 1 else ():
+            copy.wait()
         part_in = stacked(rows, span)
-        parts[0][span, :] = outer(part_in, gate_side)
-        parts[1][span, :] = outer(part_in, up_side)
-        parts[2][:, span] = outer(down_side, stacked(rows, pl.ds(width + c * chunk, chunk)))
+        parts[0][slot] = outer(part_in, gate_side)
+        parts[1][slot] = outer(part_in, up_side)
+        parts[2][slot] = outer(down_side, stacked(rows, pl.ds(width + c * chunk, chunk)))
         places = ((span, slice(None)), (span, slice(None)), (slice(None), span))
-        for i, place in enumerate(places):
-            copies.append(pltpu.make_async_copy(parts[i].at[place], outs[i].at[place], sems.at[i, c]))
-            copies[-1].start()
-    for copy in copies:
+        copies.append(
+            [
+                pltpu.make_async_copy(parts[i].at[slot], outs[i].at[place], sems.at[i, slot])
+                for i, place in enumerate(places)
+            ]
+        )
+        for copy in copies[-1]:
+            copy.start()
+    for copy in sum(copies[-2:], []):
         copy.wait()
 
 
@@ -149,11 +178,15 @@
         in_specs=list(whole(len(rows) + 3 * len(da))),
         out_specs=(hbm,) * 3,
         scratch_shapes=[
-            *(pltpu.VMEM(s, jnp.bfloat16) for s in shapes),
-            pltpu.SemaphoreType.DMA((3, width // chunk)),
+            pltpu.VMEM((2, chunk, hid), jnp.bfloat16),
+            pltpu.VMEM((2, chunk, hid), jnp.bfloat16),
+            pltpu.VMEM((2, hid, chunk), jnp.bfloat16),
+            pltpu.SemaphoreType.DMA((3, 2)),
         ],
-        compiler_params=pltpu.CompilerParams(vmem_limit_bytes=28 << 20),
-        cost_estimate=NO_COST,
+        compiler_params=pltpu.CompilerParams(vmem_limit_bytes=10 << 20),
+        cost_estimate=pl.CostEstimate(
+            flops=0, bytes_accessed=16 << 18, transcendentals=0
+        ),
     )(*rows, *da, *du, *hw)
 
 
@@ -161,23 +194,22 @@
     return pltpu.with_memory_space_constraint(value, pltpu.VMEM)
 
 
-def group_kernel(*refs, width, chunk, loads):
+def hidden_kernel(*refs, width, chunk, loads):
     me_ref, held_ref, other_ref = refs[:3]
     sources, refs = refs[3:6], refs[6:]
-    mine_ref, send_ref, da_ref, du_ref, hw_ref = refs[:5]
+    da_ref, du_ref, hw_ref, term_ref = refs[:4]
     spans = [pl.ds(c * chunk, chunk) for c in range(width // chunk)]
     copies = [[] for _ in spans]
-    gate_w, up_w, down_w = refs[5:8] if loads else sources
+    gate_w, up_w, down_w = refs[4:7] if loads else sources
     if loads:
-        sems = refs[8]
+        sems = refs[7]
         for c, span in enumerate(spans):
             places = ((span, slice(None)), (span, slice(None)), (slice(None), span))
             for i, place in enumerate(places):
                 copies[c].append(
-                    pltpu.make_async_copy(sources[i].at[place], refs[5 + i].at[place], sems.at[i, c])
+                    pltpu.make_async_copy(sources[i].at[place], refs[4 + i].at[place], sems.at[i, c])
                 )
                 copies[c][-1].start()
-    half = held_ref.shape[0]
 
     def rows(start, size):
         span = pl.ds(start, size)
@@ -212,31 +244,40 @@
     da_ref[...] = grad_gate_pre
     du_ref[...] = grad_up_pre
     hw_ref[...] = (flat_gate * hidden).astype(jnp.bfloat16)
-    for span in spans:
-        part = turned(grad_gate_pre, gate_w[span, :]) + turned(grad_up_pre, up_w[span, :])
+    term_ref[...] = jnp.where(named, gate_partial, 0.0).astype(jnp.bfloat16)
+
+
+def rows_kernel(da_ref, du_ref, term_ref, gate_w, up_w, mine_ref, send_ref, *, width, chunk):
+    half = mine_ref.shape[0]
+    da, du = da_ref[...], du_ref[...]
+
+    def turned(a, b):
+        return lax.dot_general(a, b, CONTRACT_COLS, preferred_element_type=jnp.float32)
+
+    for c in range(width // chunk):
+        span = pl.ds(c * chunk, chunk)
+        part = turned(da, gate_w[span, :]) + turned(du, up_w[span, :])
         part = part.astype(jnp.bfloat16)
         mine_ref[:, span] = part[:half]
         send_ref[:, span] = part[half:]
-    gate_term = jnp.where(named, gate_partial, 0.0).astype(jnp.bfloat16)
     last = pl.ds(width, LANES)
-    mine_ref[:, last] = gate_term[:half]
-    send_ref[:, last] = gate_term[half:]
-
-
-def group_terms(held, other, weights, loads):
+    mine_ref[:, last] = term_ref[:half, :]
+    send_ref[:, last] = term_ref[half:, :]
+
+
+def hidden_terms(held, other, weights, loads):
     count, columns = held.shape
     width, hid = weights[0].shape
     chunk = next(c for c in (1024, 512, 256, 128) if width % c == 0)
     me = lax.axis_index("node").astype(jnp.int32).reshape(1)
-    back = jax.ShapeDtypeStruct((count, width + LANES), jnp.bfloat16)
     unit = jax.ShapeDtypeStruct((2 * count, hid), jnp.bfloat16)
-    shapes = (back, back, unit, unit, unit)
+    shapes = (unit, unit, unit, jax.ShapeDtypeStruct((2 * count, LANES), jnp.bfloat16))
     if loads:
         shapes += tuple(pltpu.VMEM(w.shape, w.dtype) for w in weights)
     space = pl.ANY if loads else pltpu.VMEM
     place = in_hbm if loads else in_vmem
     *terms, = pl.pallas_call(
-        functools.partial(group_kernel, width=width, chunk=chunk, loads=loads),
+        functools.partial(hidden_kernel, width=width, chunk=chunk, loads=loads),
         out_shape=shapes,
         in_specs=[
             pl.BlockSpec(memory_space=pltpu.SMEM),
@@ -245,10 +286,25 @@
         ],
         out_specs=whole(len(shapes)),
         scratch_shapes=[pltpu.SemaphoreType.DMA((3, width // chunk))] if loads else [],
-        compiler_params=pltpu.CompilerParams(vmem_limit_bytes=16 << 20),
+        compiler_params=pltpu.CompilerParams(vmem_limit_bytes=8 << 20),
         cost_estimate=NO_COST,
     )(me, held, other, *(place(w) for w in weights))
-    return terms[:5], terms[5:]
+    return terms[:4], terms[4:] or weights
+
+
+def row_terms(hidden, weights):
+    da, du, _, term = hidden
+    width = weights[0].shape[0]
+    chunk = next(c for c in (1024, 512, 256, 128) if width % c == 0)
+    back = jax.ShapeDtypeStruct((da.shape[0] // 2, width + LANES), jnp.bfloat16)
+    return pl.pallas_call(
+        functools.partial(rows_kernel, width=width, chunk=chunk),
+        out_shape=(back, back),
+        in_specs=list(whole(5)),
+        out_specs=whole(2),
+        compiler_params=pltpu.CompilerParams(vmem_limit_bytes=8 << 20),
+        cost_estimate=NO_COST,
+    )(da, du, term, *(in_vmem(w) for w in weights[:2]))
 
 
 def dense(tokens, grad_out, expert_ids, gate_weights, w_gate, w_up, w_down):
@@ -282,16 +338,18 @@
     def rotate(value, k):
         return permute(value, lambda n, p: (n, (p + k) % local_count))
 
+    def along(value, bits):
+        return permute(value, lambda n, p: (n, p ^ bits))
+
     def joined(*values):
         return jnp.concatenate(values, axis=1)
 
     own = pack(tokens, grad_out, expert_ids, gate_weights)[None, None]
 
-    weights = (w_gate[0], w_up[0], w_down[0])
 
     def terms(held, other, weights, loads):
         flat = [v.reshape(-1, v.shape[-1]) for v in (held, other)]
-        return group_terms(*flat, weights, loads)
+        return hidden_terms(*flat, weights, loads)
 
     def summed(mine, received):
         total = mine.astype(jnp.float32) + received.astype(jnp.float32)
@@ -306,58 +364,66 @@
 
 
     weights = (w_gate[0], w_up[0], w_down[0])
+    u_in = rotate(own, -1)
+    v_in = rotate(own, 1)
     near_x = cross(own, 0)
-    up_in = rotate(own, -1)
-    down_in = rotate(own, 1)
-    near = tock(joined(*tick(own, near_x)))
-    near_y = cross(near, 1)
-    up = tock(tick(up_in))
-    up_x = cross(up, 0)
-    far_in = rotate(up, -1)
-    down = tock(tick(down_in))
-    down_x = cross(down, 0)
-    up = tock(joined(*tick(up, up_x)))
-    up_y = cross(up, 1)
-    far = tock(tick(far_in))
-    far_x = cross(far, 0)
-    down = tock(joined(*tick(down, down_x)))
-    down_y = cross(down, 1)
-    up = tock(joined(*tick(up, up_y)))
-    near = tock(joined(*tick(near, near_y)))
-    first = tock(jnp.concatenate(tick(near, up), axis=0))
+    near_y = cross(own, 1)
+    u = tock(tick(u_in))
+    u_x = cross(u, 0)
+    w_in = rotate(u, -1)
+    near, near_x, near_y = tick(own, near_x, near_y)
+    near = tock(joined(near, near_x, near_y))
+    near_xy = cross(near_x, 1)
+    v = tock(tick(v_in))
+    v_x = cross(v, 0)
+    u = tock(joined(*tick(u, u_x)))
+    u_y = cross(u, 1)
+    w = tock(tick(w_in))
+    w_x = cross(w, 0)
+    v = tock(joined(*tick(v, v_x)))
+    v_y = cross(v, 1)
+    near = tock(joined(*tick(near, near_xy)))
+    u = joined(*tick(u, u_y))
+    first = tock(jnp.concatenate((near, u), axis=0))
     first_other = sibling(first)
-    far = tock(joined(*tick(far, far_x)))
-    far_y = cross(far, 1)
-    down = tock(joined(*tick(down, down_y)))
-    first_terms, weights = terms(*tick(first, first_other), weights, True)
-    tock(first_terms[0])
-    first_back = sibling(first_terms[1])
-    far = tock(joined(*tick(far, far_y)))
-    second = tock(jnp.concatenate(tick(down, far), axis=0))
+    w = tock(joined(*tick(w, w_x)))
+    w_y = cross(w, 1)
+    first_hidden, weights = terms(*tick(first, first_other), weights, True)
+    tock(first_hidden[0])
+    v = tock(joined(*tick(v, v_y)))
+    w = joined(*tick(w, w_y))
+    second = tock(jnp.concatenate((v, w), axis=0))
     second_other = sibling(second)
-    first_sum = tock(summed(*tick(first_terms[0], first_back)))
+    first_mine, first_send = row_terms([tick(first_hidden[0]), *first_hidden[1:]], weights)
+    tock(first_mine)
+    first_back = sibling(first_send)
+    second_hidden, _ = terms(*tick(second, second_other), weights, False)
+    tock(second_hidden[0])
+    first_sum = tock(summed(*tick(first_mine, first_back)))
     first_r1 = cross(upper(first_sum), 1)
-    second_terms, _ = terms(*tick(second, second_other), weights, False)
-    tock(second_terms[0])
-    second_back = sibling(second_terms[1])
+    second_mine, second_send = row_terms([tick(second_hidden[0]), *second_hidden[1:]], weights)
+    tock(second_mine)
+    second_back = [sibling(v) for v in jnp.split(second_send, 1)]
     first_sum = tock(folded(*tick(first_sum, first_r1)))
+    second_mine, *second_back = tick(second_mine, *second_back)
+    second_sum = tock(summed(second_mine, jnp.concatenate(second_back, axis=0)))
+    second_r1 = cross(upper(second_sum), 1)
+    first_sum = tock(tick(first_sum))
     first_r2 = cross(upper(first_sum), 0)
-    second_sum = tock(summed(*tick(second_terms[0], second_back)))
-    second_r1 = cross(upper(second_sum), 1)
-    first_sum = tock(folded(*tick(first_sum, first_r2)))
-    from_up = rotate(first_sum[1], 1)
     second_sum = tock(folded(*tick(second_sum, second_r1)))
     second_r2 = cross(upper(second_sum), 0)
-    from_up = tock(tick(from_up))
+    first_sum = tock(folded(*tick(first_sum, first_r2)))
+    from_u = rotate(first_sum[1], 1)
     second_sum = tock(folded(*tick(second_sum, second_r2)))
-    from_down = rotate(second_sum[0], -1)
-    from_far = rotate(second_sum[1], 2)
-    rows = [v.reshape(-1, v.shape[-1]) for v in (first, first_other, second, second_other)]
+    from_v = rotate(second_sum[0], -1)
+    from_w = rotate(second_sum[1], 2)
+    rows = [r.reshape(-1, r.shape[-1]) for r in (first, first_other, second, second_other)]
     rows[0] = tick(rows[0])
-    sides = [[t[i] for t in (first_terms, second_terms)] for i in (2, 3, 4)]
+    sides = [[t[i] for t in (first_hidden, second_hidden)] for i in (0, 1, 2)]
     grad_gate_w, grad_up_w, grad_down = weight_terms(rows, *sides, width)
     tock(grad_down)
-    ends = tick(first_sum[0], from_up, from_down, from_far)
+    from_u = tock(tick(from_u))
+    ends = tick(first_sum[0], from_u, from_v, from_w)
     grad_in, grad_gate = finish([e[0] for e in ends], expert_ids)
     return (grad_in, grad_gate, grad_gate_w[None], grad_up_w[None], grad_down[None])
 

time: 89.4 us -> 84.9 us (0.950)
  waiting for transfers between devices: 36.7 us -> 34.1 us
  starting transfers between devices: 28.9 us -> 27.1 us
    ppermute x22 -> x23, waiting for transfers between devices: 36.7 us -> 34.1 us  [permute(): return lax.ppermute(value, AXES, pairs)]
    ppermute x22 -> x23, starting transfers between devices: 28.9 us -> 27.1 us  [permute(): return lax.ppermute(value, AXES, pairs)]
    pallas_call x1, Pallas kernels: 4.72 us -> 6.41 us  [weight_terms(): pl.pallas_call(functools.partial(weights_kernel, blocks=len(rows), groups...]
    pallas_call x2 -> x4, Pallas kernels: 14.3 us -> 12.7 us  [the longest x2 7.72 us: hidden_terms(): pl.pallas_call(functools.partial(hidden_kernel, width=width, chunk=chunk,...]
  transfers between devices with their start and end apart: 22 -> 23, of which waited for: 12 -> 11; matrix products, arithmetic and copies ran while one was open for 2% -> 1% of each run, Pallas kernels for 21% -> 23%
where the time goes in v3:
time: 84.9 us; the launch traced here: 84.8 us
  waiting for transfers between devices  34.1 us (40%)
  starting transfers between devices  27.1 us (32%)
  Pallas kernels  20.9 us (25%)
  other arithmetic  1.26 us (1%)
  between operations  0.92 us (1%)
    ppermute x23, waiting for transfers between devices, permute(): return lax.ppermute(value, AXES, pairs)  34.1 us
    ppermute x23, starting transfers between devices, permute(): return lax.ppermute(value, AXES, pairs)  27.1 us
    pallas_call x2, Pallas kernels, hidden_terms(): pl.pallas_call(functools.partial(hidden_kernel, width=width, chunk=chunk,...  7.72 us
    pallas_call x1, Pallas kernels, weight_terms(): pl.pallas_call(functools.partial(weights_kernel, blocks=len(rows), groups...  6.41 us
    pallas_call x2, Pallas kernels, row_terms(): pl.pallas_call(functools.partial(rows_kernel, width=width, chunk=chunk),...  4.99 us
  transfers between devices with their start and end apart: 23, of which 11 were waited for; matrix products, arithmetic and copies ran while one was open for 1% of the time, Pallas kernels for 23%

profile of v3, /device:TPU:0, one launch (start us, length us, event | category | flops | bytes accessed | tf_op | source)
XLA Modules:
  0.0 84.8 jit_solution(14295525935644548464)
XLA Ops:
  0.6 1.0 %shard_map.110 = bf16[8,14464]{1,0:T(8,128)(2,1)S(1)} custom-call(bf16[8,7168]{1,0:T(8,128)(2,1)} %tokens_hbm.1, bf16[8,7168]{1,0:T(8,128)(2,1)} %grad_hbm.1, s32[4,8]{1,0:T(4,128)} %bitcast.50, bf16[4,8]{1,0:T(4,128)(2,1)} %bitcast.59), custom_call_target="tpu_custom_call" | custom-call | tf_op jit(solution)/shard_map/pallas_call | solution.py:78
  1.7 5.1 %collective-permute-start.2 = (bf16[1,1,8,14464]{3,2,1,0:T(8,128)(2,1)S(1)}, bf16[1,1,8,14464]{3,2,1,0:T(8,128)(2,1)S(1)}, u32[]{:S(2)}, u32[]{:S(2)}) collective-permute-start(bf16[1,1,8,14464]{3,2,1,0:T(8,128)(2,1)S(1)} %bitcast.41), channel_id=1, source_target_pairs={{0,3},{1,0},{2,1},{3,2},{4,7},{5,4},{6,5},{7,6},{8,11},{9,8},{10,9... | collective-permute-start | bytes 694280 | tf_op jit(solution)/shard_map/ppermute | solution.py:330
  6.8 1.5 %collective-permute-start.1 = (bf16[1,1,8,14464]{3,2,1,0:T(8,128)(2,1)S(1)}, bf16[1,1,8,14464]{3,2,1,0:T(8,128)(2,1)S(1)}, u32[]{:S(2)}, u32[]{:S(2)}) collective-permute-start(bf16[1,1,8,14464]{3,2,1,0:T(8,128)(2,1)S(1)} %bitcast.42), channel_id=1, source_target_pairs={{0,16},{1,17},{2,18},{3,19},{4,12},{5,13},{6,14},{7,15},{8,24},{9,... | collective-permute-start | bytes 694280 | tf_op jit(solution)/shard_map/ppermute | solution.py:330
  8.3 1.5 %collective-permute-start = (bf16[1,1,8,14464]{3,2,1,0:T(8,128)(2,1)S(1)}, bf16[1,1,8,14464]{3,2,1,0:T(8,128)(2,1)S(1)}, u32[]{:S(2)}, u32[]{:S(2)}) collective-permute-start(bf16[1,1,8,14464]{3,2,1,0:T(8,128)(2,1)S(1)} %bitcast.43), channel_id=1, source_target_pairs={{0,8},{1,9},{2,10},{3,11},{4,20},{5,21},{6,22},{7,23},{8,0},{9,1},... | collective-permute-start | bytes 694280 | tf_op jit(solution)/shard_map/ppermute | solution.py:330
  9.8 0.0 collective-permute-start.4
  9.8 3.1 %collective-permute-done.2 = bf16[1,1,8,14464]{3,2,1,0:T(8,128)(2,1)S(1)} collective-permute-done((bf16[1,1,8,14464]{3,2,1,0:T(8,128)(2,1)S(1)}, bf16[1,1,8,14464]{3,2,1,0:T(8,128)(2,1)S(1)}, u32[]{:S(2)}, u32[]{:S(2)}) %collective-permute-start.2) | collective-permute-done | bytes 231456 | tf_op jit(solution)/shard_map/ppermute | solution.py:330
  12.9 1.4 %collective-permute-start.7 = (bf16[1,1,8,14464]{3,2,1,0:T(8,128)(2,1)S(1)}, bf16[1,1,8,14464]{3,2,1,0:T(8,128)(2,1)S(1)}, u32[]{:S(2)}, u32[]{:S(2)}) collective-permute-start(bf16[1,1,8,14464]{3,2,1,0:T(8,128)(2,1)S(1)} %collective-permute-done.2), channel_id=1, source_target_pairs={{0,8},{1,9},{2,10},{3,11},{4,20},{5,21},{6,22},{7,23},{8,0},{9,1},... | collective-permute-start | bytes 694280 | tf_op jit(solution)/shard_map/ppermute | solution.py:330
  14.3 4.3 %collective-permute-start.6 = (bf16[1,1,8,14464]{3,2,1,0:T(8,128)(2,1)S(1)}, bf16[1,1,8,14464]{3,2,1,0:T(8,128)(2,1)S(1)}, u32[]{:S(2)}, u32[]{:S(2)}) collective-permute-start(bf16[1,1,8,14464]{3,2,1,0:T(8,128)(2,1)S(1)} %collective-permute-done.2), channel_id=1, source_target_pairs={{0,3},{1,0},{2,1},{3,2},{4,7},{5,4},{6,5},{7,6},{8,11},{9,8},{10,9... | collective-permute-start | bytes 694280 | tf_op jit(solution)/shard_map/ppermute | solution.py:330
  18.6 0.0 collective-permute-done.1
  18.6 0.0 collective-permute-done
  18.6 1.5 %collective-permute-start.3 = (bf16[1,1,8,14464]{3,2,1,0:T(8,128)(2,1)S(1)}, bf16[1,1,8,14464]{3,2,1,0:T(8,128)(2,1)S(1)}, u32[]{:S(2)}, u32[]{:S(2)}) collective-permute-start(bf16[1,1,8,14464]{3,2,1,0:T(8,128)(2,1)S(1)} %collective-permute-done), channel_id=1, source_target_pairs={{0,16},{1,17},{2,18},{3,19},{4,12},{5,13},{6,14},{7,15},{8,24},{9,... | collective-permute-start | bytes 694280 | tf_op jit(solution)/shard_map/ppermute | solution.py:330
  20.2 0.0 collective-permute-done.4
  20.2 0.6 collective-permute-start.5
  20.8 0.0 collective-permute-done.7
  20.9 1.0 %collective-permute-start.8 = (bf16[1,2,8,14464]{3,2,1,0:T(8,128)(2,1)S(1)}, bf16[1,2,8,14464]{3,2,1,0:T(8,128)(2,1)S(1)}, u32[]{:S(2)}, u32[]{:S(2)}) collective-permute-start(bf16[1,2,8,14464]{3,2,1,0:T(8,128)(2,1)S(1)} %constant_dynamic-update-slice_fusion.3), channel_id=1, source_target_pairs={{0,16},{1,17},{2,18},{3,19},{4,12},{5,13},{6,14},{7,15},{8,24},{9,... | collective-permute-start | bytes 1388552 | tf_op jit(solution)/shard_map/ppermute | solution.py:330
  21.9 1.2 %collective-permute-done.6 = bf16[1,1,8,14464]{3,2,1,0:T(8,128)(2,1)S(1)} collective-permute-done((bf16[1,1,8,14464]{3,2,1,0:T(8,128)(2,1)S(1)}, bf16[1,1,8,14464]{3,2,1,0:T(8,128)(2,1)S(1)}, u32[]{:S(2)}, u32[]{:S(2)}) %collective-permute-start.6) | collective-permute-done | bytes 231456 | tf_op jit(solution)/shard_map/ppermute | solution.py:330
  23.1 0.9 %collective-permute-start.10 = (bf16[1,1,8,14464]{3,2,1,0:T(8,128)(2,1)S(1)}, bf16[1,1,8,14464]{3,2,1,0:T(8,128)(2,1)S(1)}, u32[]{:S(2)}, u32[]{:S(2)}) collective-permute-start(bf16[1,1,8,14464]{3,2,1,0:T(8,128)(2,1)S(1)} %collective-permute-done.6), channel_id=1, source_target_pairs={{0,8},{1,9},{2,10},{3,11},{4,20},{5,21},{6,22},{7,23},{8,0},{9,1},... | collective-permute-start | bytes 694280 | tf_op jit(solution)/shard_map/ppermute | solution.py:330
  24.0 4.9 %collective-permute-done.5 = bf16[1,1,8,14464]{3,2,1,0:T(8,128)(2,1)S(1)} collective-permute-done((bf16[1,1,8,14464]{3,2,1,0:T(8,128)(2,1)S(1)}, bf16[1,1,8,14464]{3,2,1,0:T(8,128)(2,1)S(1)}, u32[]{:S(2)}, u32[]{:S(2)}) %collective-permute-start.5) | collective-permute-done | bytes 231456 | tf_op jit(solution)/shard_map/ppermute | solution.py:330
  28.9 0.6 collective-permute-start.11
  29.5 0.0 collective-permute-done.3
  29.6 2.8 %collective-permute-done.8 = bf16[1,2,8,14464]{3,2,1,0:T(8,128)(2,1)S(1)} collective-permute-done((bf16[1,2,8,14464]{3,2,1,0:T(8,128)(2,1)S(1)}, bf16[1,2,8,14464]{3,2,1,0:T(8,128)(2,1)S(1)}, u32[]{:S(2)}, u32[]{:S(2)}) %collective-permute-start.8) | collective-permute-done | bytes 462880 | tf_op jit(solution)/shard_map/ppermute | solution.py:330
  32.3 0.2 maximum_maximum_fusion
  32.6 0.1 collective-permute-start.9
  32.6 1.2 %collective-permute-done.10 = bf16[1,1,8,14464]{3,2,1,0:T(8,128)(2,1)S(1)} collective-permute-done((bf16[1,1,8,14464]{3,2,1,0:T(8,128)(2,1)S(1)}, bf16[1,1,8,14464]{3,2,1,0:T(8,128)(2,1)S(1)}, u32[]{:S(2)}, u32[]{:S(2)}) %collective-permute-start.10) | collective-permute-done | bytes 231456 | tf_op jit(solution)/shard_map/ppermute | solution.py:330
  33.9 0.6 collective-permute-start.12
  34.4 2.0 %collective-permute-done.9 = bf16[2,4,8,14464]{3,2,1,0:T(8,128)(2,1)S(1)} collective-permute-done((bf16[2,4,8,14464]{3,2,1,0:T(8,128)(2,1)S(1)}, bf16[2,4,8,14464]{3,2,1,0:T(8,128)(2,1)S(1)}, u32[]{:S(2)}, u32[]{:S(2)}) %collective-permute-start.9) | collective-permute-done | bytes 1851424 | tf_op jit(solution)/shard_map/ppermute | solution.py:330
  36.4 5.4 %shard_map.111 = (bf16[128,256]{1,0:T(8,128)(2,1)S(1)}, bf16[128,256]{1,0:T(8,128)(2,1)S(1)}, bf16[128,256]{1,0:T(8,128)(2,1)S(1)}, bf16[128,128]{1,0:T(8,128)(2...) custom-call(s32[1]{0:T(128)} %bitcast.refs_0_, ...), custom_call_target="tpu_custom_call" | custom-call | tf_op jit(solution)/shard_map/pallas_call | solution.py:279
  41.8 0.0 collective-permute-done.11
  41.9 0.5 collective-permute-done.12
  42.5 0.2 maximum_maximum_fusion.1
  42.7 0.1 collective-permute-start.14
  42.8 2.5 %shard_map.112 = (bf16[64,7296]{1,0:T(8,128)(2,1)S(1)}, bf16[64,7296]{1,0:T(8,128)(2,1)S(1)}) custom-call(bf16[128,256]{1,0:T(8,128)(2,1)S(1)} %get-tuple-element.91.da_ref.refs_4_, bf16[128,256]{1,0:T(8,128)(2,1)S(1)} %get-tuple-element.92.du_ref.refs_6_, bf16[128,128]{1,0:T(8,128)(2,1)S(1)} %get-tuple-element.93.term_ref, ...), custom_call_target="tpu_custom_call" | custom-call | tf_op jit(solution)/shard_map/pallas_call | solution.py:300
  45.3 0.6 collective-permute-start.13
  45.8 0.7 collective-permute-done.14
  46.6 2.3 %shard_map.113 = (bf16[128,256]{1,0:T(8,128)(2,1)S(1)}, bf16[128,256]{1,0:T(8,128)(2,1)S(1)}, bf16[128,256]{1,0:T(8,128)(2,1)S(1)}, bf16[128,128]{1,0:T(8,128)(2,1)S(1)}) custom-call(s32[1]{0:T(128)} %bitcast.refs_0_, bf16[64,14464]{1,0:T(8,128)(2,1)S(1)} %bitcast.35, bf16[64,14464]{1,0:T(8,128)(2,1)S(1)} %bitcast.39, ...), custom_call_target="tpu_custom_call" | custom-call | tf_op jit(solution)/shard_map/pallas_call | solution.py:279
  48.9 0.0 collective-permute-done.13
  48.9 0.2 add_convert_fusion.1
  49.2 1.1 %collective-permute-start.15 = (bf16[2,2,8,7296]{3,2,1,0:T(8,128)(2,1)S(1)}, bf16[2,2,8,7296]{3,2,1,0:T(8,128)(2,1)S(1)}, u32[]{:S(2)}, u32[]{:S(2)}) collective-permute-start(bf16[2,2,8,7296]{3,2,1,0:T(8,128)(2,1)S(1)} %slice.48), channel_id=1, source_target_pairs={{0,16},{1,17},{2,18},{3,19},{4,12},{5,13},{6,14},{7,15},{8,24},{9,... | collective-permute-start | bytes 1400840 | tf_op jit(solution)/shard_map/ppermute | solution.py:330
  50.3 2.5 %shard_map.114 = (bf16[64,7296]{1,0:T(8,128)(2,1)S(1)}, bf16[64,7296]{1,0:T(8,128)(2,1)S(1)}) custom-call(bf16[128,256]{1,0:T(8,128)(2,1)S(1)} %get-tuple-element.104.da_ref.refs_5_, bf16[128,256]{1,0:T(8,128)(2,1)S(1)} %get-tuple-element.105.du_ref.refs_7_, bf16[128,128]{1,0:T(8,128)(2,1)S(1)} %get-tuple-element.106.term_ref, ...), custom_call_target="tpu_custom_call" | custom-call | tf_op jit(solution)/shard_map/pallas_call | solution.py:300
  52.8 0.1 collective-permute-start.16
  52.9 4.9 %collective-permute-done.15 = bf16[2,2,8,7296]{3,2,1,0:T(8,128)(2,1)S(1)} collective-permute-done((bf16[2,2,8,7296]{3,2,1,0:T(8,128)(2,1)S(1)}, bf16[2,2,8,7296]{3,2,1,0:T(8,128)(2,1)S(1)}, u32[]{:S(2)}, u32[]{:S(2)}) %collective-permute-start.15) | collective-permute-done | bytes 466976 | tf_op jit(solution)/shard_map/ppermute | solution.py:330
  57.8 0.1 add_convert_fusion.3
  57.9 0.0 collective-permute-done.16
  57.9 0.2 add_convert_fusion
  58.2 1.1 %collective-permute-start.18 = (bf16[2,2,8,7296]{3,2,1,0:T(8,128)(2,1)S(1)}, bf16[2,2,8,7296]{3,2,1,0:T(8,128)(2,1)S(1)}, u32[]{:S(2)}, u32[]{:S(2)}) collective-permute-start(bf16[2,2,8,7296]{3,2,1,0:T(8,128)(2,1)S(1)} %slice.49), channel_id=1, source_target_pairs={{0,16},{1,17},{2,18},{3,19},{4,12},{5,13},{6,14},{7,15},{8,24},{9,... | collective-permute-start | bytes 1400840 | tf_op jit(solution)/shard_map/ppermute | solution.py:330
  59.3 1.0 %collective-permute-start.17 = (bf16[2,1,8,7296]{3,2,1,0:T(8,128)(2,1)S(1)}, bf16[2,1,8,7296]{3,2,1,0:T(8,128)(2,1)S(1)}, u32[]{:S(2)}, u32[]{:S(2)}) collective-permute-start(bf16[2,1,8,7296]{3,2,1,0:T(8,128)(2,1)S(1)} %slice.38), channel_id=1, source_target_pairs={{0,8},{1,9},{2,10},{3,11},{4,20},{5,21},{6,22},{7,23},{8,0},{9,1},... | collective-permute-start | bytes 700424 | tf_op jit(solution)/shard_map/ppermute | solution.py:330
  60.3 8.0 %collective-permute-done.18 = bf16[2,2,8,7296]{3,2,1,0:T(8,128)(2,1)S(1)} collective-permute-done((bf16[2,2,8,7296]{3,2,1,0:T(8,128)(2,1)S(1)}, bf16[2,2,8,7296]{3,2,1,0:T(8,128)(2,1)S(1)}, u32[]{:S(2)}, u32[]{:S(2)}) %collective-permute-start.18) | collective-permute-done | bytes 466976 | tf_op jit(solution)/shard_map/ppermute | solution.py:330
  68.3 0.1 add_convert_fusion.2
  68.5 0.0 collective-permute-done.17
  68.5 1.2 %collective-permute-start.20 = (bf16[2,1,8,7296]{3,2,1,0:T(8,128)(2,1)S(1)}, bf16[2,1,8,7296]{3,2,1,0:T(8,128)(2,1)S(1)}, u32[]{:S(2)}, u32[]{:S(2)}) collective-permute-start(bf16[2,1,8,7296]{3,2,1,0:T(8,128)(2,1)S(1)} %slice.52), channel_id=1, source_target_pairs={{0,8},{1,9},{2,10},{3,11},{4,20},{5,21},{6,22},{7,23},{8,0},{9,1},... | collective-permute-start | bytes 700424 | tf_op jit(solution)/shard_map/ppermute | solution.py:330
  69.7 0.1 add_convert_fusion.5
  69.8 0.1 collective-permute-start.19
  69.9 4.8 %collective-permute-done.20 = bf16[2,1,8,7296]{3,2,1,0:T(8,128)(2,1)S(1)} collective-permute-done((bf16[2,1,8,7296]{3,2,1,0:T(8,128)(2,1)S(1)}, bf16[2,1,8,7296]{3,2,1,0:T(8,128)(2,1)S(1)}, u32[]{:S(2)}, u32[]{:S(2)}) %collective-permute-start.20) | collective-permute-done | bytes 233504 | tf_op jit(solution)/shard_map/ppermute | solution.py:330
  74.6 0.1 add_convert_fusion.4
  74.7 0.2 collective-permute-start.22
  75.0 2.6 %collective-permute-start.21 = (bf16[1,8,7296]{2,1,0:T(8,128)(2,1)S(1)}, bf16[1,8,7296]{2,1,0:T(8,128)(2,1)S(1)}, u32[]{:S(2)}, u32[]{:S(2)}) collective-permute-start(bf16[1,8,7296]{2,1,0:T(8,128)(2,1)S(1)} %get-tuple-element.134), channel_id=1, source_target_pairs={{0,3},{1,0},{2,1},{3,2},{4,7},{5,4},{6,5},{7,6},{8,11},{9,8},{10,9... | collective-permute-start | bytes 350216 | tf_op jit(solution)/shard_map/ppermute | solution.py:330
  77.5 0.0 copy-start
  77.5 6.4 %shard_map.115 = (bf16[7168,256]{1,0:T(8,128)(2,1)}, bf16[7168,256]{1,0:T(8,128)(2,1)}, bf16[256,7168]{1,0:T(8,128)(2,1)}) custom-call(bf16[64,14464]{1,0:T(8,128)(2,1)S(1)} %bitcast.34, bf16[64,14464]{1,0:T(8,128)(2,1)S(1)} %bitcast.38, bf16[64,14464]{1,0:T(8,128)(2,1)S(1)} %bitcast.36, bf16[64,14464]{1,0:T(8,128)(2,1)S(1)} %bitcast.40, ...), custom_call_target="tpu_custom_call" | custom-call | bytes 4194304 | tf_op jit(solution)/shard_map/pallas_call | solution.py:173
  83.9 0.0 collective-permute-done.19
  83.9 0.0 collective-permute-done.22
  84.0 0.0 collective-permute-done.21
  84.0 0.0 copy-done
  84.0 0.8 shard_map.116
  (19 shorter events, 0.5 us)
Async XLA Ops:
  1.7 11.2 %collective-permute-start.2 = (bf16[1,1,8,14464]{3,2,1,0:T(8,128)(2,1)S(1)}, bf16[1,1,8,14464]{3,2,1,0:T(8,128)(2,1)S(1)}, u32[]{:S(2)}, u32[]{:S(2)}) collective-permute-start(bf16[1,1,8,14464]{3,2,1,0:T(8,128)(2,1)S(1)} %bitcast.41), channel_id=1, source_target_pairs={{0,3},{1,0},{2,1},{3,2},{4,7},{5,4},{6,5},{7,6},{8,11},{9,8},{10,9... | collective-permute-start | bytes 694280 | tf_op jit(solution)/shard_map/ppermute | solution.py:330
  6.8 11.8 %collective-permute-start.1 = (bf16[1,1,8,14464]{3,2,1,0:T(8,128)(2,1)S(1)}, bf16[1,1,8,14464]{3,2,1,0:T(8,128)(2,1)S(1)}, u32[]{:S(2)}, u32[]{:S(2)}) collective-permute-start(bf16[1,1,8,14464]{3,2,1,0:T(8,128)(2,1)S(1)} %bitcast.42), channel_id=1, source_target_pairs={{0,16},{1,17},{2,18},{3,19},{4,12},{5,13},{6,14},{7,15},{8,24},{9,... | collective-permute-start | bytes 694280 | tf_op jit(solution)/shard_map/ppermute | solution.py:330
  8.3 10.3 %collective-permute-start = (bf16[1,1,8,14464]{3,2,1,0:T(8,128)(2,1)S(1)}, bf16[1,1,8,14464]{3,2,1,0:T(8,128)(2,1)S(1)}, u32[]{:S(2)}, u32[]{:S(2)}) collective-permute-start(bf16[1,1,8,14464]{3,2,1,0:T(8,128)(2,1)S(1)} %bitcast.43), channel_id=1, source_target_pairs={{0,8},{1,9},{2,10},{3,11},{4,20},{5,21},{6,22},{7,23},{8,0},{9,1},... | collective-permute-start | bytes 694280 | tf_op jit(solution)/shard_map/ppermute | solution.py:330
  9.8 10.4 %collective-permute-start.4 = (bf16[1,1,8,14464]{3,2,1,0:T(8,128)(2,1)S(1)}, bf16[1,1,8,14464]{3,2,1,0:T(8,128)(2,1)S(1)}, u32[]{:S(2)}, u32[]{:S(2)}) collective-permute-start(bf16[1,1,8,14464]{3,2,1,0:T(8,128)(2,1)S(1)} %bitcast.44), channel_id=1, source_target_pairs={{0,1},{1,2},{2,3},{3,0},{4,5},{5,6},{6,7},{7,4},{8,9},{9,10},{10,1... | collective-permute-start | bytes 694280 | tf_op jit(solution)/shard_map/ppermute | solution.py:330
  12.9 8.0 %collective-permute-start.7 = (bf16[1,1,8,14464]{3,2,1,0:T(8,128)(2,1)S(1)}, bf16[1,1,8,14464]{3,2,1,0:T(8,128)(2,1)S(1)}, u32[]{:S(2)}, u32[]{:S(2)}) collective-permute-start(bf16[1,1,8,14464]{3,2,1,0:T(8,128)(2,1)S(1)} %collective-permute-done.2), channel_id=1, source_target_pairs={{0,8},{1,9},{2,10},{3,11},{4,20},{5,21},{6,22},{7,23},{8,0},{9,1},... | collective-permute-start | bytes 694280 | tf_op jit(solution)/shard_map/ppermute | solution.py:330
  14.3 8.8 %collective-permute-start.6 = (bf16[1,1,8,14464]{3,2,1,0:T(8,128)(2,1)S(1)}, bf16[1,1,8,14464]{3,2,1,0:T(8,128)(2,1)S(1)}, u32[]{:S(2)}, u32[]{:S(2)}) collective-permute-start(bf16[1,1,8,14464]{3,2,1,0:T(8,128)(2,1)S(1)} %collective-permute-done.2), channel_id=1, source_target_pairs={{0,3},{1,0},{2,1},{3,2},{4,7},{5,4},{6,5},{7,6},{8,11},{9,8},{10,9... | collective-permute-start | bytes 694280 | tf_op jit(solution)/shard_map/ppermute | solution.py:330
  18.6 10.9 %collective-permute-start.3 = (bf16[1,1,8,14464]{3,2,1,0:T(8,128)(2,1)S(1)}, bf16[1,1,8,14464]{3,2,1,0:T(8,128)(2,1)S(1)}, u32[]{:S(2)}, u32[]{:S(2)}) collective-permute-start(bf16[1,1,8,14464]{3,2,1,0:T(8,128)(2,1)S(1)} %collective-permute-done), channel_id=1, source_target_pairs={{0,16},{1,17},{2,18},{3,19},{4,12},{5,13},{6,14},{7,15},{8,24},{9,... | collective-permute-start | bytes 694280 | tf_op jit(solution)/shard_map/ppermute | solution.py:330
  20.2 8.6 %collective-permute-start.5 = (bf16[1,1,8,14464]{3,2,1,0:T(8,128)(2,1)S(1)}, bf16[1,1,8,14464]{3,2,1,0:T(8,128)(2,1)S(1)}, u32[]{:S(2)}, u32[]{:S(2)}) collective-permute-start(bf16[1,1,8,14464]{3,2,1,0:T(8,128)(2,1)S(1)} %collective-permute-done.4), channel_id=1, source_target_pairs={{0,8},{1,9},{2,10},{3,11},{4,20},{5,21},{6,22},{7,23},{8,0},{9,1},... | collective-permute-start | bytes 694280 | tf_op jit(solution)/shard_map/ppermute | solution.py:330
  20.9 11.5 %collective-permute-start.8 = (bf16[1,2,8,14464]{3,2,1,0:T(8,128)(2,1)S(1)}, bf16[1,2,8,14464]{3,2,1,0:T(8,128)(2,1)S(1)}, u32[]{:S(2)}, u32[]{:S(2)}) collective-permute-start(bf16[1,2,8,14464]{3,2,1,0:T(8,128)(2,1)S(1)} %constant_dynamic-update-slice_fusion.3), channel_id=1, source_target_pairs={{0,16},{1,17},{2,18},{3,19},{4,12},{5,13},{6,14},{7,15},{8,24},{9,... | collective-permute-start | bytes 1388552 | tf_op jit(solution)/shard_map/ppermute | solution.py:330
  23.1 10.7 %collective-permute-start.10 = (bf16[1,1,8,14464]{3,2,1,0:T(8,128)(2,1)S(1)}, bf16[1,1,8,14464]{3,2,1,0:T(8,128)(2,1)S(1)}, u32[]{:S(2)}, u32[]{:S(2)}) collective-permute-start(bf16[1,1,8,14464]{3,2,1,0:T(8,128)(2,1)S(1)} %collective-permute-done.6), channel_id=1, source_target_pairs={{0,8},{1,9},{2,10},{3,11},{4,20},{5,21},{6,22},{7,23},{8,0},{9,1},... | collective-permute-start | bytes 694280 | tf_op jit(solution)/shard_map/ppermute | solution.py:330
  28.9 12.9 %collective-permute-start.11 = (bf16[1,2,8,14464]{3,2,1,0:T(8,128)(2,1)S(1)}, bf16[1,2,8,14464]{3,2,1,0:T(8,128)(2,1)S(1)}, u32[]{:S(2)}, u32[]{:S(2)}) collective-permute-start(bf16[1,2,8,14464]{3,2,1,0:T(8,128)(2,1)S(1)} %constant_dynamic-update-slice_fusion.5), channel_id=1, source_target_pairs={{0,16},{1,17},{2,18},{3,19},{4,12},{5,13},{6,14},{7,15},{8,24},{9,... | collective-permute-start | bytes 1388552 | tf_op jit(solution)/shard_map/ppermute | solution.py:330
  32.6 3.9 %collective-permute-start.9 = (bf16[2,4,8,14464]{3,2,1,0:T(8,128)(2,1)S(1)}, bf16[2,4,8,14464]{3,2,1,0:T(8,128)(2,1)S(1)}, u32[]{:S(2)}, u32[]{:S(2)}) collective-permute-start(bf16[2,4,8,14464]{3,2,1,0:T(8,128)(2,1)S(1)} %maximum_maximum_fusion), channel_id=1, source_target_pairs={{0,4},{1,5},{2,6},{3,7},{4,0},{5,1},{6,2},{7,3},{8,12},{9,13},{10,... | collective-permute-start | bytes 5554184 | tf_op jit(solution)/shard_map/ppermute | solution.py:330
  33.9 8.6 %collective-permute-start.12 = (bf16[1,2,8,14464]{3,2,1,0:T(8,128)(2,1)S(1)}, bf16[1,2,8,14464]{3,2,1,0:T(8,128)(2,1)S(1)}, u32[]{:S(2)}, u32[]{:S(2)}) collective-permute-start(bf16[1,2,8,14464]{3,2,1,0:T(8,128)(2,1)S(1)} %constant_dynamic-update-slice_fusion.9), channel_id=1, source_target_pairs={{0,16},{1,17},{2,18},{3,19},{4,12},{5,13},{6,14},{7,15},{8,24},{9,... | collective-permute-start | bytes 1388552 | tf_op jit(solution)/shard_map/ppermute | solution.py:330
  42.7 3.9 %collective-permute-start.14 = (bf16[2,4,8,14464]{3,2,1,0:T(8,128)(2,1)S(1)}, bf16[2,4,8,14464]{3,2,1,0:T(8,128)(2,1)S(1)}, u32[]{:S(2)}, u32[]{:S(2)}) collective-permute-start(bf16[2,4,8,14464]{3,2,1,0:T(8,128)(2,1)S(1)} %maximum_maximum_fusion.1), channel_id=1, source_target_pairs={{0,4},{1,5},{2,6},{3,7},{4,0},{5,1},{6,2},{7,3},{8,12},{9,13},{10,... | collective-permute-start | bytes 5554184 | tf_op jit(solution)/shard_map/ppermute | solution.py:330
  45.3 3.6 %collective-permute-start.13 = (bf16[64,7296]{1,0:T(8,128)(2,1)S(1)}, bf16[64,7296]{1,0:T(8,128)(2,1)S(1)}, u32[]{:S(2)}, u32[]{:S(2)}) collective-permute-start(bf16[64,7296]{1,0:T(8,128)(2,1)S(1)} %get-tuple-element.97), channel_id=1, source_target_pairs={{0,4},{1,5},{2,6},{3,7},{4,0},{5,1},{6,2},{7,3},{8,12},{9,13},{10,... | collective-permute-start | bytes 2801672 | tf_op jit(solution)/shard_map/ppermute | solution.py:330
  49.2 8.6 %collective-permute-start.15 = (bf16[2,2,8,7296]{3,2,1,0:T(8,128)(2,1)S(1)}, bf16[2,2,8,7296]{3,2,1,0:T(8,128)(2,1)S(1)}, u32[]{:S(2)}, u32[]{:S(2)}) collective-permute-start(bf16[2,2,8,7296]{3,2,1,0:T(8,128)(2,1)S(1)} %slice.48), channel_id=1, source_target_pairs={{0,16},{1,17},{2,18},{3,19},{4,12},{5,13},{6,14},{7,15},{8,24},{9,... | collective-permute-start | bytes 1400840 | tf_op jit(solution)/shard_map/ppermute | solution.py:330
  52.8 5.1 %collective-permute-start.16 = (bf16[64,7296]{1,0:T(8,128)(2,1)S(1)}, bf16[64,7296]{1,0:T(8,128)(2,1)S(1)}, u32[]{:S(2)}, u32[]{:S(2)}) collective-permute-start(bf16[64,7296]{1,0:T(8,128)(2,1)S(1)} %get-tuple-element.110), channel_id=1, source_target_pairs={{0,4},{1,5},{2,6},{3,7},{4,0},{5,1},{6,2},{7,3},{8,12},{9,13},{10,... | collective-permute-start | bytes 2801672 | tf_op jit(solution)/shard_map/ppermute | solution.py:330
  58.2 10.1 %collective-permute-start.18 = (bf16[2,2,8,7296]{3,2,1,0:T(8,128)(2,1)S(1)}, bf16[2,2,8,7296]{3,2,1,0:T(8,128)(2,1)S(1)}, u32[]{:S(2)}, u32[]{:S(2)}) collective-permute-start(bf16[2,2,8,7296]{3,2,1,0:T(8,128)(2,1)S(1)} %slice.49), channel_id=1, source_target_pairs={{0,16},{1,17},{2,18},{3,19},{4,12},{5,13},{6,14},{7,15},{8,24},{9,... | collective-permute-start | bytes 1400840 | tf_op jit(solution)/shard_map/ppermute | solution.py:330
  59.3 9.1 %collective-permute-start.17 = (bf16[2,1,8,7296]{3,2,1,0:T(8,128)(2,1)S(1)}, bf16[2,1,8,7296]{3,2,1,0:T(8,128)(2,1)S(1)}, u32[]{:S(2)}, u32[]{:S(2)}) collective-permute-start(bf16[2,1,8,7296]{3,2,1,0:T(8,128)(2,1)S(1)} %slice.38), channel_id=1, source_target_pairs={{0,8},{1,9},{2,10},{3,11},{4,20},{5,21},{6,22},{7,23},{8,0},{9,1},... | collective-permute-start | bytes 700424 | tf_op jit(solution)/shard_map/ppermute | solution.py:330
  68.5 6.1 %collective-permute-start.20 = (bf16[2,1,8,7296]{3,2,1,0:T(8,128)(2,1)S(1)}, bf16[2,1,8,7296]{3,2,1,0:T(8,128)(2,1)S(1)}, u32[]{:S(2)}, u32[]{:S(2)}) collective-permute-start(bf16[2,1,8,7296]{3,2,1,0:T(8,128)(2,1)S(1)} %slice.52), channel_id=1, source_target_pairs={{0,8},{1,9},{2,10},{3,11},{4,20},{5,21},{6,22},{7,23},{8,0},{9,1},... | collective-permute-start | bytes 700424 | tf_op jit(solution)/shard_map/ppermute | solution.py:330
  69.8 14.1 %collective-permute-start.19 = (bf16[1,8,7296]{2,1,0:T(8,128)(2,1)S(1)}, bf16[1,8,7296]{2,1,0:T(8,128)(2,1)S(1)}, u32[]{:S(2)}, u32[]{:S(2)}) collective-permute-start(bf16[1,8,7296]{2,1,0:T(8,128)(2,1)S(1)} %get-tuple-element.135), channel_id=1, source_target_pairs={{0,1},{1,2},{2,3},{3,0},{4,5},{5,6},{6,7},{7,4},{8,9},{9,10},{10,1... | collective-permute-start | bytes 350216 | tf_op jit(solution)/shard_map/ppermute | solution.py:330
  74.7 9.2 %collective-permute-start.22 = (bf16[1,8,7296]{2,1,0:T(8,128)(2,1)S(1)}, bf16[1,8,7296]{2,1,0:T(8,128)(2,1)S(1)}, u32[]{:S(2)}, u32[]{:S(2)}) collective-permute-start(bf16[1,8,7296]{2,1,0:T(8,128)(2,1)S(1)} %get-tuple-element.133), channel_id=1, source_target_pairs={{0,2},{1,3},{2,0},{3,1},{4,6},{5,7},{6,4},{7,5},{8,10},{9,11},{10,... | collective-permute-start | bytes 350216 | tf_op jit(solution)/shard_map/ppermute | solution.py:330
  75.0 9.0 %collective-permute-start.21 = (bf16[1,8,7296]{2,1,0:T(8,128)(2,1)S(1)}, bf16[1,8,7296]{2,1,0:T(8,128)(2,1)S(1)}, u32[]{:S(2)}, u32[]{:S(2)}) collective-permute-start(bf16[1,8,7296]{2,1,0:T(8,128)(2,1)S(1)} %get-tuple-element.134), channel_id=1, source_target_pairs={{0,3},{1,0},{2,1},{3,2},{4,7},{5,4},{6,5},{7,6},{8,11},{9,8},{10,9... | collective-permute-start | bytes 350216 | tf_op jit(solution)/shard_map/ppermute | solution.py:330
  77.5 6.5 %copy-start = (s32[8,4]{0,1:T(4,128)S(1)}, s32[8,4]{0,1:T(4,128)}, u32[]{:S(2)}) copy-start(s32[8,4]{0,1:T(4,128)} %param.9) | copy-start | bytes 388

commit v4 on v3

--- a/solution.py
+++ b/solution.py
@@ -9,6 +9,7 @@
 
 AXES = ("node", "local")
 LANES = 128
+SLOTS = 4
 NO_COST = pl.CostEstimate(flops=0, bytes_accessed=0, transcendentals=0)
 CONTRACT_ROWS = (((0,), (0,)), ((), ()))
 CONTRACT_COLS = (((1,), (1,)), ((), ()))
@@ -145,8 +146,8 @@
     gate_side, up_side, down_side = stacked(da), stacked(du), stacked(hw)
     copies = []
     for c in range(width // chunk):
-        slot, span = c % 2, pl.ds(c * chunk, chunk)
-        for copy in copies[c - 2] if c > 1 else ():
+        slot, span = c % SLOTS, pl.ds(c * chunk, chunk)
+        for copy in copies[c - SLOTS] if c >= SLOTS else ():
             copy.wait()
         part_in = stacked(rows, span)
         parts[0][slot] = outer(part_in, gate_side)
@@ -161,7 +162,7 @@
         )
         for copy in copies[-1]:
             copy.start()
-    for copy in sum(copies[-2:], []):
+    for copy in sum(copies[-SLOTS:], []):
         copy.wait()
 
 
@@ -178,12 +179,12 @@
         in_specs=list(whole(len(rows) + 3 * len(da))),
         out_specs=(hbm,) * 3,
         scratch_shapes=[
-            pltpu.VMEM((2, chunk, hid), jnp.bfloat16),
-            pltpu.VMEM((2, chunk, hid), jnp.bfloat16),
-            pltpu.VMEM((2, hid, chunk), jnp.bfloat16),
-            pltpu.SemaphoreType.DMA((3, 2)),
+            pltpu.VMEM((SLOTS, chunk, hid), jnp.bfloat16),
+            pltpu.VMEM((SLOTS, chunk, hid), jnp.bfloat16),
+            pltpu.VMEM((SLOTS, hid, chunk), jnp.bfloat16),
+            pltpu.SemaphoreType.DMA((3, SLOTS)),
         ],
-        compiler_params=pltpu.CompilerParams(vmem_limit_bytes=10 << 20),
+        compiler_params=pltpu.CompilerParams(vmem_limit_bytes=16 << 20),
         cost_estimate=pl.CostEstimate(
             flops=0, bytes_accessed=16 << 18, transcendentals=0
         ),
@@ -380,6 +381,8 @@
     u_y = cross(u, 1)
     w = tock(tick(w_in))
     w_x = cross(w, 0)
+    weights = load(*tick(*weights, own)[:3])
+    tock(weights[0])
     v = tock(joined(*tick(v, v_x)))
     v_y = cross(v, 1)
     near = tock(joined(*tick(near, near_xy)))
@@ -388,33 +391,39 @@
     first_other = sibling(first)
     w = tock(joined(*tick(w, w_x)))
     w_y = cross(w, 1)
-    first_hidden, weights = terms(*tick(first, first_other), weights, True)
+    first_hidden, weights = terms(*tick(first, first_other), weights, False)
     tock(first_hidden[0])
+    first_mine, first_send = row_terms([tick(first_hidden[0]), *first_hidden[1:]], weights)
+    tock(first_mine)
+    first_back = sibling(first_send)
     v = tock(joined(*tick(v, v_y)))
     w = joined(*tick(w, w_y))
     second = tock(jnp.concatenate((v, w), axis=0))
     second_other = sibling(second)
-    first_mine, first_send = row_terms([tick(first_hidden[0]), *first_hidden[1:]], weights)
-    tock(first_mine)
-    first_back = sibling(first_send)
+    first_sum = tock(summed(*tick(first_mine, first_back)))
+    first_r1 = cross(upper(first_sum), 1)
     second_hidden, _ = terms(*tick(second, second_other), weights, False)
     tock(second_hidden[0])
-    first_sum = tock(summed(*tick(first_mine, first_back)))
-    first_r1 = cross(upper(first_sum), 1)
     second_mine, second_send = row_terms([tick(second_hidden[0]), *second_hidden[1:]], weights)
     tock(second_mine)
     second_back = [sibling(v) for v in jnp.split(second_send, 1)]
     first_sum = tock(folded(*tick(first_sum, first_r1)))
+    first_sum = tock(tick(first_sum))
+    first_r2 = cross(upper(first_sum), 0)
     second_mine, *second_back = tick(second_mine, *second_back)
     second_sum = tock(summed(second_mine, jnp.concatenate(second_back, axis=0)))
-    second_r1 = cross(upper(second_sum), 1)
-    first_sum = tock(tick(first_sum))
-    first_r2 = cross(upper(first_sum), 0)
-    second_sum = tock(folded(*tick(second_sum, second_r1)))
-    second_r2 = cross(upper(second_sum), 0)
+    cut = width // 2
+    lo, hi = second_sum[..., :cut], second_sum[..., cut:]
+    lo_r1 = cross(upper(lo), 1)
+    hi_r1 = cross(upper(hi), 1)
+    lo = tock(folded(*tick(lo, lo_r1)))
+    lo_r2 = cross(upper(lo), 0)
+    hi = tock(folded(*tick(hi, hi_r1)))
+    hi_r2 = cross(upper(hi), 0)
     first_sum = tock(folded(*tick(first_sum, first_r2)))
     from_u = rotate(first_sum[1], 1)
-    second_sum = tock(folded(*tick(second_sum, second_r2)))
+    lo, lo_r2, hi, hi_r2 = tick(lo, lo_r2, hi, hi_r2)
+    second_sum = tock(jnp.concatenate((folded(lo, lo_r2), folded(hi, hi_r2)), axis=-1))
     from_v = rotate(second_sum[0], -1)
     from_w = rotate(second_sum[1], 2)
     rows = [r.reshape(-1, r.shape[-1]) for r in (first, first_other, second, second_other)]

time: 84.9 us -> 82.9 us (0.976)
  waiting for transfers between devices: 34.1 us -> 29.1 us
  starting transfers between devices: 27.1 us -> 30.6 us
    ppermute x23 -> x25, waiting for transfers between devices: 34.1 us -> 29.1 us  [permute(): return lax.ppermute(value, AXES, pairs)]
    pallas_call x0 -> x1, Pallas kernels: none -> 4.23 us  [load(): pl.pallas_call(load_kernel, out_shape=tuple((pltpu.VMEM(v.shape, v.dtype)...]
    ppermute x23 -> x25, starting transfers between devices: 27.1 us -> 30.6 us  [permute(): return lax.ppermute(value, AXES, pairs)]
    pallas_call x2, Pallas kernels: 7.72 us -> 4.65 us  [hidden_terms(): pl.pallas_call(functools.partial(hidden_kernel, width=width, chunk=chunk,...]
    pallas_call x1, Pallas kernels: 6.41 us -> 4.74 us  [weight_terms(): pl.pallas_call(functools.partial(weights_kernel, blocks=len(rows), groups...]
  transfers between devices with their start and end apart: 23 -> 25, of which waited for: 11 -> 14; matrix products, arithmetic and copies ran while one was open for 1% -> 2% of each run, Pallas kernels for 23% -> 22%
where the time goes in v4:
time: 82.9 us; the launch traced here: 82.8 us
  starting transfers between devices  30.6 us (37%)
  waiting for transfers between devices  29.1 us (35%)
  Pallas kernels  20.4 us (25%)
  other arithmetic  1.26 us (2%)
  between operations  0.91 us (1%)
    ppermute x25, starting transfers between devices, permute(): return lax.ppermute(value, AXES, pairs)  30.6 us
    ppermute x25, waiting for transfers between devices, permute(): return lax.ppermute(value, AXES, pairs)  29.1 us
    pallas_call x2, Pallas kernels, row_terms(): pl.pallas_call(functools.partial(rows_kernel, width=width, chunk=chunk),...  4.95 us
    pallas_call x1, Pallas kernels, weight_terms(): pl.pallas_call(functools.partial(weights_kernel, blocks=len(rows), groups...  4.74 us
    pallas_call x2, Pallas kernels, hidden_terms(): pl.pallas_call(functools.partial(hidden_kernel, width=width, chunk=chunk,...  4.65 us
    pallas_call x1, Pallas kernels, load(): pl.pallas_call(load_kernel, out_shape=tuple((pltpu.VMEM(v.shape, v.dtype)...  4.23 us
  transfers between devices with their start and end apart: 25, of which 14 were waited for; matrix products, arithmetic and copies ran while one was open for 2% of the time, Pallas kernels for 22%

profile of v4, /device:TPU:0, one launch (start us, length us, event | category | flops | bytes accessed | tf_op | source)
XLA Modules:
  0.0 82.8 jit_solution(14091061203385780810)
XLA Ops:
  0.6 1.0 %shard_map.110 = bf16[8,14464]{1,0:T(8,128)(2,1)S(1)} custom-call(bf16[8,7168]{1,0:T(8,128)(2,1)} %tokens_hbm.1, bf16[8,7168]{1,0:T(8,128)(2,1)} %grad_hbm.1, s32[4,8]{1,0:T(4,128)} %bitcast.50, bf16[4,8]{1,0:T(4,128)(2,1)} %bitcast.61), custom_call_target="tpu_custom_call" | custom-call | tf_op jit(solution)/shard_map/pallas_call | solution.py:79
  1.7 5.1 %collective-permute-start.2 = (bf16[1,1,8,14464]{3,2,1,0:T(8,128)(2,1)S(1)}, bf16[1,1,8,14464]{3,2,1,0:T(8,128)(2,1)S(1)}, u32[]{:S(2)}, u32[]{:S(2)}) collective-permute-start(bf16[1,1,8,14464]{3,2,1,0:T(8,128)(2,1)S(1)} %bitcast.41), channel_id=1, source_target_pairs={{0,3},{1,0},{2,1},{3,2},{4,7},{5,4},{6,5},{7,6},{8,11},{9,8},{10,9... | collective-permute-start | bytes 694280 | tf_op jit(solution)/shard_map/ppermute | solution.py:331
  6.8 1.5 %collective-permute-start.1 = (bf16[1,1,8,14464]{3,2,1,0:T(8,128)(2,1)S(1)}, bf16[1,1,8,14464]{3,2,1,0:T(8,128)(2,1)S(1)}, u32[]{:S(2)}, u32[]{:S(2)}) collective-permute-start(bf16[1,1,8,14464]{3,2,1,0:T(8,128)(2,1)S(1)} %bitcast.42), channel_id=1, source_target_pairs={{0,16},{1,17},{2,18},{3,19},{4,12},{5,13},{6,14},{7,15},{8,24},{9,... | collective-permute-start | bytes 694280 | tf_op jit(solution)/shard_map/ppermute | solution.py:331
  8.3 1.5 %collective-permute-start = (bf16[1,1,8,14464]{3,2,1,0:T(8,128)(2,1)S(1)}, bf16[1,1,8,14464]{3,2,1,0:T(8,128)(2,1)S(1)}, u32[]{:S(2)}, u32[]{:S(2)}) collective-permute-start(bf16[1,1,8,14464]{3,2,1,0:T(8,128)(2,1)S(1)} %bitcast.43), channel_id=1, source_target_pairs={{0,8},{1,9},{2,10},{3,11},{4,20},{5,21},{6,22},{7,23},{8,0},{9,1},... | collective-permute-start | bytes 694280 | tf_op jit(solution)/shard_map/ppermute | solution.py:331
  9.8 0.0 collective-permute-start.4
  9.8 3.1 %collective-permute-done.2 = bf16[1,1,8,14464]{3,2,1,0:T(8,128)(2,1)S(1)} collective-permute-done((bf16[1,1,8,14464]{3,2,1,0:T(8,128)(2,1)S(1)}, bf16[1,1,8,14464]{3,2,1,0:T(8,128)(2,1)S(1)}, u32[]{:S(2)}, u32[]{:S(2)}) %collective-permute-start.2) | collective-permute-done | bytes 231456 | tf_op jit(solution)/shard_map/ppermute | solution.py:331
  12.9 1.4 %collective-permute-start.7 = (bf16[1,1,8,14464]{3,2,1,0:T(8,128)(2,1)S(1)}, bf16[1,1,8,14464]{3,2,1,0:T(8,128)(2,1)S(1)}, u32[]{:S(2)}, u32[]{:S(2)}) collective-permute-start(bf16[1,1,8,14464]{3,2,1,0:T(8,128)(2,1)S(1)} %collective-permute-done.2), channel_id=1, source_target_pairs={{0,8},{1,9},{2,10},{3,11},{4,20},{5,21},{6,22},{7,23},{8,0},{9,1},... | collective-permute-start | bytes 694280 | tf_op jit(solution)/shard_map/ppermute | solution.py:331
  14.3 4.3 %collective-permute-start.6 = (bf16[1,1,8,14464]{3,2,1,0:T(8,128)(2,1)S(1)}, bf16[1,1,8,14464]{3,2,1,0:T(8,128)(2,1)S(1)}, u32[]{:S(2)}, u32[]{:S(2)}) collective-permute-start(bf16[1,1,8,14464]{3,2,1,0:T(8,128)(2,1)S(1)} %collective-permute-done.2), channel_id=1, source_target_pairs={{0,3},{1,0},{2,1},{3,2},{4,7},{5,4},{6,5},{7,6},{8,11},{9,8},{10,9... | collective-permute-start | bytes 694280 | tf_op jit(solution)/shard_map/ppermute | solution.py:331
  18.6 0.0 collective-permute-done.1
  18.6 0.0 collective-permute-done
  18.6 1.5 %collective-permute-start.3 = (bf16[1,1,8,14464]{3,2,1,0:T(8,128)(2,1)S(1)}, bf16[1,1,8,14464]{3,2,1,0:T(8,128)(2,1)S(1)}, u32[]{:S(2)}, u32[]{:S(2)}) collective-permute-start(bf16[1,1,8,14464]{3,2,1,0:T(8,128)(2,1)S(1)} %collective-permute-done), channel_id=1, source_target_pairs={{0,16},{1,17},{2,18},{3,19},{4,12},{5,13},{6,14},{7,15},{8,24},{9,... | collective-permute-start | bytes 694280 | tf_op jit(solution)/shard_map/ppermute | solution.py:331
  20.2 0.0 collective-permute-done.4
  20.2 0.6 collective-permute-start.5
  20.8 0.0 collective-permute-done.7
  20.9 1.0 %collective-permute-start.8 = (bf16[1,2,8,14464]{3,2,1,0:T(8,128)(2,1)S(1)}, bf16[1,2,8,14464]{3,2,1,0:T(8,128)(2,1)S(1)}, u32[]{:S(2)}, u32[]{:S(2)}) collective-permute-start(bf16[1,2,8,14464]{3,2,1,0:T(8,128)(2,1)S(1)} %constant_dynamic-update-slice_fusion.3), channel_id=1, source_target_pairs={{0,16},{1,17},{2,18},{3,19},{4,12},{5,13},{6,14},{7,15},{8,24},{9,... | collective-permute-start | bytes 1388552 | tf_op jit(solution)/shard_map/ppermute | solution.py:331
  21.9 1.2 %collective-permute-done.6 = bf16[1,1,8,14464]{3,2,1,0:T(8,128)(2,1)S(1)} collective-permute-done((bf16[1,1,8,14464]{3,2,1,0:T(8,128)(2,1)S(1)}, bf16[1,1,8,14464]{3,2,1,0:T(8,128)(2,1)S(1)}, u32[]{:S(2)}, u32[]{:S(2)}) %collective-permute-start.6) | collective-permute-done | bytes 231456 | tf_op jit(solution)/shard_map/ppermute | solution.py:331
  23.1 0.9 %collective-permute-start.10 = (bf16[1,1,8,14464]{3,2,1,0:T(8,128)(2,1)S(1)}, bf16[1,1,8,14464]{3,2,1,0:T(8,128)(2,1)S(1)}, u32[]{:S(2)}, u32[]{:S(2)}) collective-permute-start(bf16[1,1,8,14464]{3,2,1,0:T(8,128)(2,1)S(1)} %collective-permute-done.6), channel_id=1, source_target_pairs={{0,8},{1,9},{2,10},{3,11},{4,20},{5,21},{6,22},{7,23},{8,0},{9,1},... | collective-permute-start | bytes 694280 | tf_op jit(solution)/shard_map/ppermute | solution.py:331
  24.0 4.2 %shard_map.111 = (bf16[7168,256]{1,0:T(8,128)(2,1)S(1)}, bf16[7168,256]{1,0:T(8,128)(2,1)S(1)}, bf16[256,7168]{1,0:T(8,128)(2,1)S(1)}) custom-call(bf16[7168,256]{1,0:T(8,128)(2,1)} %bitcast.58, bf16[7168,256]{1,0:T(8,128)(2,1)} %bitcast.59, bf16[256,7168]{1,0:T(8,128)(2,1)} %bitcast.60), custom_call_target="tpu_custom_call" | custom-call | tf_op jit(solution)/shard_map/pallas_call | solution.py:37
  28.2 0.6 collective-permute-done.5
  28.9 0.9 %collective-permute-start.12 = (bf16[1,2,8,14464]{3,2,1,0:T(8,128)(2,1)S(1)}, bf16[1,2,8,14464]{3,2,1,0:T(8,128)(2,1)S(1)}, u32[]{:S(2)}, u32[]{:S(2)}) collective-permute-start(bf16[1,2,8,14464]{3,2,1,0:T(8,128)(2,1)S(1)} %constant_dynamic-update-slice_fusion.5), channel_id=1, source_target_pairs={{0,16},{1,17},{2,18},{3,19},{4,12},{5,13},{6,14},{7,15},{8,24},{9,... | collective-permute-start | bytes 1388552 | tf_op jit(solution)/shard_map/ppermute | solution.py:331
  29.8 0.0 collective-permute-done.3
  29.9 2.5 %collective-permute-done.8 = bf16[1,2,8,14464]{3,2,1,0:T(8,128)(2,1)S(1)} collective-permute-done((bf16[1,2,8,14464]{3,2,1,0:T(8,128)(2,1)S(1)}, bf16[1,2,8,14464]{3,2,1,0:T(8,128)(2,1)S(1)}, u32[]{:S(2)}, u32[]{:S(2)}) %collective-permute-start.8) | collective-permute-done | bytes 462880 | tf_op jit(solution)/shard_map/ppermute | solution.py:331
  32.3 0.2 maximum_maximum_fusion
  32.6 0.1 collective-permute-start.9
  32.6 0.0 collective-permute-done.10
  32.7 1.4 %collective-permute-start.13 = (bf16[1,2,8,14464]{3,2,1,0:T(8,128)(2,1)S(1)}, bf16[1,2,8,14464]{3,2,1,0:T(8,128)(2,1)S(1)}, u32[]{:S(2)}, u32[]{:S(2)}) collective-permute-start(bf16[1,2,8,14464]{3,2,1,0:T(8,128)(2,1)S(1)} %constant_dynamic-update-slice_fusion.9), channel_id=1, source_target_pairs={{0,16},{1,17},{2,18},{3,19},{4,12},{5,13},{6,14},{7,15},{8,24},{9,... | collective-permute-start | bytes 1388552 | tf_op jit(solution)/shard_map/ppermute | solution.py:331
  34.1 2.3 %collective-permute-done.9 = bf16[2,4,8,14464]{3,2,1,0:T(8,128)(2,1)S(1)} collective-permute-done((bf16[2,4,8,14464]{3,2,1,0:T(8,128)(2,1)S(1)}, bf16[2,4,8,14464]{3,2,1,0:T(8,128)(2,1)S(1)}, u32[]{:S(2)}, u32[]{:S(2)}) %collective-permute-start.9) | collective-permute-done | bytes 1851424 | tf_op jit(solution)/shard_map/ppermute | solution.py:331
  36.4 2.3 %shard_map.112 = (bf16[128,256]{1,0:T(8,128)(2,1)S(1)}, bf16[128,256]{1,0:T(8,128)(2,1)S(1)}, bf16[128,256]{1,0:T(8,128)(2,1)S(1)}, bf16[128,128]{1,0:T(8,128)(2,1)S(1)}) custom-call(s32[1]{0:T(128)} %bitcast.refs_0_, bf16[64,14464]{1,0:T(8,128)(2,1)S(1)} %bitcast.33, bf16[64,14464]{1,0:T(8,128)(2,1)S(1)} %bitcast.37, ...), custom_call_target="tpu_custom_call" | custom-call | tf_op jit(solution)/shard_map/pallas_call | solution.py:280
  38.7 2.5 %shard_map.113 = (bf16[64,7296]{1,0:T(8,128)(2,1)S(1)}, bf16[64,7296]{1,0:T(8,128)(2,1)S(1)}) custom-call(bf16[128,256]{1,0:T(8,128)(2,1)S(1)} %get-tuple-element.99.da_ref.refs_4_, bf16[128,256]{1,0:T(8,128)(2,1)S(1)} %get-tuple-element.100.du_ref.refs_6_, bf16[128,128]{1,0:T(8,128)(2,1)S(1)} %get-tuple-element.101.term_ref, ...), custom_call_target="tpu_custom_call" | custom-call | tf_op jit(solution)/shard_map/pallas_call | solution.py:301
  41.2 0.0 collective-permute-done.12
  41.3 1.1 %collective-permute-done.13 = bf16[1,2,8,14464]{3,2,1,0:T(8,128)(2,1)S(1)} collective-permute-done((bf16[1,2,8,14464]{3,2,1,0:T(8,128)(2,1)S(1)}, bf16[1,2,8,14464]{3,2,1,0:T(8,128)(2,1)S(1)}, u32[]{:S(2)}, u32[]{:S(2)}) %collective-permute-start.13) | collective-permute-done | bytes 462880 | tf_op jit(solution)/shard_map/ppermute | solution.py:331
  42.4 0.0 collective-permute-start.11
  42.4 0.2 maximum_maximum_fusion.1
  42.6 0.6 collective-permute-start.15
  43.2 1.7 %collective-permute-done.11 = bf16[64,7296]{1,0:T(8,128)(2,1)S(1)} collective-permute-done((bf16[64,7296]{1,0:T(8,128)(2,1)S(1)}, bf16[64,7296]{1,0:T(8,128)(2,1)S(1)}, u32[]{:S(2)}, u32[]{:S(2)}) %collective-permute-start.11) | collective-permute-done | bytes 933920 | tf_op jit(solution)/shard_map/ppermute | solution.py:331
  44.9 0.2 add_convert_fusion.1
  45.2 1.2 %collective-permute-start.14 = (bf16[2,2,8,7296]{3,2,1,0:T(8,128)(2,1)S(1)}, bf16[2,2,8,7296]{3,2,1,0:T(8,128)(2,1)S(1)}, u32[]{:S(2)}, u32[]{:S(2)}) collective-permute-start(bf16[2,2,8,7296]{3,2,1,0:T(8,128)(2,1)S(1)} %slice.74), channel_id=1, source_target_pairs={{0,16},{1,17},{2,18},{3,19},{4,12},{5,13},{6,14},{7,15},{8,24},{9,... | collective-permute-start | bytes 1400840 | tf_op jit(solution)/shard_map/ppermute | solution.py:331
  46.3 1.2 %collective-permute-done.15 = bf16[2,4,8,14464]{3,2,1,0:T(8,128)(2,1)S(1)} collective-permute-done((bf16[2,4,8,14464]{3,2,1,0:T(8,128)(2,1)S(1)}, bf16[2,4,8,14464]{3,2,1,0:T(8,128)(2,1)S(1)}, u32[]{:S(2)}, u32[]{:S(2)}) %collective-permute-start.15) | collective-permute-done | bytes 1851424 | tf_op jit(solution)/shard_map/ppermute | solution.py:331
  47.6 2.3 %shard_map.114 = (bf16[128,256]{1,0:T(8,128)(2,1)S(1)}, bf16[128,256]{1,0:T(8,128)(2,1)S(1)}, bf16[128,256]{1,0:T(8,128)(2,1)S(1)}, bf16[128,128]{1,0:T(8,128)(2,1)S(1)}) custom-call(s32[1]{0:T(128)} %bitcast.refs_0_, bf16[64,14464]{1,0:T(8,128)(2,1)S(1)} %bitcast.35, bf16[64,14464]{1,0:T(8,128)(2,1)S(1)} %bitcast.39, ...), custom_call_target="tpu_custom_call" | custom-call | tf_op jit(solution)/shard_map/pallas_call | solution.py:280
  49.9 2.5 %shard_map.115 = (bf16[64,7296]{1,0:T(8,128)(2,1)S(1)}, bf16[64,7296]{1,0:T(8,128)(2,1)S(1)}) custom-call(bf16[128,256]{1,0:T(8,128)(2,1)S(1)} %get-tuple-element.113.da_ref.refs_5_, bf16[128,256]{1,0:T(8,128)(2,1)S(1)} %get-tuple-element.114.du_ref.refs_7_, bf16[128,128]{1,0:T(8,128)(2,1)S(1)} %get-tuple-element.115.term_ref, ...), custom_call_target="tpu_custom_call" | custom-call | tf_op jit(solution)/shard_map/pallas_call | solution.py:301
  52.4 1.4 %collective-permute-done.14 = bf16[2,2,8,7296]{3,2,1,0:T(8,128)(2,1)S(1)} collective-permute-done((bf16[2,2,8,7296]{3,2,1,0:T(8,128)(2,1)S(1)}, bf16[2,2,8,7296]{3,2,1,0:T(8,128)(2,1)S(1)}, u32[]{:S(2)}, u32[]{:S(2)}) %collective-permute-start.14) | collective-permute-done | bytes 466976 | tf_op jit(solution)/shard_map/ppermute | solution.py:331
  53.8 0.0 collective-permute-start.17
  53.8 0.1 add_convert_fusion.2
  53.9 2.4 %collective-permute-done.17 = bf16[64,7296]{1,0:T(8,128)(2,1)S(1)} collective-permute-done((bf16[64,7296]{1,0:T(8,128)(2,1)S(1)}, bf16[64,7296]{1,0:T(8,128)(2,1)S(1)}, u32[]{:S(2)}, u32[]{:S(2)}) %collective-permute-start.17) | collective-permute-done | bytes 933920 | tf_op jit(solution)/shard_map/ppermute | solution.py:331
  56.3 0.2 add_convert_fusion
  56.5 1.2 %collective-permute-start.19 = (bf16[2,2,8,3584]{3,2,1,0:T(8,128)(2,1)S(1)}, bf16[2,2,8,3584]{3,2,1,0:T(8,128)(2,1)S(1)}, u32[]{:S(2)}, u32[]{:S(2)}) collective-permute-start(bf16[2,2,8,3584]{3,2,1,0:T(8,128)(2,1)S(1)} %slice.79), channel_id=1, source_target_pairs={{0,16},{1,17},{2,18},{3,19},{4,12},{5,13},{6,14},{7,15},{8,24},{9,... | collective-permute-start | bytes 688136 | tf_op jit(solution)/shard_map/ppermute | solution.py:331
  57.7 1.0 %collective-permute-start.16 = (bf16[2,1,8,7296]{3,2,1,0:T(8,128)(2,1)S(1)}, bf16[2,1,8,7296]{3,2,1,0:T(8,128)(2,1)S(1)}, u32[]{:S(2)}, u32[]{:S(2)}) collective-permute-start(bf16[2,1,8,7296]{3,2,1,0:T(8,128)(2,1)S(1)} %slice.75), channel_id=1, source_target_pairs={{0,8},{1,9},{2,10},{3,11},{4,20},{5,21},{6,22},{7,23},{8,0},{9,1},... | collective-permute-start | bytes 700424 | tf_op jit(solution)/shard_map/ppermute | solution.py:331
  58.8 1.0 %collective-permute-start.18 = (bf16[2,2,8,3712]{3,2,1,0:T(8,128)(2,1)S(1)}, bf16[2,2,8,3712]{3,2,1,0:T(8,128)(2,1)S(1)}, u32[]{:S(2)}, u32[]{:S(2)}) collective-permute-start(bf16[2,2,8,3712]{3,2,1,0:T(8,128)(2,1)S(1)} %slice.77), channel_id=1, source_target_pairs={{0,16},{1,17},{2,18},{3,19},{4,12},{5,13},{6,14},{7,15},{8,24},{9,... | collective-permute-start | bytes 712712 | tf_op jit(solution)/shard_map/ppermute | solution.py:331
  59.8 5.2 %collective-permute-done.19 = bf16[2,2,8,3584]{3,2,1,0:T(8,128)(2,1)S(1)} collective-permute-done((bf16[2,2,8,3584]{3,2,1,0:T(8,128)(2,1)S(1)}, bf16[2,2,8,3584]{3,2,1,0:T(8,128)(2,1)S(1)}, u32[]{:S(2)}, u32[]{:S(2)}) %collective-permute-start.19) | collective-permute-done | bytes 229408 | tf_op jit(solution)/shard_map/ppermute | solution.py:331
  65.0 0.1 add_convert_fusion.5
  65.1 1.0 %collective-permute-start.21 = (bf16[2,1,8,3584]{3,2,1,0:T(8,128)(2,1)S(1)}, bf16[2,1,8,3584]{3,2,1,0:T(8,128)(2,1)S(1)}, u32[]{:S(2)}, u32[]{:S(2)}) collective-permute-start(bf16[2,1,8,3584]{3,2,1,0:T(8,128)(2,1)S(1)} %slice.82), channel_id=1, source_target_pairs={{0,8},{1,9},{2,10},{3,11},{4,20},{5,21},{6,22},{7,23},{8,0},{9,1},... | collective-permute-start | bytes 344072 | tf_op jit(solution)/shard_map/ppermute | solution.py:331
  66.1 2.7 %collective-permute-done.18 = bf16[2,2,8,3712]{3,2,1,0:T(8,128)(2,1)S(1)} collective-permute-done((bf16[2,2,8,3712]{3,2,1,0:T(8,128)(2,1)S(1)}, bf16[2,2,8,3712]{3,2,1,0:T(8,128)(2,1)S(1)}, u32[]{:S(2)}, u32[]{:S(2)}) %collective-permute-start.18) | collective-permute-done | bytes 237600 | tf_op jit(solution)/shard_map/ppermute | solution.py:331
  68.8 0.1 add_convert_fusion.3
  68.9 0.0 collective-permute-done.16
  68.9 1.1 %collective-permute-start.22 = (bf16[2,1,8,3712]{3,2,1,0:T(8,128)(2,1)S(1)}, bf16[2,1,8,3712]{3,2,1,0:T(8,128)(2,1)S(1)}, u32[]{:S(2)}, u32[]{:S(2)}) collective-permute-start(bf16[2,1,8,3712]{3,2,1,0:T(8,128)(2,1)S(1)} %slice.83), channel_id=1, source_target_pairs={{0,8},{1,9},{2,10},{3,11},{4,20},{5,21},{6,22},{7,23},{8,0},{9,1},... | collective-permute-start | bytes 356360 | tf_op jit(solution)/shard_map/ppermute | solution.py:331
  70.0 0.1 add_convert_fusion.4
  70.1 0.1 collective-permute-start.20
  70.2 0.0 collective-permute-done.21
  70.2 3.6 %collective-permute-done.22 = bf16[2,1,8,3712]{3,2,1,0:T(8,128)(2,1)S(1)} collective-permute-done((bf16[2,1,8,3712]{3,2,1,0:T(8,128)(2,1)S(1)}, bf16[2,1,8,3712]{3,2,1,0:T(8,128)(2,1)S(1)}, u32[]{:S(2)}, u32[]{:S(2)}) %collective-permute-start.22) | collective-permute-done | bytes 118816 | tf_op jit(solution)/shard_map/ppermute | solution.py:331
  73.9 0.3 collective-permute-start.24
  74.2 3.0 %collective-permute-start.23 = (bf16[1,8,7296]{2,1,0:T(8,128)(2,1)S(1)}, bf16[1,8,7296]{2,1,0:T(8,128)(2,1)S(1)}, u32[]{:S(2)}, u32[]{:S(2)}) collective-permute-start(bf16[1,8,7296]{2,1,0:T(8,128)(2,1)S(1)} %get-tuple-element.146), channel_id=1, source_target_pairs={{0,3},{1,0},{2,1},{3,2},{4,7},{5,4},{6,5},{7,6},{8,11},{9,8},{10,9... | collective-permute-start | bytes 350216 | tf_op jit(solution)/shard_map/ppermute | solution.py:331
  77.1 4.7 %shard_map.116 = (bf16[7168,256]{1,0:T(8,128)(2,1)}, bf16[7168,256]{1,0:T(8,128)(2,1)}, bf16[256,7168]{1,0:T(8,128)(2,1)}) custom-call(bf16[64,14464]{1,0:T(8,128)(2,1)S(1)} %bitcast.34, bf16[64,14464]{1,0:T(8,128)(2,1)S(1)} %bitcast.38, bf16[64,14464]{1,0:T(8,128)(2,1)S(1)} %bitcast.36, bf16[64,14464]{1,0:T(8,128)(2,1)S(1)} %bitcast.40, ...), custom_call_target="tpu_custom_call" | custom-call | bytes 4194304 | tf_op jit(solution)/shard_map/pallas_call | solution.py:174
  81.9 0.1 collective-permute-done.24
  82.0 0.8 shard_map.117
  (29 shorter events, 0.6 us)
Async XLA Ops:
  1.7 11.2 %collective-permute-start.2 = (bf16[1,1,8,14464]{3,2,1,0:T(8,128)(2,1)S(1)}, bf16[1,1,8,14464]{3,2,1,0:T(8,128)(2,1)S(1)}, u32[]{:S(2)}, u32[]{:S(2)}) collective-permute-start(bf16[1,1,8,14464]{3,2,1,0:T(8,128)(2,1)S(1)} %bitcast.41), channel_id=1, source_target_pairs={{0,3},{1,0},{2,1},{3,2},{4,7},{5,4},{6,5},{7,6},{8,11},{9,8},{10,9... | collective-permute-start | bytes 694280 | tf_op jit(solution)/shard_map/ppermute | solution.py:331
  6.8 11.8 %collective-permute-start.1 = (bf16[1,1,8,14464]{3,2,1,0:T(8,128)(2,1)S(1)}, bf16[1,1,8,14464]{3,2,1,0:T(8,128)(2,1)S(1)}, u32[]{:S(2)}, u32[]{:S(2)}) collective-permute-start(bf16[1,1,8,14464]{3,2,1,0:T(8,128)(2,1)S(1)} %bitcast.42), channel_id=1, source_target_pairs={{0,16},{1,17},{2,18},{3,19},{4,12},{5,13},{6,14},{7,15},{8,24},{9,... | collective-permute-start | bytes 694280 | tf_op jit(solution)/shard_map/ppermute | solution.py:331
  8.3 10.3 %collective-permute-start = (bf16[1,1,8,14464]{3,2,1,0:T(8,128)(2,1)S(1)}, bf16[1,1,8,14464]{3,2,1,0:T(8,128)(2,1)S(1)}, u32[]{:S(2)}, u32[]{:S(2)}) collective-permute-start(bf16[1,1,8,14464]{3,2,1,0:T(8,128)(2,1)S(1)} %bitcast.43), channel_id=1, source_target_pairs={{0,8},{1,9},{2,10},{3,11},{4,20},{5,21},{6,22},{7,23},{8,0},{9,1},... | collective-permute-start | bytes 694280 | tf_op jit(solution)/shard_map/ppermute | solution.py:331
  9.8 10.4 %collective-permute-start.4 = (bf16[1,1,8,14464]{3,2,1,0:T(8,128)(2,1)S(1)}, bf16[1,1,8,14464]{3,2,1,0:T(8,128)(2,1)S(1)}, u32[]{:S(2)}, u32[]{:S(2)}) collective-permute-start(bf16[1,1,8,14464]{3,2,1,0:T(8,128)(2,1)S(1)} %bitcast.44), channel_id=1, source_target_pairs={{0,1},{1,2},{2,3},{3,0},{4,5},{5,6},{6,7},{7,4},{8,9},{9,10},{10,1... | collective-permute-start | bytes 694280 | tf_op jit(solution)/shard_map/ppermute | solution.py:331
  12.9 8.0 %collective-permute-start.7 = (bf16[1,1,8,14464]{3,2,1,0:T(8,128)(2,1)S(1)}, bf16[1,1,8,14464]{3,2,1,0:T(8,128)(2,1)S(1)}, u32[]{:S(2)}, u32[]{:S(2)}) collective-permute-start(bf16[1,1,8,14464]{3,2,1,0:T(8,128)(2,1)S(1)} %collective-permute-done.2), channel_id=1, source_target_pairs={{0,8},{1,9},{2,10},{3,11},{4,20},{5,21},{6,22},{7,23},{8,0},{9,1},... | collective-permute-start | bytes 694280 | tf_op jit(solution)/shard_map/ppermute | solution.py:331
  14.3 8.8 %collective-permute-start.6 = (bf16[1,1,8,14464]{3,2,1,0:T(8,128)(2,1)S(1)}, bf16[1,1,8,14464]{3,2,1,0:T(8,128)(2,1)S(1)}, u32[]{:S(2)}, u32[]{:S(2)}) collective-permute-start(bf16[1,1,8,14464]{3,2,1,0:T(8,128)(2,1)S(1)} %collective-permute-done.2), channel_id=1, source_target_pairs={{0,3},{1,0},{2,1},{3,2},{4,7},{5,4},{6,5},{7,6},{8,11},{9,8},{10,9... | collective-permute-start | bytes 694280 | tf_op jit(solution)/shard_map/ppermute | solution.py:331
  18.6 11.2 %collective-permute-start.3 = (bf16[1,1,8,14464]{3,2,1,0:T(8,128)(2,1)S(1)}, bf16[1,1,8,14464]{3,2,1,0:T(8,128)(2,1)S(1)}, u32[]{:S(2)}, u32[]{:S(2)}) collective-permute-start(bf16[1,1,8,14464]{3,2,1,0:T(8,128)(2,1)S(1)} %collective-permute-done), channel_id=1, source_target_pairs={{0,16},{1,17},{2,18},{3,19},{4,12},{5,13},{6,14},{7,15},{8,24},{9,... | collective-permute-start | bytes 694280 | tf_op jit(solution)/shard_map/ppermute | solution.py:331
  20.2 8.6 %collective-permute-start.5 = (bf16[1,1,8,14464]{3,2,1,0:T(8,128)(2,1)S(1)}, bf16[1,1,8,14464]{3,2,1,0:T(8,128)(2,1)S(1)}, u32[]{:S(2)}, u32[]{:S(2)}) collective-permute-start(bf16[1,1,8,14464]{3,2,1,0:T(8,128)(2,1)S(1)} %collective-permute-done.4), channel_id=1, source_target_pairs={{0,8},{1,9},{2,10},{3,11},{4,20},{5,21},{6,22},{7,23},{8,0},{9,1},... | collective-permute-start | bytes 694280 | tf_op jit(solution)/shard_map/ppermute | solution.py:331
  20.9 11.5 %collective-permute-start.8 = (bf16[1,2,8,14464]{3,2,1,0:T(8,128)(2,1)S(1)}, bf16[1,2,8,14464]{3,2,1,0:T(8,128)(2,1)S(1)}, u32[]{:S(2)}, u32[]{:S(2)}) collective-permute-start(bf16[1,2,8,14464]{3,2,1,0:T(8,128)(2,1)S(1)} %constant_dynamic-update-slice_fusion.3), channel_id=1, source_target_pairs={{0,16},{1,17},{2,18},{3,19},{4,12},{5,13},{6,14},{7,15},{8,24},{9,... | collective-permute-start | bytes 1388552 | tf_op jit(solution)/shard_map/ppermute | solution.py:331
  23.1 9.5 %collective-permute-start.10 = (bf16[1,1,8,14464]{3,2,1,0:T(8,128)(2,1)S(1)}, bf16[1,1,8,14464]{3,2,1,0:T(8,128)(2,1)S(1)}, u32[]{:S(2)}, u32[]{:S(2)}) collective-permute-start(bf16[1,1,8,14464]{3,2,1,0:T(8,128)(2,1)S(1)} %collective-permute-done.6), channel_id=1, source_target_pairs={{0,8},{1,9},{2,10},{3,11},{4,20},{5,21},{6,22},{7,23},{8,0},{9,1},... | collective-permute-start | bytes 694280 | tf_op jit(solution)/shard_map/ppermute | solution.py:331
  28.9 12.4 %collective-permute-start.12 = (bf16[1,2,8,14464]{3,2,1,0:T(8,128)(2,1)S(1)}, bf16[1,2,8,14464]{3,2,1,0:T(8,128)(2,1)S(1)}, u32[]{:S(2)}, u32[]{:S(2)}) collective-permute-start(bf16[1,2,8,14464]{3,2,1,0:T(8,128)(2,1)S(1)} %constant_dynamic-update-slice_fusion.5), channel_id=1, source_target_pairs={{0,16},{1,17},{2,18},{3,19},{4,12},{5,13},{6,14},{7,15},{8,24},{9,... | collective-permute-start | bytes 1388552 | tf_op jit(solution)/shard_map/ppermute | solution.py:331
  32.6 3.9 %collective-permute-start.9 = (bf16[2,4,8,14464]{3,2,1,0:T(8,128)(2,1)S(1)}, bf16[2,4,8,14464]{3,2,1,0:T(8,128)(2,1)S(1)}, u32[]{:S(2)}, u32[]{:S(2)}) collective-permute-start(bf16[2,4,8,14464]{3,2,1,0:T(8,128)(2,1)S(1)} %maximum_maximum_fusion), channel_id=1, source_target_pairs={{0,4},{1,5},{2,6},{3,7},{4,0},{5,1},{6,2},{7,3},{8,12},{9,13},{10,... | collective-permute-start | bytes 5554184 | tf_op jit(solution)/shard_map/ppermute | solution.py:331
  32.7 9.7 %collective-permute-start.13 = (bf16[1,2,8,14464]{3,2,1,0:T(8,128)(2,1)S(1)}, bf16[1,2,8,14464]{3,2,1,0:T(8,128)(2,1)S(1)}, u32[]{:S(2)}, u32[]{:S(2)}) collective-permute-start(bf16[1,2,8,14464]{3,2,1,0:T(8,128)(2,1)S(1)} %constant_dynamic-update-slice_fusion.9), channel_id=1, source_target_pairs={{0,16},{1,17},{2,18},{3,19},{4,12},{5,13},{6,14},{7,15},{8,24},{9,... | collective-permute-start | bytes 1388552 | tf_op jit(solution)/shard_map/ppermute | solution.py:331
  42.4 2.5 %collective-permute-start.11 = (bf16[64,7296]{1,0:T(8,128)(2,1)S(1)}, bf16[64,7296]{1,0:T(8,128)(2,1)S(1)}, u32[]{:S(2)}, u32[]{:S(2)}) collective-permute-start(bf16[64,7296]{1,0:T(8,128)(2,1)S(1)} %get-tuple-element.103), channel_id=1, source_target_pairs={{0,4},{1,5},{2,6},{3,7},{4,0},{5,1},{6,2},{7,3},{8,12},{9,13},{10,... | collective-permute-start | bytes 2801672 | tf_op jit(solution)/shard_map/ppermute | solution.py:331
  42.6 4.9 %collective-permute-start.15 = (bf16[2,4,8,14464]{3,2,1,0:T(8,128)(2,1)S(1)}, bf16[2,4,8,14464]{3,2,1,0:T(8,128)(2,1)S(1)}, u32[]{:S(2)}, u32[]{:S(2)}) collective-permute-start(bf16[2,4,8,14464]{3,2,1,0:T(8,128)(2,1)S(1)} %maximum_maximum_fusion.1), channel_id=1, source_target_pairs={{0,4},{1,5},{2,6},{3,7},{4,0},{5,1},{6,2},{7,3},{8,12},{9,13},{10,... | collective-permute-start | bytes 5554184 | tf_op jit(solution)/shard_map/ppermute | solution.py:331
  45.2 8.6 %collective-permute-start.14 = (bf16[2,2,8,7296]{3,2,1,0:T(8,128)(2,1)S(1)}, bf16[2,2,8,7296]{3,2,1,0:T(8,128)(2,1)S(1)}, u32[]{:S(2)}, u32[]{:S(2)}) collective-permute-start(bf16[2,2,8,7296]{3,2,1,0:T(8,128)(2,1)S(1)} %slice.74), channel_id=1, source_target_pairs={{0,16},{1,17},{2,18},{3,19},{4,12},{5,13},{6,14},{7,15},{8,24},{9,... | collective-permute-start | bytes 1400840 | tf_op jit(solution)/shard_map/ppermute | solution.py:331
  53.8 2.5 %collective-permute-start.17 = (bf16[64,7296]{1,0:T(8,128)(2,1)S(1)}, bf16[64,7296]{1,0:T(8,128)(2,1)S(1)}, u32[]{:S(2)}, u32[]{:S(2)}) collective-permute-start(bf16[64,7296]{1,0:T(8,128)(2,1)S(1)} %get-tuple-element.119), channel_id=1, source_target_pairs={{0,4},{1,5},{2,6},{3,7},{4,0},{5,1},{6,2},{7,3},{8,12},{9,13},{10,... | collective-permute-start | bytes 2801672 | tf_op jit(solution)/shard_map/ppermute | solution.py:331
  56.5 8.5 %collective-permute-start.19 = (bf16[2,2,8,3584]{3,2,1,0:T(8,128)(2,1)S(1)}, bf16[2,2,8,3584]{3,2,1,0:T(8,128)(2,1)S(1)}, u32[]{:S(2)}, u32[]{:S(2)}) collective-permute-start(bf16[2,2,8,3584]{3,2,1,0:T(8,128)(2,1)S(1)} %slice.79), channel_id=1, source_target_pairs={{0,16},{1,17},{2,18},{3,19},{4,12},{5,13},{6,14},{7,15},{8,24},{9,... | collective-permute-start | bytes 688136 | tf_op jit(solution)/shard_map/ppermute | solution.py:331
  57.7 11.1 %collective-permute-start.16 = (bf16[2,1,8,7296]{3,2,1,0:T(8,128)(2,1)S(1)}, bf16[2,1,8,7296]{3,2,1,0:T(8,128)(2,1)S(1)}, u32[]{:S(2)}, u32[]{:S(2)}) collective-permute-start(bf16[2,1,8,7296]{3,2,1,0:T(8,128)(2,1)S(1)} %slice.75), channel_id=1, source_target_pairs={{0,8},{1,9},{2,10},{3,11},{4,20},{5,21},{6,22},{7,23},{8,0},{9,1},... | collective-permute-start | bytes 700424 | tf_op jit(solution)/shard_map/ppermute | solution.py:331
  58.8 10.0 %collective-permute-start.18 = (bf16[2,2,8,3712]{3,2,1,0:T(8,128)(2,1)S(1)}, bf16[2,2,8,3712]{3,2,1,0:T(8,128)(2,1)S(1)}, u32[]{:S(2)}, u32[]{:S(2)}) collective-permute-start(bf16[2,2,8,3712]{3,2,1,0:T(8,128)(2,1)S(1)} %slice.77), channel_id=1, source_target_pairs={{0,16},{1,17},{2,18},{3,19},{4,12},{5,13},{6,14},{7,15},{8,24},{9,... | collective-permute-start | bytes 712712 | tf_op jit(solution)/shard_map/ppermute | solution.py:331
  65.1 5.1 %collective-permute-start.21 = (bf16[2,1,8,3584]{3,2,1,0:T(8,128)(2,1)S(1)}, bf16[2,1,8,3584]{3,2,1,0:T(8,128)(2,1)S(1)}, u32[]{:S(2)}, u32[]{:S(2)}) collective-permute-start(bf16[2,1,8,3584]{3,2,1,0:T(8,128)(2,1)S(1)} %slice.82), channel_id=1, source_target_pairs={{0,8},{1,9},{2,10},{3,11},{4,20},{5,21},{6,22},{7,23},{8,0},{9,1},... | collective-permute-start | bytes 344072 | tf_op jit(solution)/shard_map/ppermute | solution.py:331
  68.9 4.9 %collective-permute-start.22 = (bf16[2,1,8,3712]{3,2,1,0:T(8,128)(2,1)S(1)}, bf16[2,1,8,3712]{3,2,1,0:T(8,128)(2,1)S(1)}, u32[]{:S(2)}, u32[]{:S(2)}) collective-permute-start(bf16[2,1,8,3712]{3,2,1,0:T(8,128)(2,1)S(1)} %slice.83), channel_id=1, source_target_pairs={{0,8},{1,9},{2,10},{3,11},{4,20},{5,21},{6,22},{7,23},{8,0},{9,1},... | collective-permute-start | bytes 356360 | tf_op jit(solution)/shard_map/ppermute | solution.py:331
  70.1 11.8 %collective-permute-start.20 = (bf16[1,8,7296]{2,1,0:T(8,128)(2,1)S(1)}, bf16[1,8,7296]{2,1,0:T(8,128)(2,1)S(1)}, u32[]{:S(2)}, u32[]{:S(2)}) collective-permute-start(bf16[1,8,7296]{2,1,0:T(8,128)(2,1)S(1)} %get-tuple-element.147), channel_id=1, source_target_pairs={{0,1},{1,2},{2,3},{3,0},{4,5},{5,6},{6,7},{7,4},{8,9},{9,10},{10,1... | collective-permute-start | bytes 350216 | tf_op jit(solution)/shard_map/ppermute | solution.py:331
  73.9 8.1 %collective-permute-start.24 = (bf16[1,8,7296]{2,1,0:T(8,128)(2,1)S(1)}, bf16[1,8,7296]{2,1,0:T(8,128)(2,1)S(1)}, u32[]{:S(2)}, u32[]{:S(2)}) collective-permute-start(bf16[1,8,7296]{2,1,0:T(8,128)(2,1)S(1)} %get-tuple-element.145), channel_id=1, source_target_pairs={{0,2},{1,3},{2,0},{3,1},{4,6},{5,7},{6,4},{7,5},{8,10},{9,11},{10,... | collective-permute-start | bytes 350216 | tf_op jit(solution)/shard_map/ppermute | solution.py:331
  74.2 7.8 %collective-permute-start.23 = (bf16[1,8,7296]{2,1,0:T(8,128)(2,1)S(1)}, bf16[1,8,7296]{2,1,0:T(8,128)(2,1)S(1)}, u32[]{:S(2)}, u32[]{:S(2)}) collective-permute-start(bf16[1,8,7296]{2,1,0:T(8,128)(2,1)S(1)} %get-tuple-element.146), channel_id=1, source_target_pairs={{0,3},{1,0},{2,1},{3,2},{4,7},{5,4},{6,5},{7,6},{8,11},{9,8},{10,9... | collective-permute-start | bytes 350216 | tf_op jit(solution)/shard_map/ppermute | solution.py:331
  77.1 4.8 %copy-start = (s32[8,4]{0,1:T(4,128)S(1)}, s32[8,4]{0,1:T(4,128)}, u32[]{:S(2)}) copy-start(s32[8,4]{0,1:T(4,128)} %param.9) | copy-start | bytes 388

commit v5 on v4

--- a/solution.py
+++ b/solution.py
@@ -418,10 +418,10 @@
     hi_r1 = cross(upper(hi), 1)
     lo = tock(folded(*tick(lo, lo_r1)))
     lo_r2 = cross(upper(lo), 0)
+    first_sum = tock(folded(*tick(first_sum, first_r2)))
+    from_u = rotate(first_sum[1], 1)
     hi = tock(folded(*tick(hi, hi_r1)))
     hi_r2 = cross(upper(hi), 0)
-    first_sum = tock(folded(*tick(first_sum, first_r2)))
-    from_u = rotate(first_sum[1], 1)
     lo, lo_r2, hi, hi_r2 = tick(lo, lo_r2, hi, hi_r2)
     second_sum = tock(jnp.concatenate((folded(lo, lo_r2), folded(hi, hi_r2)), axis=-1))
     from_v = rotate(second_sum[0], -1)

time: 82.9 us -> 82 us (0.989)
  waiting for transfers between devices: 29.1 us -> 27.6 us
    ppermute x25, waiting for transfers between devices: 29.1 us -> 27.6 us  [permute(): return lax.ppermute(value, AXES, pairs)]
  transfers between devices with their start and end apart: 25 -> 25, of which waited for: 14 -> 15; matrix products, arithmetic and copies ran while one was open for 2% -> 2% of each run, Pallas kernels for 22% -> 23%
where the time goes in v5:
time: 82 us; the launch traced here: 81.8 us
  starting transfers between devices  31.2 us (38%)
  waiting for transfers between devices  27.6 us (34%)
  Pallas kernels  20.4 us (25%)
  other arithmetic  1.27 us (2%)
  between operations  0.9 us (1%)
    ppermute x25, starting transfers between devices, permute(): return lax.ppermute(value, AXES, pairs)  31.2 us
    ppermute x25, waiting for transfers between devices, permute(): return lax.ppermute(value, AXES, pairs)  27.6 us
    pallas_call x2, Pallas kernels, row_terms(): pl.pallas_call(functools.partial(rows_kernel, width=width, chunk=chunk),...  4.95 us
    pallas_call x1, Pallas kernels, weight_terms(): pl.pallas_call(functools.partial(weights_kernel, blocks=len(rows), groups...  4.75 us
    pallas_call x2, Pallas kernels, hidden_terms(): pl.pallas_call(functools.partial(hidden_kernel, width=width, chunk=chunk,...  4.65 us
    pallas_call x1, Pallas kernels, load(): pl.pallas_call(load_kernel, out_shape=tuple((pltpu.VMEM(v.shape, v.dtype)...  4.23 us
  transfers between devices with their start and end apart: 25, of which 15 were waited for; matrix products, arithmetic and copies ran while one was open for 2% of the time, Pallas kernels for 23%

profile of v5, /device:TPU:0, one launch (start us, length us, event | category | flops | bytes accessed | tf_op | source)
XLA Modules:
  0.0 81.8 jit_solution(7931792290717751888)
XLA Ops:
  0.6 1.0 %shard_map.110 = bf16[8,14464]{1,0:T(8,128)(2,1)S(1)} custom-call(bf16[8,7168]{1,0:T(8,128)(2,1)} %tokens_hbm.1, bf16[8,7168]{1,0:T(8,128)(2,1)} %grad_hbm.1, s32[4,8]{1,0:T(4,128)} %bitcast.50, bf16[4,8]{1,0:T(4,128)(2,1)} %bitcast.61), custom_call_target="tpu_custom_call" | custom-call | tf_op jit(solution)/shard_map/pallas_call | solution.py:79
  1.7 5.1 %collective-permute-start.2 = (bf16[1,1,8,14464]{3,2,1,0:T(8,128)(2,1)S(1)}, bf16[1,1,8,14464]{3,2,1,0:T(8,128)(2,1)S(1)}, u32[]{:S(2)}, u32[]{:S(2)}) collective-permute-start(bf16[1,1,8,14464]{3,2,1,0:T(8,128)(2,1)S(1)} %bitcast.41), channel_id=1, source_target_pairs={{0,3},{1,0},{2,1},{3,2},{4,7},{5,4},{6,5},{7,6},{8,11},{9,8},{10,9... | collective-permute-start | bytes 694280 | tf_op jit(solution)/shard_map/ppermute | solution.py:331
  6.8 1.5 %collective-permute-start.1 = (bf16[1,1,8,14464]{3,2,1,0:T(8,128)(2,1)S(1)}, bf16[1,1,8,14464]{3,2,1,0:T(8,128)(2,1)S(1)}, u32[]{:S(2)}, u32[]{:S(2)}) collective-permute-start(bf16[1,1,8,14464]{3,2,1,0:T(8,128)(2,1)S(1)} %bitcast.42), channel_id=1, source_target_pairs={{0,16},{1,17},{2,18},{3,19},{4,12},{5,13},{6,14},{7,15},{8,24},{9,... | collective-permute-start | bytes 694280 | tf_op jit(solution)/shard_map/ppermute | solution.py:331
  8.3 1.5 %collective-permute-start = (bf16[1,1,8,14464]{3,2,1,0:T(8,128)(2,1)S(1)}, bf16[1,1,8,14464]{3,2,1,0:T(8,128)(2,1)S(1)}, u32[]{:S(2)}, u32[]{:S(2)}) collective-permute-start(bf16[1,1,8,14464]{3,2,1,0:T(8,128)(2,1)S(1)} %bitcast.43), channel_id=1, source_target_pairs={{0,8},{1,9},{2,10},{3,11},{4,20},{5,21},{6,22},{7,23},{8,0},{9,1},... | collective-permute-start | bytes 694280 | tf_op jit(solution)/shard_map/ppermute | solution.py:331
  9.8 0.0 collective-permute-start.4
  9.8 3.1 %collective-permute-done.2 = bf16[1,1,8,14464]{3,2,1,0:T(8,128)(2,1)S(1)} collective-permute-done((bf16[1,1,8,14464]{3,2,1,0:T(8,128)(2,1)S(1)}, bf16[1,1,8,14464]{3,2,1,0:T(8,128)(2,1)S(1)}, u32[]{:S(2)}, u32[]{:S(2)}) %collective-permute-start.2) | collective-permute-done | bytes 231456 | tf_op jit(solution)/shard_map/ppermute | solution.py:331
  12.9 1.4 %collective-permute-start.7 = (bf16[1,1,8,14464]{3,2,1,0:T(8,128)(2,1)S(1)}, bf16[1,1,8,14464]{3,2,1,0:T(8,128)(2,1)S(1)}, u32[]{:S(2)}, u32[]{:S(2)}) collective-permute-start(bf16[1,1,8,14464]{3,2,1,0:T(8,128)(2,1)S(1)} %collective-permute-done.2), channel_id=1, source_target_pairs={{0,8},{1,9},{2,10},{3,11},{4,20},{5,21},{6,22},{7,23},{8,0},{9,1},... | collective-permute-start | bytes 694280 | tf_op jit(solution)/shard_map/ppermute | solution.py:331
  14.3 4.3 %collective-permute-start.6 = (bf16[1,1,8,14464]{3,2,1,0:T(8,128)(2,1)S(1)}, bf16[1,1,8,14464]{3,2,1,0:T(8,128)(2,1)S(1)}, u32[]{:S(2)}, u32[]{:S(2)}) collective-permute-start(bf16[1,1,8,14464]{3,2,1,0:T(8,128)(2,1)S(1)} %collective-permute-done.2), channel_id=1, source_target_pairs={{0,3},{1,0},{2,1},{3,2},{4,7},{5,4},{6,5},{7,6},{8,11},{9,8},{10,9... | collective-permute-start | bytes 694280 | tf_op jit(solution)/shard_map/ppermute | solution.py:331
  18.6 0.0 collective-permute-done.1
  18.6 1.5 %collective-permute-start.3 = (bf16[1,1,8,14464]{3,2,1,0:T(8,128)(2,1)S(1)}, bf16[1,1,8,14464]{3,2,1,0:T(8,128)(2,1)S(1)}, u32[]{:S(2)}, u32[]{:S(2)}) collective-permute-start(bf16[1,1,8,14464]{3,2,1,0:T(8,128)(2,1)S(1)} %collective-permute-done), channel_id=1, source_target_pairs={{0,16},{1,17},{2,18},{3,19},{4,12},{5,13},{6,14},{7,15},{8,24},{9,... | collective-permute-start | bytes 694280 | tf_op jit(solution)/shard_map/ppermute | solution.py:331
  20.2 0.6 collective-permute-start.5
  20.8 0.0 collective-permute-done.7
  20.9 1.0 %collective-permute-start.8 = (bf16[1,2,8,14464]{3,2,1,0:T(8,128)(2,1)S(1)}, bf16[1,2,8,14464]{3,2,1,0:T(8,128)(2,1)S(1)}, u32[]{:S(2)}, u32[]{:S(2)}) collective-permute-start(bf16[1,2,8,14464]{3,2,1,0:T(8,128)(2,1)S(1)} %constant_dynamic-update-slice_fusion.3), channel_id=1, source_target_pairs={{0,16},{1,17},{2,18},{3,19},{4,12},{5,13},{6,14},{7,15},{8,24},{9,... | collective-permute-start | bytes 1388552 | tf_op jit(solution)/shard_map/ppermute | solution.py:331
  21.9 1.2 %collective-permute-done.6 = bf16[1,1,8,14464]{3,2,1,0:T(8,128)(2,1)S(1)} collective-permute-done((bf16[1,1,8,14464]{3,2,1,0:T(8,128)(2,1)S(1)}, bf16[1,1,8,14464]{3,2,1,0:T(8,128)(2,1)S(1)}, u32[]{:S(2)}, u32[]{:S(2)}) %collective-permute-start.6) | collective-permute-done | bytes 231456 | tf_op jit(solution)/shard_map/ppermute | solution.py:331
  23.1 0.9 %collective-permute-start.10 = (bf16[1,1,8,14464]{3,2,1,0:T(8,128)(2,1)S(1)}, bf16[1,1,8,14464]{3,2,1,0:T(8,128)(2,1)S(1)}, u32[]{:S(2)}, u32[]{:S(2)}) collective-permute-start(bf16[1,1,8,14464]{3,2,1,0:T(8,128)(2,1)S(1)} %collective-permute-done.6), channel_id=1, source_target_pairs={{0,8},{1,9},{2,10},{3,11},{4,20},{5,21},{6,22},{7,23},{8,0},{9,1},... | collective-permute-start | bytes 694280 | tf_op jit(solution)/shard_map/ppermute | solution.py:331
  24.0 4.2 %shard_map.111 = (bf16[7168,256]{1,0:T(8,128)(2,1)S(1)}, bf16[7168,256]{1,0:T(8,128)(2,1)S(1)}, bf16[256,7168]{1,0:T(8,128)(2,1)S(1)}) custom-call(bf16[7168,256]{1,0:T(8,128)(2,1)} %bitcast.58, bf16[7168,256]{1,0:T(8,128)(2,1)} %bitcast.59, bf16[256,7168]{1,0:T(8,128)(2,1)} %bitcast.60), custom_call_target="tpu_custom_call" | custom-call | tf_op jit(solution)/shard_map/pallas_call | solution.py:37
  28.2 0.6 collective-permute-done.5
  28.9 0.9 %collective-permute-start.12 = (bf16[1,2,8,14464]{3,2,1,0:T(8,128)(2,1)S(1)}, bf16[1,2,8,14464]{3,2,1,0:T(8,128)(2,1)S(1)}, u32[]{:S(2)}, u32[]{:S(2)}) collective-permute-start(bf16[1,2,8,14464]{3,2,1,0:T(8,128)(2,1)S(1)} %constant_dynamic-update-slice_fusion.5), channel_id=1, source_target_pairs={{0,16},{1,17},{2,18},{3,19},{4,12},{5,13},{6,14},{7,15},{8,24},{9,... | collective-permute-start | bytes 1388552 | tf_op jit(solution)/shard_map/ppermute | solution.py:331
  29.8 0.0 collective-permute-done.3
  29.9 2.5 %collective-permute-done.8 = bf16[1,2,8,14464]{3,2,1,0:T(8,128)(2,1)S(1)} collective-permute-done((bf16[1,2,8,14464]{3,2,1,0:T(8,128)(2,1)S(1)}, bf16[1,2,8,14464]{3,2,1,0:T(8,128)(2,1)S(1)}, u32[]{:S(2)}, u32[]{:S(2)}) %collective-permute-start.8) | collective-permute-done | bytes 462880 | tf_op jit(solution)/shard_map/ppermute | solution.py:331
  32.3 0.2 maximum_maximum_fusion
  32.6 0.1 collective-permute-start.9
  32.6 0.0 collective-permute-done.10
  32.7 1.4 %collective-permute-start.13 = (bf16[1,2,8,14464]{3,2,1,0:T(8,128)(2,1)S(1)}, bf16[1,2,8,14464]{3,2,1,0:T(8,128)(2,1)S(1)}, u32[]{:S(2)}, u32[]{:S(2)}) collective-permute-start(bf16[1,2,8,14464]{3,2,1,0:T(8,128)(2,1)S(1)} %constant_dynamic-update-slice_fusion.9), channel_id=1, source_target_pairs={{0,16},{1,17},{2,18},{3,19},{4,12},{5,13},{6,14},{7,15},{8,24},{9,... | collective-permute-start | bytes 1388552 | tf_op jit(solution)/shard_map/ppermute | solution.py:331
  34.1 2.3 %collective-permute-done.9 = bf16[2,4,8,14464]{3,2,1,0:T(8,128)(2,1)S(1)} collective-permute-done((bf16[2,4,8,14464]{3,2,1,0:T(8,128)(2,1)S(1)}, bf16[2,4,8,14464]{3,2,1,0:T(8,128)(2,1)S(1)}, u32[]{:S(2)}, u32[]{:S(2)}) %collective-permute-start.9) | collective-permute-done | bytes 1851424 | tf_op jit(solution)/shard_map/ppermute | solution.py:331
  36.4 2.3 %shard_map.112 = (bf16[128,256]{1,0:T(8,128)(2,1)S(1)}, bf16[128,256]{1,0:T(8,128)(2,1)S(1)}, bf16[128,256]{1,0:T(8,128)(2,1)S(1)}, bf16[128,128]{1,0:T(8,128)(2,1)S(1)}) custom-call(s32[1]{0:T(128)} %bitcast.refs_0_, bf16[64,14464]{1,0:T(8,128)(2,1)S(1)} %bitcast.33, bf16[64,14464]{1,0:T(8,128)(2,1)S(1)} %bitcast.37, ...), custom_call_target="tpu_custom_call" | custom-call | tf_op jit(solution)/shard_map/pallas_call | solution.py:280
  38.7 2.5 %shard_map.113 = (bf16[64,7296]{1,0:T(8,128)(2,1)S(1)}, bf16[64,7296]{1,0:T(8,128)(2,1)S(1)}) custom-call(bf16[128,256]{1,0:T(8,128)(2,1)S(1)} %get-tuple-element.99.da_ref.refs_4_, bf16[128,256]{1,0:T(8,128)(2,1)S(1)} %get-tuple-element.100.du_ref.refs_6_, bf16[128,128]{1,0:T(8,128)(2,1)S(1)} %get-tuple-element.101.term_ref, ...), custom_call_target="tpu_custom_call" | custom-call | tf_op jit(solution)/shard_map/pallas_call | solution.py:301
  41.2 0.0 collective-permute-done.12
  41.3 1.1 %collective-permute-done.13 = bf16[1,2,8,14464]{3,2,1,0:T(8,128)(2,1)S(1)} collective-permute-done((bf16[1,2,8,14464]{3,2,1,0:T(8,128)(2,1)S(1)}, bf16[1,2,8,14464]{3,2,1,0:T(8,128)(2,1)S(1)}, u32[]{:S(2)}, u32[]{:S(2)}) %collective-permute-start.13) | collective-permute-done | bytes 462880 | tf_op jit(solution)/shard_map/ppermute | solution.py:331
  42.4 0.0 collective-permute-start.11
  42.4 0.2 maximum_maximum_fusion.1
  42.6 0.6 collective-permute-start.15
  43.2 1.7 %collective-permute-done.11 = bf16[64,7296]{1,0:T(8,128)(2,1)S(1)} collective-permute-done((bf16[64,7296]{1,0:T(8,128)(2,1)S(1)}, bf16[64,7296]{1,0:T(8,128)(2,1)S(1)}, u32[]{:S(2)}, u32[]{:S(2)}) %collective-permute-start.11) | collective-permute-done | bytes 933920 | tf_op jit(solution)/shard_map/ppermute | solution.py:331
  44.9 0.2 add_convert_fusion.1
  45.2 1.2 %collective-permute-start.14 = (bf16[2,2,8,7296]{3,2,1,0:T(8,128)(2,1)S(1)}, bf16[2,2,8,7296]{3,2,1,0:T(8,128)(2,1)S(1)}, u32[]{:S(2)}, u32[]{:S(2)}) collective-permute-start(bf16[2,2,8,7296]{3,2,1,0:T(8,128)(2,1)S(1)} %slice.74), channel_id=1, source_target_pairs={{0,16},{1,17},{2,18},{3,19},{4,12},{5,13},{6,14},{7,15},{8,24},{9,... | collective-permute-start | bytes 1400840 | tf_op jit(solution)/shard_map/ppermute | solution.py:331
  46.3 1.2 %collective-permute-done.15 = bf16[2,4,8,14464]{3,2,1,0:T(8,128)(2,1)S(1)} collective-permute-done((bf16[2,4,8,14464]{3,2,1,0:T(8,128)(2,1)S(1)}, bf16[2,4,8,14464]{3,2,1,0:T(8,128)(2,1)S(1)}, u32[]{:S(2)}, u32[]{:S(2)}) %collective-permute-start.15) | collective-permute-done | bytes 1851424 | tf_op jit(solution)/shard_map/ppermute | solution.py:331
  47.6 2.3 %shard_map.114 = (bf16[128,256]{1,0:T(8,128)(2,1)S(1)}, bf16[128,256]{1,0:T(8,128)(2,1)S(1)}, bf16[128,256]{1,0:T(8,128)(2,1)S(1)}, bf16[128,128]{1,0:T(8,128)(2,1)S(1)}) custom-call(s32[1]{0:T(128)} %bitcast.refs_0_, bf16[64,14464]{1,0:T(8,128)(2,1)S(1)} %bitcast.35, bf16[64,14464]{1,0:T(8,128)(2,1)S(1)} %bitcast.39, ...), custom_call_target="tpu_custom_call" | custom-call | tf_op jit(solution)/shard_map/pallas_call | solution.py:280
  49.9 2.5 %shard_map.115 = (bf16[64,7296]{1,0:T(8,128)(2,1)S(1)}, bf16[64,7296]{1,0:T(8,128)(2,1)S(1)}) custom-call(bf16[128,256]{1,0:T(8,128)(2,1)S(1)} %get-tuple-element.113.da_ref.refs_5_, bf16[128,256]{1,0:T(8,128)(2,1)S(1)} %get-tuple-element.114.du_ref.refs_7_, bf16[128,128]{1,0:T(8,128)(2,1)S(1)} %get-tuple-element.115.term_ref, ...), custom_call_target="tpu_custom_call" | custom-call | tf_op jit(solution)/shard_map/pallas_call | solution.py:301
  52.4 1.4 %collective-permute-done.14 = bf16[2,2,8,7296]{3,2,1,0:T(8,128)(2,1)S(1)} collective-permute-done((bf16[2,2,8,7296]{3,2,1,0:T(8,128)(2,1)S(1)}, bf16[2,2,8,7296]{3,2,1,0:T(8,128)(2,1)S(1)}, u32[]{:S(2)}, u32[]{:S(2)}) %collective-permute-start.14) | collective-permute-done | bytes 466976 | tf_op jit(solution)/shard_map/ppermute | solution.py:331
  53.8 0.0 collective-permute-start.17
  53.8 0.1 add_convert_fusion.2
  53.9 2.4 %collective-permute-done.17 = bf16[64,7296]{1,0:T(8,128)(2,1)S(1)} collective-permute-done((bf16[64,7296]{1,0:T(8,128)(2,1)S(1)}, bf16[64,7296]{1,0:T(8,128)(2,1)S(1)}, u32[]{:S(2)}, u32[]{:S(2)}) %collective-permute-start.17) | collective-permute-done | bytes 933920 | tf_op jit(solution)/shard_map/ppermute | solution.py:331
  56.3 0.2 add_convert_fusion
  56.5 1.2 %collective-permute-start.18 = (bf16[2,2,8,3584]{3,2,1,0:T(8,128)(2,1)S(1)}, bf16[2,2,8,3584]{3,2,1,0:T(8,128)(2,1)S(1)}, u32[]{:S(2)}, u32[]{:S(2)}) collective-permute-start(bf16[2,2,8,3584]{3,2,1,0:T(8,128)(2,1)S(1)} %slice.77), channel_id=1, source_target_pairs={{0,16},{1,17},{2,18},{3,19},{4,12},{5,13},{6,14},{7,15},{8,24},{9,... | collective-permute-start | bytes 688136 | tf_op jit(solution)/shard_map/ppermute | solution.py:331
  57.7 1.0 %collective-permute-start.16 = (bf16[2,1,8,7296]{3,2,1,0:T(8,128)(2,1)S(1)}, bf16[2,1,8,7296]{3,2,1,0:T(8,128)(2,1)S(1)}, u32[]{:S(2)}, u32[]{:S(2)}) collective-permute-start(bf16[2,1,8,7296]{3,2,1,0:T(8,128)(2,1)S(1)} %slice.75), channel_id=1, source_target_pairs={{0,8},{1,9},{2,10},{3,11},{4,20},{5,21},{6,22},{7,23},{8,0},{9,1},... | collective-permute-start | bytes 700424 | tf_op jit(solution)/shard_map/ppermute | solution.py:331
  58.8 1.0 %collective-permute-start.21 = (bf16[2,2,8,3712]{3,2,1,0:T(8,128)(2,1)S(1)}, bf16[2,2,8,3712]{3,2,1,0:T(8,128)(2,1)S(1)}, u32[]{:S(2)}, u32[]{:S(2)}) collective-permute-start(bf16[2,2,8,3712]{3,2,1,0:T(8,128)(2,1)S(1)} %slice.82), channel_id=1, source_target_pairs={{0,16},{1,17},{2,18},{3,19},{4,12},{5,13},{6,14},{7,15},{8,24},{9,... | collective-permute-start | bytes 712712 | tf_op jit(solution)/shard_map/ppermute | solution.py:331
  59.8 5.2 %collective-permute-done.18 = bf16[2,2,8,3584]{3,2,1,0:T(8,128)(2,1)S(1)} collective-permute-done((bf16[2,2,8,3584]{3,2,1,0:T(8,128)(2,1)S(1)}, bf16[2,2,8,3584]{3,2,1,0:T(8,128)(2,1)S(1)}, u32[]{:S(2)}, u32[]{:S(2)}) %collective-permute-start.18) | collective-permute-done | bytes 229408 | tf_op jit(solution)/shard_map/ppermute | solution.py:331
  65.0 0.1 add_convert_fusion.5
  65.1 1.3 %collective-permute-done.16 = bf16[2,1,8,7296]{3,2,1,0:T(8,128)(2,1)S(1)} collective-permute-done((bf16[2,1,8,7296]{3,2,1,0:T(8,128)(2,1)S(1)}, bf16[2,1,8,7296]{3,2,1,0:T(8,128)(2,1)S(1)}, u32[]{:S(2)}, u32[]{:S(2)}) %collective-permute-start.16) | collective-permute-done | bytes 233504 | tf_op jit(solution)/shard_map/ppermute | solution.py:331
  66.4 0.9 %collective-permute-start.20 = (bf16[2,1,8,3584]{3,2,1,0:T(8,128)(2,1)S(1)}, bf16[2,1,8,3584]{3,2,1,0:T(8,128)(2,1)S(1)}, u32[]{:S(2)}, u32[]{:S(2)}) collective-permute-start(bf16[2,1,8,3584]{3,2,1,0:T(8,128)(2,1)S(1)} %slice.80), channel_id=1, source_target_pairs={{0,8},{1,9},{2,10},{3,11},{4,20},{5,21},{6,22},{7,23},{8,0},{9,1},... | collective-permute-start | bytes 344072 | tf_op jit(solution)/shard_map/ppermute | solution.py:331
  67.4 0.1 add_convert_fusion.4
  67.4 0.1 collective-permute-done.21
  67.6 0.1 add_convert_fusion.3
  67.6 1.1 %collective-permute-start.22 = (bf16[2,1,8,3712]{3,2,1,0:T(8,128)(2,1)S(1)}, bf16[2,1,8,3712]{3,2,1,0:T(8,128)(2,1)S(1)}, u32[]{:S(2)}, u32[]{:S(2)}) collective-permute-start(bf16[2,1,8,3712]{3,2,1,0:T(8,128)(2,1)S(1)} %slice.83), channel_id=1, source_target_pairs={{0,8},{1,9},{2,10},{3,11},{4,20},{5,21},{6,22},{7,23},{8,0},{9,1},... | collective-permute-start | bytes 356360 | tf_op jit(solution)/shard_map/ppermute | solution.py:331
  68.8 0.4 collective-permute-start.19
  69.1 2.1 %collective-permute-done.20 = bf16[2,1,8,3584]{3,2,1,0:T(8,128)(2,1)S(1)} collective-permute-done((bf16[2,1,8,3584]{3,2,1,0:T(8,128)(2,1)S(1)}, bf16[2,1,8,3584]{3,2,1,0:T(8,128)(2,1)S(1)}, u32[]{:S(2)}, u32[]{:S(2)}) %collective-permute-start.20) | collective-permute-done | bytes 114720 | tf_op jit(solution)/shard_map/ppermute | solution.py:331
  71.2 1.3 %collective-permute-done.22 = bf16[2,1,8,3712]{3,2,1,0:T(8,128)(2,1)S(1)} collective-permute-done((bf16[2,1,8,3712]{3,2,1,0:T(8,128)(2,1)S(1)}, bf16[2,1,8,3712]{3,2,1,0:T(8,128)(2,1)S(1)}, u32[]{:S(2)}, u32[]{:S(2)}) %collective-permute-start.22) | collective-permute-done | bytes 118816 | tf_op jit(solution)/shard_map/ppermute | solution.py:331
  72.6 0.6 collective-permute-start.24
  73.2 3.0 %collective-permute-start.23 = (bf16[1,8,7296]{2,1,0:T(8,128)(2,1)S(1)}, bf16[1,8,7296]{2,1,0:T(8,128)(2,1)S(1)}, u32[]{:S(2)}, u32[]{:S(2)}) collective-permute-start(bf16[1,8,7296]{2,1,0:T(8,128)(2,1)S(1)} %get-tuple-element.146), channel_id=1, source_target_pairs={{0,3},{1,0},{2,1},{3,2},{4,7},{5,4},{6,5},{7,6},{8,11},{9,8},{10,9... | collective-permute-start | bytes 350216 | tf_op jit(solution)/shard_map/ppermute | solution.py:331
  76.2 4.7 %shard_map.116 = (bf16[7168,256]{1,0:T(8,128)(2,1)}, bf16[7168,256]{1,0:T(8,128)(2,1)}, bf16[256,7168]{1,0:T(8,128)(2,1)}) custom-call(bf16[64,14464]{1,0:T(8,128)(2,1)S(1)} %bitcast.34, bf16[64,14464]{1,0:T(8,128)(2,1)S(1)} %bitcast.38, bf16[64,14464]{1,0:T(8,128)(2,1)S(1)} %bitcast.36, bf16[64,14464]{1,0:T(8,128)(2,1)S(1)} %bitcast.40, ...), custom_call_target="tpu_custom_call" | custom-call | bytes 4194304 | tf_op jit(solution)/shard_map/pallas_call | solution.py:174
  81.0 0.0 collective-permute-done.19
  81.0 0.0 collective-permute-done.24
  81.0 0.0 collective-permute-done.23
  81.0 0.8 shard_map.117
  (29 shorter events, 0.6 us)
Async XLA Ops:
  1.7 11.2 %collective-permute-start.2 = (bf16[1,1,8,14464]{3,2,1,0:T(8,128)(2,1)S(1)}, bf16[1,1,8,14464]{3,2,1,0:T(8,128)(2,1)S(1)}, u32[]{:S(2)}, u32[]{:S(2)}) collective-permute-start(bf16[1,1,8,14464]{3,2,1,0:T(8,128)(2,1)S(1)} %bitcast.41), channel_id=1, source_target_pairs={{0,3},{1,0},{2,1},{3,2},{4,7},{5,4},{6,5},{7,6},{8,11},{9,8},{10,9... | collective-permute-start | bytes 694280 | tf_op jit(solution)/shard_map/ppermute | solution.py:331
  6.8 11.8 %collective-permute-start.1 = (bf16[1,1,8,14464]{3,2,1,0:T(8,128)(2,1)S(1)}, bf16[1,1,8,14464]{3,2,1,0:T(8,128)(2,1)S(1)}, u32[]{:S(2)}, u32[]{:S(2)}) collective-permute-start(bf16[1,1,8,14464]{3,2,1,0:T(8,128)(2,1)S(1)} %bitcast.42), channel_id=1, source_target_pairs={{0,16},{1,17},{2,18},{3,19},{4,12},{5,13},{6,14},{7,15},{8,24},{9,... | collective-permute-start | bytes 694280 | tf_op jit(solution)/shard_map/ppermute | solution.py:331
  8.3 10.3 %collective-permute-start = (bf16[1,1,8,14464]{3,2,1,0:T(8,128)(2,1)S(1)}, bf16[1,1,8,14464]{3,2,1,0:T(8,128)(2,1)S(1)}, u32[]{:S(2)}, u32[]{:S(2)}) collective-permute-start(bf16[1,1,8,14464]{3,2,1,0:T(8,128)(2,1)S(1)} %bitcast.43), channel_id=1, source_target_pairs={{0,8},{1,9},{2,10},{3,11},{4,20},{5,21},{6,22},{7,23},{8,0},{9,1},... | collective-permute-start | bytes 694280 | tf_op jit(solution)/shard_map/ppermute | solution.py:331
  9.8 10.4 %collective-permute-start.4 = (bf16[1,1,8,14464]{3,2,1,0:T(8,128)(2,1)S(1)}, bf16[1,1,8,14464]{3,2,1,0:T(8,128)(2,1)S(1)}, u32[]{:S(2)}, u32[]{:S(2)}) collective-permute-start(bf16[1,1,8,14464]{3,2,1,0:T(8,128)(2,1)S(1)} %bitcast.44), channel_id=1, source_target_pairs={{0,1},{1,2},{2,3},{3,0},{4,5},{5,6},{6,7},{7,4},{8,9},{9,10},{10,1... | collective-permute-start | bytes 694280 | tf_op jit(solution)/shard_map/ppermute | solution.py:331
  12.9 8.0 %collective-permute-start.7 = (bf16[1,1,8,14464]{3,2,1,0:T(8,128)(2,1)S(1)}, bf16[1,1,8,14464]{3,2,1,0:T(8,128)(2,1)S(1)}, u32[]{:S(2)}, u32[]{:S(2)}) collective-permute-start(bf16[1,1,8,14464]{3,2,1,0:T(8,128)(2,1)S(1)} %collective-permute-done.2), channel_id=1, source_target_pairs={{0,8},{1,9},{2,10},{3,11},{4,20},{5,21},{6,22},{7,23},{8,0},{9,1},... | collective-permute-start | bytes 694280 | tf_op jit(solution)/shard_map/ppermute | solution.py:331
  14.3 8.8 %collective-permute-start.6 = (bf16[1,1,8,14464]{3,2,1,0:T(8,128)(2,1)S(1)}, bf16[1,1,8,14464]{3,2,1,0:T(8,128)(2,1)S(1)}, u32[]{:S(2)}, u32[]{:S(2)}) collective-permute-start(bf16[1,1,8,14464]{3,2,1,0:T(8,128)(2,1)S(1)} %collective-permute-done.2), channel_id=1, source_target_pairs={{0,3},{1,0},{2,1},{3,2},{4,7},{5,4},{6,5},{7,6},{8,11},{9,8},{10,9... | collective-permute-start | bytes 694280 | tf_op jit(solution)/shard_map/ppermute | solution.py:331
  18.6 11.2 %collective-permute-start.3 = (bf16[1,1,8,14464]{3,2,1,0:T(8,128)(2,1)S(1)}, bf16[1,1,8,14464]{3,2,1,0:T(8,128)(2,1)S(1)}, u32[]{:S(2)}, u32[]{:S(2)}) collective-permute-start(bf16[1,1,8,14464]{3,2,1,0:T(8,128)(2,1)S(1)} %collective-permute-done), channel_id=1, source_target_pairs={{0,16},{1,17},{2,18},{3,19},{4,12},{5,13},{6,14},{7,15},{8,24},{9,... | collective-permute-start | bytes 694280 | tf_op jit(solution)/shard_map/ppermute | solution.py:331
  20.2 8.6 %collective-permute-start.5 = (bf16[1,1,8,14464]{3,2,1,0:T(8,128)(2,1)S(1)}, bf16[1,1,8,14464]{3,2,1,0:T(8,128)(2,1)S(1)}, u32[]{:S(2)}, u32[]{:S(2)}) collective-permute-start(bf16[1,1,8,14464]{3,2,1,0:T(8,128)(2,1)S(1)} %collective-permute-done.4), channel_id=1, source_target_pairs={{0,8},{1,9},{2,10},{3,11},{4,20},{5,21},{6,22},{7,23},{8,0},{9,1},... | collective-permute-start | bytes 694280 | tf_op jit(solution)/shard_map/ppermute | solution.py:331
  20.9 11.5 %collective-permute-start.8 = (bf16[1,2,8,14464]{3,2,1,0:T(8,128)(2,1)S(1)}, bf16[1,2,8,14464]{3,2,1,0:T(8,128)(2,1)S(1)}, u32[]{:S(2)}, u32[]{:S(2)}) collective-permute-start(bf16[1,2,8,14464]{3,2,1,0:T(8,128)(2,1)S(1)} %constant_dynamic-update-slice_fusion.3), channel_id=1, source_target_pairs={{0,16},{1,17},{2,18},{3,19},{4,12},{5,13},{6,14},{7,15},{8,24},{9,... | collective-permute-start | bytes 1388552 | tf_op jit(solution)/shard_map/ppermute | solution.py:331
  23.1 9.5 %collective-permute-start.10 = (bf16[1,1,8,14464]{3,2,1,0:T(8,128)(2,1)S(1)}, bf16[1,1,8,14464]{3,2,1,0:T(8,128)(2,1)S(1)}, u32[]{:S(2)}, u32[]{:S(2)}) collective-permute-start(bf16[1,1,8,14464]{3,2,1,0:T(8,128)(2,1)S(1)} %collective-permute-done.6), channel_id=1, source_target_pairs={{0,8},{1,9},{2,10},{3,11},{4,20},{5,21},{6,22},{7,23},{8,0},{9,1},... | collective-permute-start | bytes 694280 | tf_op jit(solution)/shard_map/ppermute | solution.py:331
  28.9 12.4 %collective-permute-start.12 = (bf16[1,2,8,14464]{3,2,1,0:T(8,128)(2,1)S(1)}, bf16[1,2,8,14464]{3,2,1,0:T(8,128)(2,1)S(1)}, u32[]{:S(2)}, u32[]{:S(2)}) collective-permute-start(bf16[1,2,8,14464]{3,2,1,0:T(8,128)(2,1)S(1)} %constant_dynamic-update-slice_fusion.5), channel_id=1, source_target_pairs={{0,16},{1,17},{2,18},{3,19},{4,12},{5,13},{6,14},{7,15},{8,24},{9,... | collective-permute-start | bytes 1388552 | tf_op jit(solution)/shard_map/ppermute | solution.py:331
  32.6 3.9 %collective-permute-start.9 = (bf16[2,4,8,14464]{3,2,1,0:T(8,128)(2,1)S(1)}, bf16[2,4,8,14464]{3,2,1,0:T(8,128)(2,1)S(1)}, u32[]{:S(2)}, u32[]{:S(2)}) collective-permute-start(bf16[2,4,8,14464]{3,2,1,0:T(8,128)(2,1)S(1)} %maximum_maximum_fusion), channel_id=1, source_target_pairs={{0,4},{1,5},{2,6},{3,7},{4,0},{5,1},{6,2},{7,3},{8,12},{9,13},{10,... | collective-permute-start | bytes 5554184 | tf_op jit(solution)/shard_map/ppermute | solution.py:331
  32.7 9.7 %collective-permute-start.13 = (bf16[1,2,8,14464]{3,2,1,0:T(8,128)(2,1)S(1)}, bf16[1,2,8,14464]{3,2,1,0:T(8,128)(2,1)S(1)}, u32[]{:S(2)}, u32[]{:S(2)}) collective-permute-start(bf16[1,2,8,14464]{3,2,1,0:T(8,128)(2,1)S(1)} %constant_dynamic-update-slice_fusion.9), channel_id=1, source_target_pairs={{0,16},{1,17},{2,18},{3,19},{4,12},{5,13},{6,14},{7,15},{8,24},{9,... | collective-permute-start | bytes 1388552 | tf_op jit(solution)/shard_map/ppermute | solution.py:331
  42.4 2.5 %collective-permute-start.11 = (bf16[64,7296]{1,0:T(8,128)(2,1)S(1)}, bf16[64,7296]{1,0:T(8,128)(2,1)S(1)}, u32[]{:S(2)}, u32[]{:S(2)}) collective-permute-start(bf16[64,7296]{1,0:T(8,128)(2,1)S(1)} %get-tuple-element.103), channel_id=1, source_target_pairs={{0,4},{1,5},{2,6},{3,7},{4,0},{5,1},{6,2},{7,3},{8,12},{9,13},{10,... | collective-permute-start | bytes 2801672 | tf_op jit(solution)/shard_map/ppermute | solution.py:331
  42.6 4.9 %collective-permute-start.15 = (bf16[2,4,8,14464]{3,2,1,0:T(8,128)(2,1)S(1)}, bf16[2,4,8,14464]{3,2,1,0:T(8,128)(2,1)S(1)}, u32[]{:S(2)}, u32[]{:S(2)}) collective-permute-start(bf16[2,4,8,14464]{3,2,1,0:T(8,128)(2,1)S(1)} %maximum_maximum_fusion.1), channel_id=1, source_target_pairs={{0,4},{1,5},{2,6},{3,7},{4,0},{5,1},{6,2},{7,3},{8,12},{9,13},{10,... | collective-permute-start | bytes 5554184 | tf_op jit(solution)/shard_map/ppermute | solution.py:331
  45.2 8.6 %collective-permute-start.14 = (bf16[2,2,8,7296]{3,2,1,0:T(8,128)(2,1)S(1)}, bf16[2,2,8,7296]{3,2,1,0:T(8,128)(2,1)S(1)}, u32[]{:S(2)}, u32[]{:S(2)}) collective-permute-start(bf16[2,2,8,7296]{3,2,1,0:T(8,128)(2,1)S(1)} %slice.74), channel_id=1, source_target_pairs={{0,16},{1,17},{2,18},{3,19},{4,12},{5,13},{6,14},{7,15},{8,24},{9,... | collective-permute-start | bytes 1400840 | tf_op jit(solution)/shard_map/ppermute | solution.py:331
  53.8 2.5 %collective-permute-start.17 = (bf16[64,7296]{1,0:T(8,128)(2,1)S(1)}, bf16[64,7296]{1,0:T(8,128)(2,1)S(1)}, u32[]{:S(2)}, u32[]{:S(2)}) collective-permute-start(bf16[64,7296]{1,0:T(8,128)(2,1)S(1)} %get-tuple-element.119), channel_id=1, source_target_pairs={{0,4},{1,5},{2,6},{3,7},{4,0},{5,1},{6,2},{7,3},{8,12},{9,13},{10,... | collective-permute-start | bytes 2801672 | tf_op jit(solution)/shard_map/ppermute | solution.py:331
  56.5 8.5 %collective-permute-start.18 = (bf16[2,2,8,3584]{3,2,1,0:T(8,128)(2,1)S(1)}, bf16[2,2,8,3584]{3,2,1,0:T(8,128)(2,1)S(1)}, u32[]{:S(2)}, u32[]{:S(2)}) collective-permute-start(bf16[2,2,8,3584]{3,2,1,0:T(8,128)(2,1)S(1)} %slice.77), channel_id=1, source_target_pairs={{0,16},{1,17},{2,18},{3,19},{4,12},{5,13},{6,14},{7,15},{8,24},{9,... | collective-permute-start | bytes 688136 | tf_op jit(solution)/shard_map/ppermute | solution.py:331
  57.7 8.7 %collective-permute-start.16 = (bf16[2,1,8,7296]{3,2,1,0:T(8,128)(2,1)S(1)}, bf16[2,1,8,7296]{3,2,1,0:T(8,128)(2,1)S(1)}, u32[]{:S(2)}, u32[]{:S(2)}) collective-permute-start(bf16[2,1,8,7296]{3,2,1,0:T(8,128)(2,1)S(1)} %slice.75), channel_id=1, source_target_pairs={{0,8},{1,9},{2,10},{3,11},{4,20},{5,21},{6,22},{7,23},{8,0},{9,1},... | collective-permute-start | bytes 700424 | tf_op jit(solution)/shard_map/ppermute | solution.py:331
  58.8 8.7 %collective-permute-start.21 = (bf16[2,2,8,3712]{3,2,1,0:T(8,128)(2,1)S(1)}, bf16[2,2,8,3712]{3,2,1,0:T(8,128)(2,1)S(1)}, u32[]{:S(2)}, u32[]{:S(2)}) collective-permute-start(bf16[2,2,8,3712]{3,2,1,0:T(8,128)(2,1)S(1)} %slice.82), channel_id=1, source_target_pairs={{0,16},{1,17},{2,18},{3,19},{4,12},{5,13},{6,14},{7,15},{8,24},{9,... | collective-permute-start | bytes 712712 | tf_op jit(solution)/shard_map/ppermute | solution.py:331
  66.4 4.8 %collective-permute-start.20 = (bf16[2,1,8,3584]{3,2,1,0:T(8,128)(2,1)S(1)}, bf16[2,1,8,3584]{3,2,1,0:T(8,128)(2,1)S(1)}, u32[]{:S(2)}, u32[]{:S(2)}) collective-permute-start(bf16[2,1,8,3584]{3,2,1,0:T(8,128)(2,1)S(1)} %slice.80), channel_id=1, source_target_pairs={{0,8},{1,9},{2,10},{3,11},{4,20},{5,21},{6,22},{7,23},{8,0},{9,1},... | collective-permute-start | bytes 344072 | tf_op jit(solution)/shard_map/ppermute | solution.py:331
  67.6 4.9 %collective-permute-start.22 = (bf16[2,1,8,3712]{3,2,1,0:T(8,128)(2,1)S(1)}, bf16[2,1,8,3712]{3,2,1,0:T(8,128)(2,1)S(1)}, u32[]{:S(2)}, u32[]{:S(2)}) collective-permute-start(bf16[2,1,8,3712]{3,2,1,0:T(8,128)(2,1)S(1)} %slice.83), channel_id=1, source_target_pairs={{0,8},{1,9},{2,10},{3,11},{4,20},{5,21},{6,22},{7,23},{8,0},{9,1},... | collective-permute-start | bytes 356360 | tf_op jit(solution)/shard_map/ppermute | solution.py:331
  68.8 12.2 %collective-permute-start.19 = (bf16[1,8,7296]{2,1,0:T(8,128)(2,1)S(1)}, bf16[1,8,7296]{2,1,0:T(8,128)(2,1)S(1)}, u32[]{:S(2)}, u32[]{:S(2)}) collective-permute-start(bf16[1,8,7296]{2,1,0:T(8,128)(2,1)S(1)} %get-tuple-element.147), channel_id=1, source_target_pairs={{0,1},{1,2},{2,3},{3,0},{4,5},{5,6},{6,7},{7,4},{8,9},{9,10},{10,1... | collective-permute-start | bytes 350216 | tf_op jit(solution)/shard_map/ppermute | solution.py:331
  72.6 8.3 %collective-permute-start.24 = (bf16[1,8,7296]{2,1,0:T(8,128)(2,1)S(1)}, bf16[1,8,7296]{2,1,0:T(8,128)(2,1)S(1)}, u32[]{:S(2)}, u32[]{:S(2)}) collective-permute-start(bf16[1,8,7296]{2,1,0:T(8,128)(2,1)S(1)} %get-tuple-element.145), channel_id=1, source_target_pairs={{0,2},{1,3},{2,0},{3,1},{4,6},{5,7},{6,4},{7,5},{8,10},{9,11},{10,... | collective-permute-start | bytes 350216 | tf_op jit(solution)/shard_map/ppermute | solution.py:331
  73.2 7.8 %collective-permute-start.23 = (bf16[1,8,7296]{2,1,0:T(8,128)(2,1)S(1)}, bf16[1,8,7296]{2,1,0:T(8,128)(2,1)S(1)}, u32[]{:S(2)}, u32[]{:S(2)}) collective-permute-start(bf16[1,8,7296]{2,1,0:T(8,128)(2,1)S(1)} %get-tuple-element.146), channel_id=1, source_target_pairs={{0,3},{1,0},{2,1},{3,2},{4,7},{5,4},{6,5},{7,6},{8,11},{9,8},{10,9... | collective-permute-start | bytes 350216 | tf_op jit(solution)/shard_map/ppermute | solution.py:331
  76.2 4.8 %copy-start = (s32[8,4]{0,1:T(4,128)S(1)}, s32[8,4]{0,1:T(4,128)}, u32[]{:S(2)}) copy-start(s32[8,4]{0,1:T(4,128)} %param.9) | copy-start | bytes 388
